TPU v7x, 32 devices: a whole 2x2x4 slice. The times are simulated.
32 devices in a mesh: rows: 8 (over y, x, core), vecs: 4 (over z).
Axes of the slice: x: 2, y: 2, z: 4, core: 2. Of those that a mesh axis runs over, the one named last changes fastest.
Arguments:
- eigvecs: bfloat16 [8192, 1024], P('rows', 'vecs'), may hold values from -6 to 6
- reflectors: bfloat16 [2, 8192, 1024], P(None, 'rows', 'vecs'), may hold values from -0.125 to 0.125
- factors: bfloat16 [2, 1024, 1024], replicated, as said below
Outputs:
- back_vecs: bfloat16 [8192, 1024], P('rows', 'vecs')
Inputs may be any that keep to these rules, and one draw needn't show every extreme that they name: `factors`: each factor is upper triangular, its diagonal between 0.15 and 0.35.
All inputs are finite; a program needn't handle non-finite values.
Results may differ from a plain program's by a relative error of at most 0.01.
Values may be sent and summed in bfloat16 or wider, within the bound.
No kernel may reach another device: no remote copies, remote signals or barrier semaphores. Data moves between devices by JAX's collectives and lax.ppermute only.
A program may use at most 64 MiB of HBM per device.

v0:
```python
import jax
import jax.numpy as jnp
from jax import lax
from jax.sharding import PartitionSpec as P


def body(eigvecs, reflectors, factors):
    current = eigvecs
    for which in (1, 0):
        panel = lax.all_gather(reflectors[which], "vecs", axis=1, tiled=True)
        partial_value = lax.dot_general(
            panel, current, (((0,), (0,)), ((), ())), preferred_element_type=jnp.float32
        )
        coeff = lax.psum(partial_value, "rows").astype(jnp.bfloat16)
        scaled = jnp.dot(factors[which], coeff, preferred_element_type=jnp.float32).astype(
            jnp.bfloat16
        )
        update = jnp.dot(panel, scaled, preferred_element_type=jnp.float32)
        current = (current.astype(jnp.float32) - update).astype(jnp.bfloat16)
    return current


def solution(mesh):
    in_specs = (P("rows", "vecs"), P(None, "rows", "vecs"), P())
    out_specs = P("rows", "vecs")
    return jax.shard_map(body, mesh=mesh, in_specs=in_specs, out_specs=out_specs, check_vma=False)
```

profile of v0, /device:TPU:0, one launch (start us, length us, event | category | flops | bytes accessed | tf_op | source)
XLA Modules:
  0.0 181.6 jit_solution(3180974861312839648)
XLA Ops:
  6.5 0.0 copy-start.1
  6.5 0.0 all-gather.5.cloned.1.call-start
  6.5 2.3 %fusion.49 = (bf16[1,1024,256]{2,1,0:T(8,128)(2,1)}, bf16[1,1024,256]{2,1,0:T(8,128)(2,1)}) fusion(bf16[2,1024,256]{2,1,0:T(8,128)(2,1)} %param.4), kind=kLoop, calls=%fused_computation.25 | loop fusion | bytes 2097152 | tf_op jit(solution)/shard_map/slice | solution.py:10
  8.8 0.0 all-gather.5.cloned.1.call-update
  8.9 0.0 all-gather.7.cloned.1.call-start
  8.9 0.7 all-gather.7.cloned.1.call-update
  9.6 0.0 copy-done.1
  9.6 0.2 copy.4
  9.8 48.1 %all-gather.5.cloned.1.call-done = bf16[1,1024,1024]{2,1,0:T(8,128)(2,1)} async-done(((bf16[1,1024,256]{2,1,0:T(8,128)(2,1)}), bf16[1,1024,1024]{2,1,0:T(8,128)(2,1)}) %all-gather.5.cloned.1.call-update) | async-done | bytes 2097168 | tf_op jit(solution)/shard_map/all_gather | solution.py:10
  58.0 2.3 %fusion.10 = f32[1024,256]{1,0:T(8,128)S(1)} fusion(bf16[1024,256]{1,0:T(8,128)(2,1)S(1)} %copy-done.1, bf16[1,1024,1024]{2,1,0:T(8,128)(2,1)} %all-gather.5.cloned.1.call-done), kind=kOutput, calls=%fused_computation.10 | convolution fusion | flops 536870912 | bytes 3670016 | tf_op jit(solution)/shard_map/dot_general | solution.py:11
  60.3 53.6 %all-reduce.2 = bf16[1024,256]{1,0:T(8,128)(2,1)S(1)} all-reduce(f32[1024,256]{1,0:T(8,128)S(1)} %fusion.10), channel_id=1, replica_groups=mesh['rows'=8,'vecs'=4] {'rows'}, use_global_device_ids=true, to_apply=%region_0.0 | all-reduce | flops 262144 | bytes 1572864 | tf_op jit(solution)/shard_map/psum | solution.py:14
  113.9 4.3 %fusion.35 = bf16[1024,256]{0,1:T(8,128)(2,1)} fusion(bf16[1,1024,1024]{2,1,0:T(8,128)(2,1)} %all-gather.5.cloned.1.call-done, bf16[1024,256]{0,1:T(8,128)(2,1)S(1)} %copy.4, bf16[2,1024,1024]{2,1,0:T(8,128)(2,1)} %param.5, bf16[1024,256]{1,0:T(8,128)(2,1)S(1)} %all-reduce.2), kind=kOutput, calls=%fused_computation.21 | convolution fusion | flops 1074790400 | bytes 5767168 | tf_op jit(solution)/shard_map/dot_general | solution.py:18
  118.2 0.0 all-gather.7.cloned.1.call-done
  118.2 0.0 copy-start
  118.2 2.6 %fusion.17 = f32[1024,256]{0,1:T(8,128)S(1)} fusion(bf16[1024,256]{0,1:T(8,128)(2,1)} %fusion.35, bf16[1,1024,1024]{2,1,0:T(8,128)(2,1)} %all-gather.7.cloned.1.call-done), kind=kOutput, calls=%fused_computation.15 | convolution fusion | flops 536870912 | bytes 3670016 | tf_op jit(solution)/shard_map/dot_general | solution.py:11
  120.8 49.8 %all-reduce.3 = bf16[1024,256]{0,1:T(8,128)(2,1)} all-reduce(f32[1024,256]{0,1:T(8,128)S(1)} %fusion.17), channel_id=1, replica_groups=mesh['rows'=8,'vecs'=4] {'rows'}, use_global_device_ids=true, to_apply=%region_1.0 | all-reduce | flops 262144 | bytes 1572864 | tf_op jit(solution)/shard_map/psum | solution.py:14
  170.6 0.0 copy-done
  170.6 3.1 %fusion.38 = bf16[1024,256]{0,1:T(8,128)(2,1)S(1)} fusion(bf16[1,1024,1024]{2,1,0:T(8,128)(2,1)S(1)} %copy-done, bf16[1024,256]{0,1:T(8,128)(2,1)} %fusion.35, bf16[2,1024,1024]{2,1,0:T(8,128)(2,1)} %param.5, bf16[1024,256]{0,1:T(8,128)(2,1)} %all-reduce.3), kind=kOutput, calls=%fused_computation.22 | convolution fusion | flops 1074790400 | bytes 5767168 | tf_op jit(solution)/shard_map/dot_general | solution.py:18
  173.8 1.0 copy.5
Async XLA Ops:
  6.5 3.1 %copy-start.1 = (bf16[1024,256]{1,0:T(8,128)(2,1)S(1)}, bf16[1024,256]{1,0:T(8,128)(2,1)}, u32[]{:S(2)}) copy-start(bf16[1024,256]{1,0:T(8,128)(2,1)} %param.3) | copy-start | bytes 1572868
  6.5 51.4 %all-gather.5.cloned.1.call-start = ((), (), s32[]{:S(2)}) async-start(), calls=%async_computation | async-start | bytes 2621440 | tf_op jit(solution)/shard_map/all_gather | solution.py:10
  8.9 109.4 %all-gather.7.cloned.1.call-start = ((), (), s32[]{:S(2)}) async-start(), calls=%async_computation.1 | async-start | bytes 2621440 | tf_op jit(solution)/shard_map/all_gather | solution.py:10
  118.2 52.4 %copy-start = (bf16[1,1024,1024]{2,1,0:T(8,128)(2,1)S(1)}, bf16[1,1024,1024]{2,1,0:T(8,128)(2,1)}, u32[]{:S(2)}) copy-start(bf16[1,1024,1024]{2,1,0:T(8,128)(2,1)} %all-gather.7.cloned.1.call-done) | copy-start | bytes 6291460
Sparse Core Ops, SparseCore 0:
  9.0 48.9 all-gather.4
  59.5 44.4 all-gather.6
where the time goes:
time: 182 us
  blocking collectives  103 us (57%)
  waiting for transfers between devices  48.8 us (27%)
  between operations  13.4 us (7%)
  matrix products  12.4 us (7%)
  local copies, waits for them, and re-layouts  3.51 us (2%)
    psum x2, blocking collectives, body(): coeff = lax.psum(partial_value, 'rows').astype(jnp.bfloat16)  103 us
    all_gather x2, waiting for transfers between devices, body(): panel = lax.all_gather(reflectors[which], 'vecs', axis=1, tiled=True)  48.1 us
    dot_general x2, matrix products, body(): update = jnp.dot(panel, scaled, preferred_element_type=jnp.float32)  7.44 us
    dot_general x2, matrix products, body(): lax.dot_general(panel, current, (((0,), (0,)), ((), ())), preferred_eleme...  4.93 us
  transfers between devices with their start and end apart: 2, of which 1 were waited for; matrix products, arithmetic and copies ran while one was open for 4% of the time, Pallas kernels for 0%

commit v1 on v0

v1 whole, which is shorter than its diff:
```python
import functools

import jax
import jax.numpy as jnp
from jax import lax
from jax.experimental import pallas as pl
from jax.experimental.pallas import tpu as pltpu
from jax.sharding import PartitionSpec as P

F32, BF16 = jnp.float32, jnp.bfloat16


def after(x, *others):
    return lax.optimization_barrier((x,) + others)[0]


def dot0(a, b):
    return lax.dot_general(a, b, (((0,), (0,)), ((), ())), preferred_element_type=F32)


def swap(x, bit, m):
    return lax.ppermute(x, "rows", [(i, i ^ bit) for i in range(m)])


def sum_rows(part, wide, m):
    odd = lax.axis_index("rows") % 2
    part = part.astype(BF16).reshape(-1, 2, wide // 2, part.shape[1])
    mine = lax.dynamic_index_in_dim(part, odd, 1, keepdims=False)
    other = lax.dynamic_index_in_dim(part, 1 - odd, 1, keepdims=False)
    mine = (mine.astype(F32) + swap(other, 1, m).astype(F32)).astype(BF16)
    bit = 2
    while bit < m:
        steps = [s * bit for s in range(1, 4) if s * bit < m]
        got = [swap(mine, s, m) for s in steps]
        mine = sum([g.astype(F32) for g in got], mine.astype(F32)).astype(BF16)
        bit *= 4
    return mine, swap(mine, 1, m)


def update_kernel(halves, pieces, wide, at_ref, factor_ref, current_ref, *refs):
    coeff_refs, panel_refs = refs[:halves], refs[halves : halves + pieces]
    out_ref, coeff, scaled = refs[halves + pieces :]

    @pl.when(pl.program_id(0) == 0)
    def _():
        at = 0
        for ref in coeff_refs:
            for k in range(ref.shape[0]):
                h = ref.shape[1]
                coeff[pl.ds(pl.multiple_of(at_ref[at], h), h), :] = ref[k]
                at += 1
        scaled[...] = jnp.dot(factor_ref[...], coeff[...], preferred_element_type=F32).astype(BF16)

    total = current_ref[...].astype(F32)
    first = sum(ref.shape[0] for ref in coeff_refs)
    update = None
    for k, ref in enumerate(panel_refs):
        rows = pl.ds(pl.multiple_of(at_ref[first + k], wide), wide)
        term = jnp.dot(ref[...], scaled[rows, :], preferred_element_type=F32)
        update = term if update is None else update + term
    out_ref[...] = (total - update).astype(BF16)


def update(current, factor, coeffs, panels, where):
    rows, columns = current.shape
    size, wide = factor.shape[0], panels[0].shape[1]
    tile = min(rows, 256)
    whole = lambda shape: pl.BlockSpec(shape, lambda i, at: (0,) * len(shape))
    grid_spec = pltpu.PrefetchScalarGridSpec(
        num_scalar_prefetch=1,
        grid=(rows // tile,),
        in_specs=[whole(factor.shape), pl.BlockSpec((tile, columns), lambda i, at: (i, 0))]
        + [whole(c.shape) for c in coeffs]
        + [pl.BlockSpec((tile, wide), lambda i, at: (i, 0)) for _ in panels],
        out_specs=pl.BlockSpec((tile, columns), lambda i, at: (i, 0)),
        scratch_shapes=[pltpu.VMEM((size, columns), BF16), pltpu.VMEM((size, columns), BF16)],
    )
    flops = 2 * size * columns * (size + rows)
    return pl.pallas_call(
        functools.partial(update_kernel, len(coeffs), len(panels), wide),
        grid_spec=grid_spec,
        out_shape=jax.ShapeDtypeStruct(current.shape, BF16),
        compiler_params=pltpu.CompilerParams(vmem_limit_bytes=32 << 20),
        cost_estimate=pl.CostEstimate(flops=flops, bytes_accessed=2 * size * (size + 2 * rows), transcendentals=0),
    )(where, factor, current, *coeffs, *panels)


class Line:
    def __init__(self, n):
        self.n = n
        self.me = lax.axis_index("vecs")

    def pairs(self, s, parity):
        out = []
        for i in range(parity, self.n - 1, 2):
            if i - s + 1 >= 0:
                out.append((i, i + 1))
            if i + s < self.n:
                out.append((i + 1, i))
        return out

    def send(self, x, pairs):
        return lax.ppermute(x, "vecs", pairs) if pairs else None

    def index(self, s, parity):
        return jnp.where(self.me % 2 == parity, self.me + s, self.me - s)


def body(n, m, eigvecs, reflectors, factors):
    line = Line(n)
    me = line.me
    wide = reflectors.shape[2]
    p1, p0 = reflectors[1], reflectors[0]
    current = eigvecs

    def gather(panel, gate_even, gate_odd):
        even, odd = {}, {}
        for s in range(1, n):
            from_e = panel if s == 1 else odd[s - 1]
            from_o = panel if s == 1 else even[s - 1]
            even[s] = line.send(gate_even(s, from_e), line.pairs(s, 0)) if from_e is not None else None
            odd[s] = line.send(gate_odd(s, from_o), line.pairs(s, 1)) if from_o is not None else None
        return even, odd

    keep = lambda s, x: x
    even1, odd1 = gather(p1, keep, keep)
    last = max(s for s in even1 if even1[s] is not None)
    e_gate = lambda s, x: after(x, even1[last]) if s == 1 else x
    o_gate = lambda s, x: after(x, even1[last - 1], odd1[last - 1]) if s == 1 else x
    even0, odd0 = gather(p0, e_gate, o_gate)

    def slots(panel, even, odd):
        out = [(me, [panel])]
        if n > 1:
            out.append((line.index(1, 0), [even[1]]))
        for s in range(1, n - 1):
            c = n - s - 1 if s % 2 else n - s + 1
            i, j = line.index(s, 1), line.index(c, 0)
            there = (i >= 0) & (i < n)
            out.append((jnp.where(there, i, j), [x for x in (odd[s], even[c]) if x is not None]))
        return out

    half = lax.axis_index("rows") % 2 * (wide // 2)
    for p, panel, even, odd in ((1, p1, even1, odd1), (0, p0, even0, odd0)):
        blocks = slots(panel, even, odd)
        groups = [blocks[:2]] + [[b] for b in blocks[2:]] if p == 1 else [blocks[:3]] + [[b] for b in blocks[3:]]
        coeffs, where, pieces, meets = [], [], [], []
        for group in groups:
            part = jnp.concatenate([sum(dot0(x, current) for x in xs) for _, xs in group], 0)
            coeffs += sum_rows(part, wide, m)
            where += [i * wide + half for i, _ in group] + [i * wide + wide // 2 - half for i, _ in group]
            for i, xs in group:
                pieces += xs
                meets += [i * wide for _ in xs]
        current = update(current, factors[p], coeffs, pieces, jnp.stack(where + meets).astype(jnp.int32))
    return current


def solution(mesh):
    n, m = mesh.shape["vecs"], mesh.shape["rows"]
    in_specs = (P("rows", "vecs"), P(None, "rows", "vecs"), P())
    out_specs = P("rows", "vecs")
    return jax.shard_map(
        functools.partial(body, n, m), mesh=mesh, in_specs=in_specs, out_specs=out_specs, check_vma=False
    )
```

time: 182 us -> 138 us (0.76)
  blocking collectives: 103 us -> 0 us
  starting transfers between devices: 0.04 us -> 29.7 us
  waiting for transfers between devices: 48.8 us -> 73.1 us
  local copies, waits for them, and re-layouts: 3.51 us -> 17.9 us
  between operations: 13.4 us -> 0.58 us
  Pallas kernels: 0 us -> 8.57 us
  matrix products: 12.4 us -> 6.2 us
    psum x2 -> x0, blocking collectives: 103 us -> none  [body(): coeff = lax.psum(partial_value, 'rows').astype(jnp.bfloat16)]
    ppermute x0 -> x35, waiting for transfers between devices: none -> 73.1 us  [the longest x10 51.5 us: send(): return lax.ppermute(x, 'vecs', pairs) if pairs else None]
    all_gather x2 -> x0, waiting for transfers between devices: 48.1 us -> none  [body(): panel = lax.all_gather(reflectors[which], 'vecs', axis=1, tiled=True)]
    ppermute x0 -> x35, starting transfers between devices: none -> 29.7 us  [the longest x25 17.8 us: swap(): return lax.ppermute(x, 'rows', [(i, i ^ bit) for i in range(m)])]
    unnamed x5 -> x50, local copies, waits for them, and re-layouts: 0.21 us -> 13.7 us
    pallas_call x0 -> x2, Pallas kernels: none -> 8.57 us  [update(): pl.pallas_call(functools.partial(update_kernel, len(coeffs), len(panels),...]
    dot_general x4 -> x12, matrix products: 12.4 us -> 6.2 us  [dot0(): lax.dot_general(a, b, (((0,), (0,)), ((), ())), preferred_element_type=F32)]
    squeeze x0 -> x7, local copies, waits for them, and re-layouts: none -> 4.06 us  [the longest x1 2.18 us: body(): p1, p0 = (reflectors[1], reflectors[0])]
  transfers between devices with their start and end apart: 2 -> 35, of which waited for: 1 -> 19; matrix products, arithmetic and copies ran while one was open for 4% -> 6% of each run, Pallas kernels for 0% -> 2%
where the time goes in v1:
time: 138 us; the launch traced here: 137 us
  waiting for transfers between devices  73.1 us (53%)
  starting transfers between devices  29.7 us (22%)
  local copies, waits for them, and re-layouts  17.9 us (13%)
  Pallas kernels  8.57 us (6%)
  matrix products  6.2 us (4%)
    ppermute x10, waiting for transfers between devices, send(): return lax.ppermute(x, 'vecs', pairs) if pairs else None  51.5 us
    ppermute x25, waiting for transfers between devices, swap(): return lax.ppermute(x, 'rows', [(i, i ^ bit) for i in range(m)])  21.7 us
    ppermute x25, starting transfers between devices, swap(): return lax.ppermute(x, 'rows', [(i, i ^ bit) for i in range(m)])  17.8 us
    unnamed x50, local copies, waits for them, and re-layouts  13.7 us
    ppermute x10, starting transfers between devices, send(): return lax.ppermute(x, 'vecs', pairs) if pairs else None  11.9 us
    pallas_call x2, Pallas kernels, update(): pl.pallas_call(functools.partial(update_kernel, len(coeffs), len(panels),...  8.57 us
    dot_general x12, matrix products, dot0(): lax.dot_general(a, b, (((0,), (0,)), ((), ())), preferred_element_type=F32)  6.2 us
  transfers between devices with their start and end apart: 35, of which 19 were waited for; matrix products, arithmetic and copies ran while one was open for 6% of the time, Pallas kernels for 2%

profile of v1, /device:TPU:0, one launch (start us, length us, event | category | flops | bytes accessed | tf_op | source)
XLA Modules:
  0.0 136.6 jit_solution(16979732930507263675)
XLA Ops:
  0.0 2.2 %slice_bitcast_fusion.2 = (bf16[1024,256]{1,0:T(8,128)(2,1)}, bf16[1024,256]{1,0:T(8,128)(2,1)S(1)}) fusion(bf16[2,1024,256]{2,1,0:T(8,128)(2,1)} %param.4), kind=kLoop, calls=%fused_computation.15 | loop fusion | bytes 2097152 | tf_op jit(solution)/shard_map/squeeze | solution.py:113
  2.2 3.0 %collective-permute-start = (bf16[1024,256]{1,0:T(8,128)(2,1)S(1)}, bf16[1024,256]{1,0:T(8,128)(2,1)S(1)}, u32[]{:S(2)}, u32[]{:S(2)}) collective-permute-start(bf16[1024,256]{1,0:T(8,128)(2,1)S(1)} %get-tuple-element.12.refs_6_), channel_id=1, source_target_pairs={{0,1},{1,0},{2,3},{3,2},{4,5},{5,4},{6,7},{7,6},{8,9},{9,8},{10,11... | collective-permute-start | bytes 1572872 | tf_op jit(solution)/shard_map/ppermute | solution.py:103
  5.2 0.7 collective-permute-start.6
  6.3 10.8 %collective-permute-done.refs_7_ = bf16[1024,256]{1,0:T(8,128)(2,1)S(1)} collective-permute-done((bf16[1024,256]{1,0:T(8,128)(2,1)S(1)}, bf16[1024,256]{1,0:T(8,128)(2,1)S(1)}, u32[]{:S(2)}, u32[]{:S(2)}) %collective-permute-start) | collective-permute-done | bytes 524320 | tf_op jit(solution)/shard_map/ppermute | solution.py:103
  17.6 0.7 collective-permute-start.13
  18.3 1.3 collective-permute-start.7
  19.7 2.7 %collective-permute-start.4 = (bf16[2,128,256]{2,1,0:T(8,128)(2,1)S(1)}, bf16[2,128,256]{2,1,0:T(8,128)(2,1)S(1)}, u32[]{:S(2)}, u32[]{:S(2)}) collective-permute-start(bf16[2,128,256]{2,1,0:T(8,128)(2,1)S(1)} %fusion.6), channel_id=1, source_target_pairs={{0,24},{4,28},{8,16},{12,20},{16,8},{20,12},{24,0},{28,4},{1,25},{... | collective-permute-start | bytes 393224 | tf_op jit(solution)/shard_map/ppermute | solution.py:22
  23.6 3.1 %collective-permute-done.4 = bf16[2,128,256]{2,1,0:T(8,128)(2,1)S(1)} collective-permute-done((bf16[2,128,256]{2,1,0:T(8,128)(2,1)S(1)}, bf16[2,128,256]{2,1,0:T(8,128)(2,1)S(1)}, u32[]{:S(2)}, u32[]{:S(2)}) %collective-permute-start.4) | collective-permute-done | bytes 131104 | tf_op jit(solution)/shard_map/ppermute | solution.py:22
  26.7 2.7 %collective-permute-done.3 = bf16[2,128,256]{2,1,0:T(8,128)(2,1)S(1)} collective-permute-done((bf16[2,128,256]{2,1,0:T(8,128)(2,1)S(1)}, bf16[2,128,256]{2,1,0:T(8,128)(2,1)S(1)}, u32[]{:S(2)}, u32[]{:S(2)}) %collective-permute-start.3) | collective-permute-done | bytes 131104 | tf_op jit(solution)/shard_map/ppermute | solution.py:22
  29.8 1.3 collective-permute-start.14
  31.1 5.3 %collective-permute-done.7.refs_9_ = bf16[1024,256]{1,0:T(8,128)(2,1)S(1)} collective-permute-done((bf16[1024,256]{1,0:T(8,128)(2,1)S(1)}, bf16[1024,256]{1,0:T(8,128)(2,1)S(1)}, u32[]{:S(2)}, u32[]{:S(2)}) %collective-permute-start.7) | collective-permute-done | bytes 524320 | tf_op jit(solution)/shard_map/ppermute | solution.py:103
  36.9 1.6 %collective-permute-start.21 = (bf16[1024,256]{1,0:T(8,128)(2,1)}, bf16[1024,256]{1,0:T(8,128)(2,1)}, u32[]{:S(2)}, u32[]{:S(2)}) collective-permute-start(bf16[1024,256]{1,0:T(8,128)(2,1)} %get-tuple-element.7.refs_4_), channel_id=1, source_target_pairs={{1,2},{2,1},{5,6},{6,5},{9,10},{10,9},{13,14},{14,13},{17,18},{18,... | collective-permute-start | bytes 1572872 | tf_op jit(solution)/shard_map/ppermute | solution.py:103
  38.9 9.8 %collective-permute-done.14.refs_11_ = bf16[1024,256]{1,0:T(8,128)(2,1)S(1)} collective-permute-done((bf16[1024,256]{1,0:T(8,128)(2,1)S(1)}, bf16[1024,256]{1,0:T(8,128)(2,1)S(1)}, u32[]{:S(2)}, u32[]{:S(2)}) %collective-permute-start.14) | collective-permute-done | bytes 524320 | tf_op jit(solution)/shard_map/ppermute | solution.py:103
  49.1 2.5 %collective-permute-start.11 = (bf16[1,128,256]{2,1,0:T(8,128)(2,1)S(1)}, bf16[1,128,256]{2,1,0:T(8,128)(2,1)S(1)}, u32[]{:S(2)}, u32[]{:S(2)}) collective-permute-start(bf16[1,128,256]{2,1,0:T(8,128)(2,1)S(1)} %fusion.9), channel_id=1, source_target_pairs={{0,24},{4,28},{8,16},{12,20},{16,8},{20,12},{24,0},{28,4},{1,25},{... | collective-permute-start | bytes 196616 | tf_op jit(solution)/shard_map/ppermute | solution.py:22
  52.7 1.9 %collective-permute-done.11 = bf16[1,128,256]{2,1,0:T(8,128)(2,1)S(1)} collective-permute-done((bf16[1,128,256]{2,1,0:T(8,128)(2,1)S(1)}, bf16[1,128,256]{2,1,0:T(8,128)(2,1)S(1)}, u32[]{:S(2)}, u32[]{:S(2)}) %collective-permute-start.11) | collective-permute-done | bytes 65568 | tf_op jit(solution)/shard_map/ppermute | solution.py:22
  54.6 2.8 %collective-permute-start.18 = (bf16[1,128,256]{2,1,0:T(8,128)(2,1)S(1)}, bf16[1,128,256]{2,1,0:T(8,128)(2,1)S(1)}, u32[]{:S(2)}, u32[]{:S(2)}) collective-permute-start(bf16[1,128,256]{2,1,0:T(8,128)(2,1)S(1)} %fusion.8), channel_id=1, source_target_pairs={{0,24},{4,28},{8,16},{12,20},{16,8},{20,12},{24,0},{28,4},{1,25},{... | collective-permute-start | bytes 196616 | tf_op jit(solution)/shard_map/ppermute | solution.py:22
  58.3 1.5 %collective-permute-done.18 = bf16[1,128,256]{2,1,0:T(8,128)(2,1)S(1)} collective-permute-done((bf16[1,128,256]{2,1,0:T(8,128)(2,1)S(1)}, bf16[1,128,256]{2,1,0:T(8,128)(2,1)S(1)}, u32[]{:S(2)}, u32[]{:S(2)}) %collective-permute-start.18) | collective-permute-done | bytes 65568 | tf_op jit(solution)/shard_map/ppermute | solution.py:22
  59.9 1.8 %collective-permute-done.17 = bf16[1,128,256]{2,1,0:T(8,128)(2,1)S(1)} collective-permute-done((bf16[1,128,256]{2,1,0:T(8,128)(2,1)S(1)}, bf16[1,128,256]{2,1,0:T(8,128)(2,1)S(1)}, u32[]{:S(2)}, u32[]{:S(2)}) %collective-permute-start.17) | collective-permute-done | bytes 65568 | tf_op jit(solution)/shard_map/ppermute | solution.py:22
  62.0 1.8 %slice_bitcast_fusion = (bf16[1024,1024]{1,0:T(8,128)(2,1)}, bf16[1024,1024]{1,0:T(8,128)(2,1)S(1)}) fusion(bf16[2,1024,1024]{2,1,0:T(8,128)(2,1)S(1)} %copy-done.22), kind=kLoop, calls=%fused_computation | loop fusion | bytes 8388608 | tf_op jit(solution)/shard_map/squeeze | solution.py:155
  64.0 1.3 collective-permute-start.22
  66.5 1.6 %copy-done.1 = bf16[1024,1024]{1,0:T(8,128)(2,1)S(1)} copy-done((bf16[1024,1024]{1,0:T(8,128)(2,1)S(1)}, bf16[1024,1024]{1,0:T(8,128)(2,1)}, u32[]{:S(2)}) %copy-start.1) | copy-done | bytes 2097176
  68.1 1.0 copy-done.3
  69.2 1.0 copy-done.5
  70.2 1.0 copy-done.7
  71.2 1.0 copy-done.9
  72.3 1.0 copy-done.11
  73.3 1.0 copy-done.17
  74.4 0.8 copy-done.19
  75.2 0.8 copy-done.21
  76.0 2.9 %shard_map.37.current_ref = bf16[1024,256]{1,0:T(8,128)(2,1)S(1)} custom-call(s32[14]{0:T(128)S(1)} %stack.71.at_ref, bf16[1024,1024]{1,0:T(8,128)(2,1)S(1)} %copy-done.1, bf16[1024,256]{1,0:T(8,128)(2,1)S(1)} %copy-done, bf16[2,128,256]{2,1,0:T(8,128)(2,1)S(1)} %add_convert_fusion.1.refs_0_, bf16[2,128,256]{2,1,0:T(8,128)(2,1)S(1)} %collective-permute-done.5.refs_1_, ...), custom_call_target="tpu_custom_call" | custom-call | flops 1073741824 | bytes 6291456 | tf_op jit(solution)/shard_map/pallas_call | solution.py:79
  79.0 0.7 collective-permute-start.28
  80.1 1.4 %fusion.12 = f32[256,256]{1,0:T(8,128)S(1)} fusion(bf16[1024,256]{1,0:T(8,128)(2,1)} %collective-permute-done.21.refs_6_, bf16[1024,256]{1,0:T(8,128)(2,1)S(1)} %shard_map.37.current_ref), kind=kOutput, calls=%fused_computation.41 | convolution fusion | flops 134217728 | bytes 1310720 | tf_op jit(solution)/shard_map/dot_general | solution.py:18
  81.4 4.2 %collective-permute-done.22.refs_7_ = bf16[1024,256]{1,0:T(8,128)(2,1)S(1)} collective-permute-done((bf16[1024,256]{1,0:T(8,128)(2,1)}, bf16[1024,256]{1,0:T(8,128)(2,1)S(1)}, u32[]{:S(2)}, u32[]{:S(2)}) %collective-permute-start.22) | collective-permute-done | bytes 524320 | tf_op jit(solution)/shard_map/ppermute | solution.py:103
  86.0 1.3 collective-permute-start.29
  87.3 1.4 %convolution_convert_fusion = bf16[256,256]{1,0:T(8,128)(2,1)S(1)} fusion(bf16[1024,256]{1,0:T(8,128)(2,1)} %collective-permute-done.20.refs_5_, bf16[1024,256]{1,0:T(8,128)(2,1)S(1)} %shard_map.37.current_ref), kind=kOutput, calls=%fused_computation.6 | convolution fusion | flops 134283264 | bytes 1179648 | tf_op jit(solution)/shard_map/dot_general | solution.py:18
  89.2 21.3 %collective-permute-done.29.refs_9_ = bf16[1024,256]{1,0:T(8,128)(2,1)S(1)} collective-permute-done((bf16[1024,256]{1,0:T(8,128)(2,1)S(1)}, bf16[1024,256]{1,0:T(8,128)(2,1)S(1)}, u32[]{:S(2)}, u32[]{:S(2)}) %collective-permute-start.29) | collective-permute-done | bytes 524320 | tf_op jit(solution)/shard_map/ppermute | solution.py:103
  110.9 0.8 copy-done.14
  111.8 1.6 %collective-permute-start.26 = (bf16[3,128,256]{2,1,0:T(8,128)(2,1)S(1)}, bf16[3,128,256]{2,1,0:T(8,128)(2,1)S(1)}, u32[]{:S(2)}, u32[]{:S(2)}) collective-permute-start(bf16[3,128,256]{2,1,0:T(8,128)(2,1)S(1)} %fusion.5), channel_id=1, source_target_pairs={{0,24},{4,28},{8,16},{12,20},{16,8},{20,12},{24,0},{28,4},{1,25},{... | collective-permute-start | bytes 589832 | tf_op jit(solution)/shard_map/ppermute | solution.py:22
  114.0 1.4 collective-permute-start.24
  115.4 1.6 %collective-permute-start.33 = (bf16[1,128,256]{2,1,0:T(8,128)(2,1)S(1)}, bf16[1,128,256]{2,1,0:T(8,128)(2,1)S(1)}, u32[]{:S(2)}, u32[]{:S(2)}) collective-permute-start(bf16[1,128,256]{2,1,0:T(8,128)(2,1)S(1)} %fusion.7), channel_id=1, source_target_pairs={{0,24},{4,28},{8,16},{12,20},{16,8},{20,12},{24,0},{28,4},{1,25},{... | collective-permute-start | bytes 196616 | tf_op jit(solution)/shard_map/ppermute | solution.py:22
  117.6 2.9 %collective-permute-done.26 = bf16[3,128,256]{2,1,0:T(8,128)(2,1)S(1)} collective-permute-done((bf16[3,128,256]{2,1,0:T(8,128)(2,1)S(1)}, bf16[3,128,256]{2,1,0:T(8,128)(2,1)S(1)}, u32[]{:S(2)}, u32[]{:S(2)}) %collective-permute-start.26) | collective-permute-done | bytes 196640 | tf_op jit(solution)/shard_map/ppermute | solution.py:22
  121.2 3.6 %collective-permute-done.25 = bf16[3,128,256]{2,1,0:T(8,128)(2,1)S(1)} collective-permute-done((bf16[3,128,256]{2,1,0:T(8,128)(2,1)S(1)}, bf16[3,128,256]{2,1,0:T(8,128)(2,1)S(1)}, u32[]{:S(2)}, u32[]{:S(2)}) %collective-permute-start.25) | collective-permute-done | bytes 196640 | tf_op jit(solution)/shard_map/ppermute | solution.py:22
  125.3 0.9 collective-permute-done.33
  126.1 1.0 collective-permute-done.32
  127.7 1.1 collective-permute-done.34.refs_3_
  128.9 1.0 copy-done.13
  129.9 1.0 copy-done.15
  130.9 5.6 %shard_map.38 = bf16[1024,256]{1,0:T(8,128)(2,1)} custom-call(s32[14]{0:T(128)S(1)} %stack.70.at_ref, bf16[1024,1024]{1,0:T(8,128)(2,1)S(1)} %get-tuple-element.10.factor_ref, bf16[1024,256]{1,0:T(8,128)(2,1)S(1)} %shard_map.37.current_ref, bf16[3,128,256]{2,1,0:T(8,128)(2,1)S(1)} %add_convert_fusion.refs_0_, ...), custom_call_target="tpu_custom_call" | custom-call | flops 1073741824 | bytes 6291456 | tf_op jit(solution)/shard_map/pallas_call | solution.py:79
  (107 shorter events, 12.0 us)
Async XLA Ops:
  0.0 5.9 %copy-start.23 = (bf16[2,1024,256]{2,1,0:T(8,128)(2,1)S(1)}, bf16[2,1024,256]{2,1,0:T(8,128)(2,1)}, u32[]{:S(2)}) copy-start(bf16[2,1024,256]{2,1,0:T(8,128)(2,1)} %param.4) | copy-start | bytes 3145732
  0.0 5.9 %copy-start = (bf16[1024,256]{1,0:T(8,128)(2,1)S(1)}, bf16[1024,256]{1,0:T(8,128)(2,1)}, u32[]{:S(2)}) copy-start(bf16[1024,256]{1,0:T(8,128)(2,1)} %current_ref.1) | copy-start | bytes 1572868
  2.2 21.4 %copy-start.6 = (bf16[1024,256]{1,0:T(8,128)(2,1)}, bf16[1024,256]{1,0:T(8,128)(2,1)S(1)}, u32[]{:S(2)}) copy-start(bf16[1024,256]{1,0:T(8,128)(2,1)S(1)} %get-tuple-element.12.refs_6_) | copy-start | bytes 1572868
  2.2 14.9 %collective-permute-start = (bf16[1024,256]{1,0:T(8,128)(2,1)S(1)}, bf16[1024,256]{1,0:T(8,128)(2,1)S(1)}, u32[]{:S(2)}, u32[]{:S(2)}) collective-permute-start(bf16[1024,256]{1,0:T(8,128)(2,1)S(1)} %get-tuple-element.12.refs_6_), channel_id=1, source_target_pairs={{0,1},{1,0},{2,3},{3,2},{4,5},{5,4},{6,7},{7,6},{8,9},{9,8},{10,11... | collective-permute-start | bytes 1572872 | tf_op jit(solution)/shard_map/ppermute | solution.py:103
  5.2 13.1 %collective-permute-start.6 = (bf16[1024,256]{1,0:T(8,128)(2,1)S(1)}, bf16[1024,256]{1,0:T(8,128)(2,1)S(1)}, u32[]{:S(2)}, u32[]{:S(2)}) collective-permute-start(bf16[1024,256]{1,0:T(8,128)(2,1)S(1)} %get-tuple-element.12.refs_6_), channel_id=1, source_target_pairs={{1,2},{2,1},{5,6},{6,5},{9,10},{10,9},{13,14},{14,13},{17,18},{18,... | collective-permute-start | bytes 1572872 | tf_op jit(solution)/shard_map/ppermute | solution.py:103
  17.1 12.6 %copy-start.16 = (bf16[1024,256]{1,0:T(8,128)(2,1)}, bf16[1024,256]{1,0:T(8,128)(2,1)S(1)}, u32[]{:S(2)}) copy-start(bf16[1024,256]{1,0:T(8,128)(2,1)S(1)} %collective-permute-done.refs_7_) | copy-start | bytes 1572868
  17.5 2.1 %collective-permute-start.1 = (bf16[2,128,256]{2,1,0:T(8,128)(2,1)S(1)}, bf16[2,128,256]{2,1,0:T(8,128)(2,1)S(1)}, u32[]{:S(2)}, u32[]{:S(2)}) collective-permute-start(bf16[2,128,256]{2,1,0:T(8,128)(2,1)S(1)} %dynamic-slice_bitcast_fusion.1), channel_id=1, source_target_pairs={{0,4},{4,0},{8,12},{12,8},{16,20},{20,16},{24,28},{28,24},{1,5},{5... | collective-permute-start | bytes 393224 | tf_op jit(solution)/shard_map/ppermute | solution.py:22
  17.6 12.2 %collective-permute-start.13 = (bf16[1024,256]{1,0:T(8,128)(2,1)S(1)}, bf16[1024,256]{1,0:T(8,128)(2,1)S(1)}, u32[]{:S(2)}, u32[]{:S(2)}) collective-permute-start(bf16[1024,256]{1,0:T(8,128)(2,1)S(1)} %collective-permute-done.refs_7_), channel_id=1, source_target_pairs={{1,2},{2,1},{5,6},{6,5},{9,10},{10,9},{13,14},{14,13},{17,18},{18,... | collective-permute-start | bytes 1572872 | tf_op jit(solution)/shard_map/ppermute | solution.py:103
  18.3 20.5 %copy-start.2 = (bf16[1024,256]{1,0:T(8,128)(2,1)}, bf16[1024,256]{1,0:T(8,128)(2,1)S(1)}, u32[]{:S(2)}) copy-start(bf16[1024,256]{1,0:T(8,128)(2,1)S(1)} %collective-permute-done.6.refs_8_) | copy-start | bytes 1572868
  18.3 18.1 %collective-permute-start.7 = (bf16[1024,256]{1,0:T(8,128)(2,1)S(1)}, bf16[1024,256]{1,0:T(8,128)(2,1)S(1)}, u32[]{:S(2)}, u32[]{:S(2)}) collective-permute-start(bf16[1024,256]{1,0:T(8,128)(2,1)S(1)} %collective-permute-done.6.refs_8_), channel_id=1, source_target_pairs={{1,0},{2,3},{5,4},{6,7},{9,8},{10,11},{13,12},{14,15},{17,16},{18,... | collective-permute-start | bytes 1572872 | tf_op jit(solution)/shard_map/ppermute | solution.py:103
  19.7 7.0 %collective-permute-start.4 = (bf16[2,128,256]{2,1,0:T(8,128)(2,1)S(1)}, bf16[2,128,256]{2,1,0:T(8,128)(2,1)S(1)}, u32[]{:S(2)}, u32[]{:S(2)}) collective-permute-start(bf16[2,128,256]{2,1,0:T(8,128)(2,1)S(1)} %fusion.6), channel_id=1, source_target_pairs={{0,24},{4,28},{8,16},{12,20},{16,8},{20,12},{24,0},{28,4},{1,25},{... | collective-permute-start | bytes 393224 | tf_op jit(solution)/shard_map/ppermute | solution.py:22
  22.4 7.0 %collective-permute-start.3 = (bf16[2,128,256]{2,1,0:T(8,128)(2,1)S(1)}, bf16[2,128,256]{2,1,0:T(8,128)(2,1)S(1)}, u32[]{:S(2)}, u32[]{:S(2)}) collective-permute-start(bf16[2,128,256]{2,1,0:T(8,128)(2,1)S(1)} %fusion.6), channel_id=1, source_target_pairs={{0,16},{4,20},{8,24},{12,28},{16,0},{20,4},{24,8},{28,12},{1,17},{... | collective-permute-start | bytes 393224 | tf_op jit(solution)/shard_map/ppermute | solution.py:22
  22.9 6.7 %collective-permute-start.2 = (bf16[2,128,256]{2,1,0:T(8,128)(2,1)S(1)}, bf16[2,128,256]{2,1,0:T(8,128)(2,1)S(1)}, u32[]{:S(2)}, u32[]{:S(2)}) collective-permute-start(bf16[2,128,256]{2,1,0:T(8,128)(2,1)S(1)} %fusion.6), channel_id=1, source_target_pairs={{0,8},{4,12},{8,0},{12,4},{16,24},{20,28},{24,16},{28,20},{1,9},{5... | collective-permute-start | bytes 393224 | tf_op jit(solution)/shard_map/ppermute | solution.py:22
  29.7 35.5 %collective-permute-start.5 = (bf16[2,128,256]{2,1,0:T(8,128)(2,1)S(1)}, bf16[2,128,256]{2,1,0:T(8,128)(2,1)S(1)}, u32[]{:S(2)}, u32[]{:S(2)}) collective-permute-start(bf16[2,128,256]{2,1,0:T(8,128)(2,1)S(1)} %add_convert_fusion.1.refs_0_), channel_id=1, source_target_pairs={{0,4},{4,0},{8,12},{12,8},{16,20},{20,16},{24,28},{28,24},{1,5},{5... | collective-permute-start | bytes 393224 | tf_op jit(solution)/shard_map/ppermute | solution.py:22
  29.8 19.2 %copy-start.4 = (bf16[1024,256]{1,0:T(8,128)(2,1)}, bf16[1024,256]{1,0:T(8,128)(2,1)S(1)}, u32[]{:S(2)}) copy-start(bf16[1024,256]{1,0:T(8,128)(2,1)S(1)} %collective-permute-done.13.refs_10_) | copy-start | bytes 1572868
  29.8 18.8 %collective-permute-start.14 = (bf16[1024,256]{1,0:T(8,128)(2,1)S(1)}, bf16[1024,256]{1,0:T(8,128)(2,1)S(1)}, u32[]{:S(2)}, u32[]{:S(2)}) collective-permute-start(bf16[1024,256]{1,0:T(8,128)(2,1)S(1)} %collective-permute-done.13.refs_10_), channel_id=1, source_target_pairs={{1,0},{2,3},{5,4},{6,7},{9,8},{10,11},{13,12},{14,15},{17,16},{18,... | collective-permute-start | bytes 1572872 | tf_op jit(solution)/shard_map/ppermute | solution.py:103
  36.4 12.5 %copy-start.8 = (bf16[1024,256]{1,0:T(8,128)(2,1)}, bf16[1024,256]{1,0:T(8,128)(2,1)S(1)}, u32[]{:S(2)}) copy-start(bf16[1024,256]{1,0:T(8,128)(2,1)S(1)} %collective-permute-done.7.refs_9_) | copy-start | bytes 1572868
  36.4 25.6 %copy-start.22 = (bf16[2,1024,1024]{2,1,0:T(8,128)(2,1)S(1)}, bf16[2,1024,1024]{2,1,0:T(8,128)(2,1)}, u32[]{:S(2)}) copy-start(bf16[2,1024,1024]{2,1,0:T(8,128)(2,1)} %param.5) | copy-start | bytes 12582916
  36.8 12.3 %collective-permute-start.8 = (bf16[1,128,256]{2,1,0:T(8,128)(2,1)S(1)}, bf16[1,128,256]{2,1,0:T(8,128)(2,1)S(1)}, u32[]{:S(2)}, u32[]{:S(2)}) collective-permute-start(bf16[1,128,256]{2,1,0:T(8,128)(2,1)S(1)} %dynamic-slice_bitcast_fusion.4), channel_id=1, source_target_pairs={{0,4},{4,0},{8,12},{12,8},{16,20},{20,16},{24,28},{28,24},{1,5},{5... | collective-permute-start | bytes 196616 | tf_op jit(solution)/shard_map/ppermute | solution.py:22
  36.9 27.0 %collective-permute-start.21 = (bf16[1024,256]{1,0:T(8,128)(2,1)}, bf16[1024,256]{1,0:T(8,128)(2,1)}, u32[]{:S(2)}, u32[]{:S(2)}) collective-permute-start(bf16[1024,256]{1,0:T(8,128)(2,1)} %get-tuple-element.7.refs_4_), channel_id=1, source_target_pairs={{1,2},{2,1},{5,6},{6,5},{9,10},{10,9},{13,14},{14,13},{17,18},{18,... | collective-permute-start | bytes 1572872 | tf_op jit(solution)/shard_map/ppermute | solution.py:103
  48.6 13.3 %copy-start.10 = (bf16[1024,256]{1,0:T(8,128)(2,1)}, bf16[1024,256]{1,0:T(8,128)(2,1)S(1)}, u32[]{:S(2)}) copy-start(bf16[1024,256]{1,0:T(8,128)(2,1)S(1)} %collective-permute-done.14.refs_11_) | copy-start | bytes 1572868
  49.0 3.1 %collective-permute-start.15 = (bf16[1,128,256]{2,1,0:T(8,128)(2,1)S(1)}, bf16[1,128,256]{2,1,0:T(8,128)(2,1)S(1)}, u32[]{:S(2)}, u32[]{:S(2)}) collective-permute-start(bf16[1,128,256]{2,1,0:T(8,128)(2,1)S(1)} %dynamic-slice_bitcast_fusion.3), channel_id=1, source_target_pairs={{0,4},{4,0},{8,12},{12,8},{16,20},{20,16},{24,28},{28,24},{1,5},{5... | collective-permute-start | bytes 196616 | tf_op jit(solution)/shard_map/ppermute | solution.py:22
  49.1 5.5 %collective-permute-start.11 = (bf16[1,128,256]{2,1,0:T(8,128)(2,1)S(1)}, bf16[1,128,256]{2,1,0:T(8,128)(2,1)S(1)}, u32[]{:S(2)}, u32[]{:S(2)}) collective-permute-start(bf16[1,128,256]{2,1,0:T(8,128)(2,1)S(1)} %fusion.9), channel_id=1, source_target_pairs={{0,24},{4,28},{8,16},{12,20},{16,8},{20,12},{24,0},{28,4},{1,25},{... | collective-permute-start | bytes 196616 | tf_op jit(solution)/shard_map/ppermute | solution.py:22
  51.6 5.8 %collective-permute-start.10 = (bf16[1,128,256]{2,1,0:T(8,128)(2,1)S(1)}, bf16[1,128,256]{2,1,0:T(8,128)(2,1)S(1)}, u32[]{:S(2)}, u32[]{:S(2)}) collective-permute-start(bf16[1,128,256]{2,1,0:T(8,128)(2,1)S(1)} %fusion.9), channel_id=1, source_target_pairs={{0,16},{4,20},{8,24},{12,28},{16,0},{20,4},{24,8},{28,12},{1,17},{... | collective-permute-start | bytes 196616 | tf_op jit(solution)/shard_map/ppermute | solution.py:22
  52.1 5.5 %collective-permute-start.9 = (bf16[1,128,256]{2,1,0:T(8,128)(2,1)S(1)}, bf16[1,128,256]{2,1,0:T(8,128)(2,1)S(1)}, u32[]{:S(2)}, u32[]{:S(2)}) collective-permute-start(bf16[1,128,256]{2,1,0:T(8,128)(2,1)S(1)} %fusion.9), channel_id=1, source_target_pairs={{0,8},{4,12},{8,0},{12,4},{16,24},{20,28},{24,16},{28,20},{1,9},{5... | collective-permute-start | bytes 196616 | tf_op jit(solution)/shard_map/ppermute | solution.py:22
  54.6 5.3 %collective-permute-start.18 = (bf16[1,128,256]{2,1,0:T(8,128)(2,1)S(1)}, bf16[1,128,256]{2,1,0:T(8,128)(2,1)S(1)}, u32[]{:S(2)}, u32[]{:S(2)}) collective-permute-start(bf16[1,128,256]{2,1,0:T(8,128)(2,1)S(1)} %fusion.8), channel_id=1, source_target_pairs={{0,24},{4,28},{8,16},{12,20},{16,8},{20,12},{24,0},{28,4},{1,25},{... | collective-permute-start | bytes 196616 | tf_op jit(solution)/shard_map/ppermute | solution.py:22
  57.4 4.3 %collective-permute-start.17 = (bf16[1,128,256]{2,1,0:T(8,128)(2,1)S(1)}, bf16[1,128,256]{2,1,0:T(8,128)(2,1)S(1)}, u32[]{:S(2)}, u32[]{:S(2)}) collective-permute-start(bf16[1,128,256]{2,1,0:T(8,128)(2,1)S(1)} %fusion.8), channel_id=1, source_target_pairs={{0,16},{4,20},{8,24},{12,28},{16,0},{20,4},{24,8},{28,12},{1,17},{... | collective-permute-start | bytes 196616 | tf_op jit(solution)/shard_map/ppermute | solution.py:22
  57.6 4.3 %collective-permute-start.16 = (bf16[1,128,256]{2,1,0:T(8,128)(2,1)S(1)}, bf16[1,128,256]{2,1,0:T(8,128)(2,1)S(1)}, u32[]{:S(2)}, u32[]{:S(2)}) collective-permute-start(bf16[1,128,256]{2,1,0:T(8,128)(2,1)S(1)} %fusion.8), channel_id=1, source_target_pairs={{0,8},{4,12},{8,0},{12,4},{16,24},{20,28},{24,16},{28,20},{1,9},{5... | collective-permute-start | bytes 196616 | tf_op jit(solution)/shard_map/ppermute | solution.py:22
  59.9 5.4 %collective-permute-start.12 = (bf16[1,128,256]{2,1,0:T(8,128)(2,1)S(1)}, bf16[1,128,256]{2,1,0:T(8,128)(2,1)S(1)}, u32[]{:S(2)}, u32[]{:S(2)}) collective-permute-start(bf16[1,128,256]{2,1,0:T(8,128)(2,1)S(1)} %add_convert_fusion.4.refs_2_), channel_id=1, source_target_pairs={{0,4},{4,0},{8,12},{12,8},{16,20},{20,16},{24,28},{28,24},{1,5},{5... | collective-permute-start | bytes 196616 | tf_op jit(solution)/shard_map/ppermute | solution.py:22
  61.7 17.3 %collective-permute-start.20 = (bf16[1024,256]{1,0:T(8,128)(2,1)}, bf16[1024,256]{1,0:T(8,128)(2,1)}, u32[]{:S(2)}, u32[]{:S(2)}) collective-permute-start(bf16[1024,256]{1,0:T(8,128)(2,1)} %get-tuple-element.7.refs_4_), channel_id=1, source_target_pairs={{0,1},{1,0},{2,3},{3,2},{4,5},{5,4},{6,7},{7,6},{8,9},{9,8},{10,11... | collective-permute-start | bytes 1572872 | tf_op jit(solution)/shard_map/ppermute | solution.py:103
  62.0 3.9 %collective-permute-start.19 = (bf16[1,128,256]{2,1,0:T(8,128)(2,1)S(1)}, bf16[1,128,256]{2,1,0:T(8,128)(2,1)S(1)}, u32[]{:S(2)}, u32[]{:S(2)}) collective-permute-start(bf16[1,128,256]{2,1,0:T(8,128)(2,1)S(1)} %add_convert_fusion.3.refs_4_), channel_id=1, source_target_pairs={{0,4},{4,0},{8,12},{12,8},{16,20},{20,16},{24,28},{28,24},{1,5},{5... | collective-permute-start | bytes 196616 | tf_op jit(solution)/shard_map/ppermute | solution.py:22
  64.0 21.7 %collective-permute-start.22 = (bf16[1024,256]{1,0:T(8,128)(2,1)}, bf16[1024,256]{1,0:T(8,128)(2,1)S(1)}, u32[]{:S(2)}, u32[]{:S(2)}) collective-permute-start(bf16[1024,256]{1,0:T(8,128)(2,1)} %collective-permute-done.21.refs_6_), channel_id=1, source_target_pairs={{1,0},{2,3},{5,4},{6,7},{9,8},{10,11},{13,12},{14,15},{17,16},{18,... | collective-permute-start | bytes 1572872 | tf_op jit(solution)/shard_map/ppermute | solution.py:103
  66.5 1.6 %copy-start.1 = (bf16[1024,1024]{1,0:T(8,128)(2,1)S(1)}, bf16[1024,1024]{1,0:T(8,128)(2,1)}, u32[]{:S(2)}) copy-start(bf16[1024,1024]{1,0:T(8,128)(2,1)} %get-tuple-element.9.factor_ref) | copy-start | bytes 6291460
  76.0 3.7 %copy-start.24 = (bf16[2,1024,256]{2,1,0:T(8,128)(2,1)S(1)}, bf16[2,1024,256]{2,1,0:T(8,128)(2,1)}, u32[]{:S(2)}) copy-start(bf16[2,1024,256]{2,1,0:T(8,128)(2,1)} %param.4) | copy-start | bytes 3145732
  79.0 7.0 %collective-permute-start.28 = (bf16[1024,256]{1,0:T(8,128)(2,1)}, bf16[1024,256]{1,0:T(8,128)(2,1)S(1)}, u32[]{:S(2)}, u32[]{:S(2)}) collective-permute-start(bf16[1024,256]{1,0:T(8,128)(2,1)} %collective-permute-done.20.refs_5_), channel_id=1, source_target_pairs={{1,2},{2,1},{5,6},{6,5},{9,10},{10,9},{13,14},{14,13},{17,18},{18,... | collective-permute-start | bytes 1572872 | tf_op jit(solution)/shard_map/ppermute | solution.py:103
  85.6 3.5 %copy-start.12 = (bf16[1024,256]{1,0:T(8,128)(2,1)}, bf16[1024,256]{1,0:T(8,128)(2,1)S(1)}, u32[]{:S(2)}) copy-start(bf16[1024,256]{1,0:T(8,128)(2,1)S(1)} %collective-permute-done.22.refs_7_) | copy-start | bytes 1572868
  86.0 24.5 %collective-permute-start.29 = (bf16[1024,256]{1,0:T(8,128)(2,1)S(1)}, bf16[1024,256]{1,0:T(8,128)(2,1)S(1)}, u32[]{:S(2)}, u32[]{:S(2)}) collective-permute-start(bf16[1024,256]{1,0:T(8,128)(2,1)S(1)} %collective-permute-done.28.refs_8_), channel_id=1, source_target_pairs={{1,0},{2,3},{5,4},{6,7},{9,8},{10,11},{13,12},{14,15},{17,16},{18,... | collective-permute-start | bytes 1572872 | tf_op jit(solution)/shard_map/ppermute | solution.py:103
  88.8 22.9 %collective-permute-start.23 = (bf16[3,128,256]{2,1,0:T(8,128)(2,1)S(1)}, bf16[3,128,256]{2,1,0:T(8,128)(2,1)S(1)}, u32[]{:S(2)}, u32[]{:S(2)}) collective-permute-start(bf16[3,128,256]{2,1,0:T(8,128)(2,1)S(1)} %dynamic-slice_bitcast_fusion), channel_id=1, source_target_pairs={{0,4},{4,0},{8,12},{12,8},{16,20},{20,16},{24,28},{28,24},{1,5},{5... | collective-permute-start | bytes 589832 | tf_op jit(solution)/shard_map/ppermute | solution.py:22
  111.7 3.6 %collective-permute-start.30 = (bf16[1,128,256]{2,1,0:T(8,128)(2,1)S(1)}, bf16[1,128,256]{2,1,0:T(8,128)(2,1)S(1)}, u32[]{:S(2)}, u32[]{:S(2)}) collective-permute-start(bf16[1,128,256]{2,1,0:T(8,128)(2,1)S(1)} %dynamic-slice_bitcast_fusion.2), channel_id=1, source_target_pairs={{0,4},{4,0},{8,12},{12,8},{16,20},{20,16},{24,28},{28,24},{1,5},{5... | collective-permute-start | bytes 196616 | tf_op jit(solution)/shard_map/ppermute | solution.py:22
  111.8 8.7 %collective-permute-start.26 = (bf16[3,128,256]{2,1,0:T(8,128)(2,1)S(1)}, bf16[3,128,256]{2,1,0:T(8,128)(2,1)S(1)}, u32[]{:S(2)}, u32[]{:S(2)}) collective-permute-start(bf16[3,128,256]{2,1,0:T(8,128)(2,1)S(1)} %fusion.5), channel_id=1, source_target_pairs={{0,24},{4,28},{8,16},{12,20},{16,8},{20,12},{24,0},{28,4},{1,25},{... | collective-permute-start | bytes 589832 | tf_op jit(solution)/shard_map/ppermute | solution.py:22
  113.4 11.4 %collective-permute-start.25 = (bf16[3,128,256]{2,1,0:T(8,128)(2,1)S(1)}, bf16[3,128,256]{2,1,0:T(8,128)(2,1)S(1)}, u32[]{:S(2)}, u32[]{:S(2)}) collective-permute-start(bf16[3,128,256]{2,1,0:T(8,128)(2,1)S(1)} %fusion.5), channel_id=1, source_target_pairs={{0,16},{4,20},{8,24},{12,28},{16,0},{20,4},{24,8},{28,12},{1,17},{... | collective-permute-start | bytes 589832 | tf_op jit(solution)/shard_map/ppermute | solution.py:22
  114.0 11.1 %collective-permute-start.24 = (bf16[3,128,256]{2,1,0:T(8,128)(2,1)S(1)}, bf16[3,128,256]{2,1,0:T(8,128)(2,1)S(1)}, u32[]{:S(2)}, u32[]{:S(2)}) collective-permute-start(bf16[3,128,256]{2,1,0:T(8,128)(2,1)S(1)} %fusion.5), channel_id=1, source_target_pairs={{0,8},{4,12},{8,0},{12,4},{16,24},{20,28},{24,16},{28,20},{1,9},{5... | collective-permute-start | bytes 589832 | tf_op jit(solution)/shard_map/ppermute | solution.py:22
  115.4 10.7 %collective-permute-start.33 = (bf16[1,128,256]{2,1,0:T(8,128)(2,1)S(1)}, bf16[1,128,256]{2,1,0:T(8,128)(2,1)S(1)}, u32[]{:S(2)}, u32[]{:S(2)}) collective-permute-start(bf16[1,128,256]{2,1,0:T(8,128)(2,1)S(1)} %fusion.7), channel_id=1, source_target_pairs={{0,24},{4,28},{8,16},{12,20},{16,8},{20,12},{24,0},{28,4},{1,25},{... | collective-permute-start | bytes 196616 | tf_op jit(solution)/shard_map/ppermute | solution.py:22
  116.9 10.1 %collective-permute-start.32 = (bf16[1,128,256]{2,1,0:T(8,128)(2,1)S(1)}, bf16[1,128,256]{2,1,0:T(8,128)(2,1)S(1)}, u32[]{:S(2)}, u32[]{:S(2)}) collective-permute-start(bf16[1,128,256]{2,1,0:T(8,128)(2,1)S(1)} %fusion.7), channel_id=1, source_target_pairs={{0,16},{4,20},{8,24},{12,28},{16,0},{20,4},{24,8},{28,12},{1,17},{... | collective-permute-start | bytes 196616 | tf_op jit(solution)/shard_map/ppermute | solution.py:22
  120.5 7.0 %collective-permute-start.31 = (bf16[1,128,256]{2,1,0:T(8,128)(2,1)S(1)}, bf16[1,128,256]{2,1,0:T(8,128)(2,1)S(1)}, u32[]{:S(2)}, u32[]{:S(2)}) collective-permute-start(bf16[1,128,256]{2,1,0:T(8,128)(2,1)S(1)} %fusion.7), channel_id=1, source_target_pairs={{0,8},{4,12},{8,0},{12,4},{16,24},{20,28},{24,16},{28,20},{1,9},{5... | collective-permute-start | bytes 196616 | tf_op jit(solution)/shard_map/ppermute | solution.py:22
  125.2 2.5 %collective-permute-start.27 = (bf16[3,128,256]{2,1,0:T(8,128)(2,1)S(1)}, bf16[3,128,256]{2,1,0:T(8,128)(2,1)}, u32[]{:S(2)}, u32[]{:S(2)}) collective-permute-start(bf16[3,128,256]{2,1,0:T(8,128)(2,1)S(1)} %add_convert_fusion.refs_0_), channel_id=1, source_target_pairs={{0,4},{4,0},{8,12},{12,8},{16,20},{20,16},{24,28},{28,24},{1,5},{5... | collective-permute-start | bytes 589832 | tf_op jit(solution)/shard_map/ppermute | solution.py:22
  127.5 1.3 collective-permute-start.34
  128.9 1.0 copy-start.13
  (12 other events, 11.0 us)

commit v2 on v0

v2 whole, which is shorter than its diff:
```python
import functools

import jax
import jax.numpy as jnp
from jax import lax
from jax.experimental import pallas as pl
from jax.experimental.pallas import tpu as pltpu
from jax.sharding import PartitionSpec as P

F32, BF16 = jnp.float32, jnp.bfloat16
VMEM = 16 << 20
ANY = pl.BlockSpec(memory_space=pl.ANY)
IN_VMEM = pl.BlockSpec(memory_space=pltpu.VMEM)


def after(x, *others):
    return lax.optimization_barrier((x,) + others)[0]


def held(*xs):
    return [x for x in xs if x is not None]


def dot(a, b, ca, cb):
    return lax.dot_general(a, b, (((ca,), (cb,)), ((), ())), preferred_element_type=F32)


def swap(x, bit, m):
    return lax.ppermute(x, "rows", [(i, i ^ bit) for i in range(m)])


def sum_rows(mine, other, m, late=()):
    mine = (mine.astype(F32) + swap(other, 1, m).astype(F32)).astype(BF16)
    bit = 2
    while bit < m:
        got = [swap(mine, s * bit, m) for s in range(1, 4) if s * bit < m]
        mine = sum([after(g, *late).astype(F32) for g in got], mine.astype(F32)).astype(BF16)
        bit *= 4
    return mine, swap(mine, 1, m)


class Part:
    def __init__(self, arrays, blocks, here=None):
        self.arrays, self.blocks, self.here = arrays, blocks, here
        self.count, self.width = len(arrays), arrays[0].shape[1]


def start_parts(parts, refs, panels, sems):
    waits, at, column = [], 0, 0
    for k, part in enumerate(parts):
        place = panels.at[:, pl.ds(column, part.width)]
        copies = [pltpu.make_async_copy(ref, place, sems.at[k]) for ref in refs[at : at + part.count]]
        if part.count == 1:
            copies[0].start()
        else:
            here = part.here(lax.axis_index("vecs"))
            pl.when(here)(copies[0].start)
            pl.when(jnp.logical_not(here))(copies[1].start)
        waits.append(copies[0].wait)
        at += part.count
        column += part.width
    return waits


def coeff_kernel(parts, current_ref, *refs):
    n = sum(part.count for part in parts)
    mine_ref, other_ref, current, panels, sems = refs[n:]
    copy = pltpu.make_async_copy(current_ref, current, sems.at[len(parts)])
    copy.start()
    waits = start_parts(parts, refs[:n], panels, sems)
    copy.wait()
    half = current.shape[0] // 2
    odd = lax.axis_index("rows") % 2 == 1
    column = 0
    for part, wait in zip(parts, waits):
        wait()
        at = slice(column, column + part.width)
        total = dot(current[...], panels[:, at], 1, 0)
        mine_ref[:, at] = jnp.where(odd, total[half:], total[:half]).astype(BF16)
        other_ref[:, at] = jnp.where(odd, total[:half], total[half:]).astype(BF16)
        column += part.width


def update_kernel(p, last, groups, parts, factors_ref, current_ref, *refs):
    n = sum(part.count for part in parts)
    coeff_refs, panel_refs = refs[: 2 * len(groups)], refs[2 * len(groups) : 2 * len(groups) + n]
    out_ref, factor, coeff, scaled, met, current, panels, sems, panel_sems = refs[2 * len(groups) + n :]
    size, half = factor.shape[0], coeff.shape[0] // 2
    r, z = lax.axis_index("rows"), lax.axis_index("vecs")
    copies = []

    def copy(source, target):
        copies.append(pltpu.make_async_copy(source, target, sems.at[len(copies)]))
        copies[-1].start()
        return copies[-1]

    def columns(place, width):
        return pl.ds(pl.multiple_of(place(z), width), width)

    here = copy(current_ref, current)
    first = []
    for k, ref in enumerate(coeff_refs):
        rows = pl.ds(pl.multiple_of(jnp.where(r % 2 == k % 2, 0, half), half), half)
        at = 0
        for part in groups[k // 2]:
            for place, offset, width in part.blocks:
                first.append(copy(ref.at[:, pl.ds(at + offset, width)], coeff.at[rows, columns(place, width)]))
            at += part.width
    tiles = []
    for t in reversed(range(0, size, 256)):
        rows, cols = pl.ds(t, 256), pl.ds(t, size - t)
        tiles.append((t, copy(factors_ref.at[p, rows, cols], factor.at[rows, cols])))
    waits = start_parts(parts, panel_refs, panels, panel_sems)
    here.wait()
    start = current[...].astype(F32)
    if last:
        start = start.T
    for c in first:
        c.wait()
    for t, c in tiles:
        c.wait()
        scaled[:, t : t + 256] = dot(coeff[:, t:], factor[t : t + 256, t:], 1, 1).astype(BF16)
    at = 0
    for part in parts:
        for place, offset, width in part.blocks:
            met[:, at + offset : at + offset + width] = scaled[:, columns(place, width)]
        at += part.width
    for wait in waits:
        wait()
    total = dot(panels[...], met[...], 1, 1) if last else dot(met[...], panels[...], 1, 1)
    out_ref[...] = (start - total).astype(BF16)


def coeff(current, parts):
    columns, rows = current.shape
    size = sum(part.width for part in parts)
    arrays = [x for part in parts for x in part.arrays]
    return pl.pallas_call(
        functools.partial(coeff_kernel, parts),
        in_specs=[ANY] * (1 + len(arrays)),
        out_specs=[IN_VMEM] * 2,
        out_shape=[jax.ShapeDtypeStruct((columns // 2, size), BF16)] * 2,
        scratch_shapes=[
            pltpu.VMEM((columns, rows), BF16),
            pltpu.VMEM((rows, size), BF16),
            pltpu.SemaphoreType.DMA((len(parts) + 1,)),
        ],
        compiler_params=pltpu.CompilerParams(vmem_limit_bytes=VMEM),
        cost_estimate=pl.CostEstimate(flops=2 * size * columns * rows, bytes_accessed=2 * rows * size, transcendentals=0),
    )(current, *arrays)


class Panel:
    def __init__(self, p, current, m):
        self.p, self.current, self.m = p, current, m
        self.groups, self.coeffs = [], []

    def take(self, parts, early=(), late=()):
        mine, other = coeff(after(self.current, *early), parts)
        self.coeffs += sum_rows(mine, other, self.m, late)
        self.groups.append(parts)
        return self.coeffs[-2:]

    def update(self, factors, last):
        columns, rows = self.current.shape
        size = factors.shape[1]
        parts = [part for group in self.groups for part in group]
        arrays = [x for part in parts for x in part.arrays]
        n_copies = 1 + 2 * sum(len(part.blocks) for part in parts) + size // 256
        flops = 2 * size * columns * (size + rows)
        return pl.pallas_call(
            functools.partial(update_kernel, self.p, last, self.groups, parts),
            in_specs=[ANY] * (2 + len(self.coeffs) + len(arrays)),
            out_specs=IN_VMEM,
            out_shape=jax.ShapeDtypeStruct((rows, columns) if last else (columns, rows), BF16),
            scratch_shapes=[
                pltpu.VMEM((size, size), BF16),
                pltpu.VMEM((columns, size), BF16),
                pltpu.VMEM((columns, size), BF16),
                pltpu.VMEM((columns, size), BF16),
                pltpu.VMEM((columns, rows), BF16),
                pltpu.VMEM((rows, size), BF16),
                pltpu.SemaphoreType.DMA((n_copies,)),
                pltpu.SemaphoreType.DMA((len(parts),)),
            ],
            compiler_params=pltpu.CompilerParams(vmem_limit_bytes=VMEM),
            cost_estimate=pl.CostEstimate(flops=flops, bytes_accessed=2 * size * (size + rows), transcendentals=0),
        )(factors, self.current, *self.coeffs, *arrays)


class Line:
    def __init__(self, own, n):
        self.own, self.n, self.even, self.odd = own, n, {}, {}

    def pairs(self, s, parity):
        out = []
        for i in range(parity, self.n - 1, 2):
            out += [(i, i + 1)] if i - s + 1 >= 0 else []
            out += [(i + 1, i)] if i + s < self.n else []
        return out

    def send(self, x, pairs, ready):
        return lax.ppermute(after(x, *ready), "vecs", pairs) if x is not None and pairs else None

    def send_even(self, s, ready):
        self.even[s] = self.send(self.own if s == 1 else self.odd[s - 1], self.pairs(s, 0), ready)
        return held(self.even[s])

    def send_odd(self, s, ready):
        self.odd[s] = self.send(self.own if s == 1 else self.even[s - 1], self.pairs(s, 1), ready)
        return held(self.odd[s])

    def part(self, g):
        n, wide = self.n, self.own.shape[1]

        def index(z, s, parity):
            return jnp.where(z % 2 == parity, z + s, z - s)

        if g == 0:
            return Part([self.own], [(lambda z: z * wide, 0, wide)])
        if g == 1:
            return Part([self.even[1]], [(lambda z: index(z, 1, 0) * wide, 0, wide)])
        s = g - 1
        c = n - s - 1 if s % 2 else n - s + 1

        def here(z):
            i = index(z, s, 1)
            return (i >= 0) & (i < n)

        place = lambda z: jnp.where(here(z), index(z, s, 1), index(z, c, 0)) * wide
        return Part([self.odd[s], self.even[c]], [(place, 0, wide)], here)


def body(n, m, eigvecs, reflectors, factors):
    p1 = reflectors[1]
    p0 = after(reflectors, p1)[0]
    one, zero = Line(p1, n), Line(p0, n)
    panel1 = Panel(1, after(eigvecs, p1).T, m)
    end1 = 3
    ready = []
    for w in range(1, 2 * n - 2):
        got = []
        if w < n:
            got += one.send_even(w, ready) + one.send_odd(w, ready)
        if w == 2:
            zero.send_even(1, ready)
        if w == n - 1:
            got += zero.send_odd(1, ready)
        if 2 <= w - n + 2 < n:
            got += zero.send_even(w - n + 2, ready) + zero.send_odd(w - n + 2, ready)
        if w == n - 1:
            got += panel1.take([one.part(g) for g in range(n) if g != end1], ready, got)
        if w == n:
            got += panel1.take([one.part(end1)], ready)
        if w == n + 1:
            panel0 = Panel(0, after(panel1.update(factors, False), *ready), m)
        if w == 2 * n - 3:
            panel0.take([zero.part(g) for g in range(n) if g != end1], ready, got)
        ready = got
    panel0.take([zero.part(end1)], ready)
    return panel0.update(factors, True)


def plain_body(n, m, eigvecs, reflectors, factors):
    current = eigvecs
    for p in (1, 0):
        panel = lax.all_gather(reflectors[p], "vecs", axis=1, tiled=True)
        mine, other = jnp.split(dot(current, panel, 0, 0).astype(BF16), 2)
        odd = lax.axis_index("rows") % 2 == 1
        mine, other = sum_rows(jnp.where(odd, other, mine), jnp.where(odd, mine, other), m)
        total = jnp.where(odd, jnp.concatenate([other, mine]), jnp.concatenate([mine, other]))
        scaled = dot(factors[p], total, 1, 1).astype(BF16)
        current = (current.astype(F32) - dot(panel, scaled, 1, 0)).astype(BF16)
    return current


def solution(mesh):
    n, m = mesh.shape["vecs"], mesh.shape["rows"]

    def local(eigvecs, reflectors, factors):
        wide, columns, size = reflectors.shape[2], eigvecs.shape[1], factors.shape[1]
        fits = wide % 256 == 0 and columns % 32 == 0 and size % 256 == 0 and n % 2 == 0 and n >= 4
        return (body if fits else plain_body)(n, m, eigvecs, reflectors, factors)

    in_specs = (P("rows", "vecs"), P(None, "rows", "vecs"), P())
    out_specs = P("rows", "vecs")
    return jax.shard_map(local, mesh=mesh, in_specs=in_specs, out_specs=out_specs, check_vma=False)
```

time: 182 us -> 110 us (0.60)
  blocking collectives: 103 us -> 0 us
  starting transfers between devices: 0.04 us -> 32.4 us
  waiting for transfers between devices: 48.8 us -> 62.4 us
  between operations: 13.4 us -> 0.3 us
  matrix products: 12.4 us -> 0 us
  Pallas kernels: 0 us -> 10.5 us
    psum x2 -> x0, blocking collectives: 103 us -> none  [body(): coeff = lax.psum(partial_value, 'rows').astype(jnp.bfloat16)]
    ppermute x0 -> x30, waiting for transfers between devices: none -> 62.4 us  [the longest x10 45.5 us: send(): lax.ppermute(after(x, *ready), 'vecs', pairs)]
    all_gather x2 -> x0, waiting for transfers between devices: 48.1 us -> none  [body(): panel = lax.all_gather(reflectors[which], 'vecs', axis=1, tiled=True)]
    ppermute x0 -> x30, starting transfers between devices: none -> 32.4 us  [the longest x10 17.4 us: send(): lax.ppermute(after(x, *ready), 'vecs', pairs)]
    dot_general x4 -> x0, matrix products: 12.4 us -> none  [the longest x2 7.44 us: body(): update = jnp.dot(panel, scaled, preferred_element_type=jnp.float32)]
    pallas_call x0 -> x6, Pallas kernels: none -> 10.5 us  [the longest x2 6.98 us: update(): pl.pallas_call(functools.partial(update_kernel, self.p, last, self.groups...]
    slice x1 -> x0, local copies, waits for them, and re-layouts: 2.3 us -> none  [body(): panel = lax.all_gather(reflectors[which], 'vecs', axis=1, tiled=True)]
    squeeze x0 -> x2, local copies, waits for them, and re-layouts: none -> 2.15 us  [the longest x1 1.08 us: body(): p0 = after(reflectors, p1)[0]]
  transfers between devices with their start and end apart: 2 -> 30, of which waited for: 1 -> 16; matrix products, arithmetic and copies ran while one was open for 4% -> 2% of each run, Pallas kernels for 0% -> 3%
where the time goes in v2:
time: 110 us; the launch traced here: 109 us
  waiting for transfers between devices  62.4 us (57%)
  starting transfers between devices  32.4 us (29%)
  Pallas kernels  10.5 us (10%)
  local copies, waits for them, and re-layouts  3.41 us (3%)
    ppermute x10, waiting for transfers between devices, send(): lax.ppermute(after(x, *ready), 'vecs', pairs)  45.5 us
    ppermute x10, starting transfers between devices, send(): lax.ppermute(after(x, *ready), 'vecs', pairs)  17.4 us
    ppermute x20, waiting for transfers between devices, swap(): return lax.ppermute(x, 'rows', [(i, i ^ bit) for i in range(m)])  16.9 us
    ppermute x20, starting transfers between devices, swap(): return lax.ppermute(x, 'rows', [(i, i ^ bit) for i in range(m)])  15.1 us
    pallas_call x2, Pallas kernels, update(): pl.pallas_call(functools.partial(update_kernel, self.p, last, self.groups...  6.98 us
    pallas_call x4, Pallas kernels, coeff(): pl.pallas_call(functools.partial(coeff_kernel, parts), in_specs=[ANY] * (...  3.55 us
  transfers between devices with their start and end apart: 30, of which 16 were waited for; matrix products, arithmetic and copies ran while one was open for 2% of the time, Pallas kernels for 3%

profile of v2, /device:TPU:0, one launch (start us, length us, event | category | flops | bytes accessed | tf_op | source)
XLA Modules:
  0.0 109.4 jit_solution(16478786383114283285)
XLA Ops:
  0.0 1.1 slice_bitcast_fusion.1.refs_0_.refs_4_
  1.1 3.1 %collective-permute-start.1 = (bf16[1024,256]{1,0:T(8,128)(2,1)S(1)}, bf16[1024,256]{1,0:T(8,128)(2,1)S(1)}, u32[]{:S(2)}, u32[]{:S(2)}) collective-permute-start(bf16[1024,256]{1,0:T(8,128)(2,1)S(1)} %slice_bitcast_fusion.1.refs_0_.refs_4_), channel_id=1, source_target_pairs={{0,1},{1,0},{2,3},{3,2},{4,5},{5,4},{6,7},{7,6},{8,9},{9,8},{10,11... | collective-permute-start | bytes 1572872 | tf_op jit(solution)/shard_map/ppermute | solution.py:203
  4.2 0.7 collective-permute-start
  4.9 11.2 %collective-permute-done.1.refs_1_.refs_5_ = bf16[1024,256]{1,0:T(8,128)(2,1)S(1)} collective-permute-done((bf16[1024,256]{1,0:T(8,128)(2,1)S(1)}, bf16[1024,256]{1,0:T(8,128)(2,1)S(1)}, u32[]{:S(2)}, u32[]{:S(2)}) %collective-permute-start.1) | collective-permute-done | bytes 524320 | tf_op jit(solution)/shard_map/ppermute | solution.py:203
  16.1 1.3 %collective-permute-start.2 = (bf16[1024,256]{1,0:T(8,128)(2,1)S(1)}, bf16[1024,256]{1,0:T(8,128)(2,1)S(1)}, u32[]{:S(2)}, u32[]{:S(2)}) collective-permute-start(bf16[1024,256]{1,0:T(8,128)(2,1)S(1)} %collective-permute-done.refs_2_.refs_6_), channel_id=1, source_target_pairs={{1,0},{2,3},{5,4},{6,7},{9,8},{10,11},{13,12},{14,15},{17,16},{18,... | collective-permute-start | bytes 1572872 | tf_op jit(solution)/shard_map/ppermute | solution.py:203
  17.4 0.7 collective-permute-start.3
  18.1 1.2 %copy.4 = bf16[1024,256]{0,1:T(8,128)(2,1)S(1)} copy(bf16[1024,256]{1,0:T(8,128)(2,1)} %param.3) | data formatting | bytes 1048576 | tf_op jit(solution)/shard_map/optimization_barrier | solution.py:17
  19.4 13.8 %collective-permute-done.2.refs_3_.refs_7_ = bf16[1024,256]{1,0:T(8,128)(2,1)S(1)} collective-permute-done((bf16[1024,256]{1,0:T(8,128)(2,1)S(1)}, bf16[1024,256]{1,0:T(8,128)(2,1)S(1)}, u32[]{:S(2)}, u32[]{:S(2)}) %collective-permute-start.2) | collective-permute-done | bytes 524320 | tf_op jit(solution)/shard_map/ppermute | solution.py:203
  33.2 1.4 %shard_map.37 = (bf16[128,768]{1,0:T(8,128)(2,1)S(1)}, bf16[128,768]{1,0:T(8,128)(2,1)S(1)}) custom-call(bf16[256,1024]{1,0:T(8,128)(2,1)S(1)} %bitcast.5, bf16[1024,256]{1,0:T(8,128)(2,1)S(1)} %slice_bitcast_fusion.1.refs_0_.refs_4_, bf16[1024,256]{1,0:T(8,128)(2,1)S(1)} %collective-permute-done.1.refs_1_.refs_5_, ...), custom_call_target="tpu_custom_call" | custom-call | flops 402653184 | bytes 1572864 | tf_op jit(solution)/shard_map/pallas_call | solution.py:138
  34.6 1.1 slice_bitcast_fusion.refs_0_.refs_4_
  35.7 1.3 %collective-permute-start.6 = (bf16[1024,256]{1,0:T(8,128)(2,1)S(1)}, bf16[1024,256]{1,0:T(8,128)(2,1)S(1)}, u32[]{:S(2)}, u32[]{:S(2)}) collective-permute-start(bf16[1024,256]{1,0:T(8,128)(2,1)S(1)} %collective-permute-done.3.refs_0_.refs_8_), channel_id=1, source_target_pairs={{1,0},{2,3},{5,4},{6,7},{9,8},{10,11},{13,12},{14,15},{17,16},{18,... | collective-permute-start | bytes 1572872 | tf_op jit(solution)/shard_map/ppermute | solution.py:203
  37.0 0.7 collective-permute-start.7
  37.8 2.5 %collective-permute-start.9 = (bf16[128,768]{1,0:T(8,128)(2,1)S(1)}, bf16[128,768]{1,0:T(8,128)(2,1)S(1)}, u32[]{:S(2)}, u32[]{:S(2)}) collective-permute-start(bf16[128,768]{1,0:T(8,128)(2,1)S(1)} %add_convert_fusion.3), channel_id=1, source_target_pairs={{0,24},{4,28},{8,16},{12,20},{16,8},{20,12},{24,0},{28,4},{1,25},{... | collective-permute-start | bytes 589832 | tf_op jit(solution)/shard_map/ppermute | solution.py:29
  40.3 0.5 collective-permute-start.8
  40.8 0.5 collective-permute-start.5
  41.3 5.1 %collective-permute-done.9 = bf16[128,768]{1,0:T(8,128)(2,1)S(1)} collective-permute-done((bf16[128,768]{1,0:T(8,128)(2,1)S(1)}, bf16[128,768]{1,0:T(8,128)(2,1)S(1)}, u32[]{:S(2)}, u32[]{:S(2)}) %collective-permute-start.9) | collective-permute-done | bytes 196640 | tf_op jit(solution)/shard_map/ppermute | solution.py:29
  46.5 6.4 %collective-permute-start.17 = (bf16[1024,256]{1,0:T(8,128)(2,1)S(1)}, bf16[1024,256]{1,0:T(8,128)(2,1)S(1)}, u32[]{:S(2)}, u32[]{:S(2)}) collective-permute-start(bf16[1024,256]{1,0:T(8,128)(2,1)S(1)} %slice_bitcast_fusion.refs_0_.refs_4_), channel_id=1, source_target_pairs={{0,1},{1,0},{2,3},{3,2},{4,5},{5,4},{6,7},{7,6},{8,9},{9,8},{10,11... | collective-permute-start | bytes 1572872 | tf_op jit(solution)/shard_map/ppermute | solution.py:203
  52.8 0.6 collective-permute-done.6.refs_1_.refs_9_
  53.6 1.4 %collective-permute-done.10.refs_1_ = bf16[128,768]{1,0:T(8,128)(2,1)S(1)} collective-permute-done((bf16[128,768]{1,0:T(8,128)(2,1)S(1)}, bf16[128,768]{1,0:T(8,128)(2,1)S(1)}, u32[]{:S(2)}, u32[]{:S(2)}) %collective-permute-start.10) | collective-permute-done | bytes 196640 | tf_op jit(solution)/shard_map/ppermute | solution.py:29
  55.1 0.4 shard_map.38
  55.5 0.2 collective-permute-start.11
  55.7 1.3 %collective-permute-start.16 = (bf16[1024,256]{1,0:T(8,128)(2,1)S(1)}, bf16[1024,256]{1,0:T(8,128)(2,1)S(1)}, u32[]{:S(2)}, u32[]{:S(2)}) collective-permute-start(bf16[1024,256]{1,0:T(8,128)(2,1)S(1)} %collective-permute-done.7.refs_2_.refs_6_), channel_id=1, source_target_pairs={{1,0},{2,3},{5,4},{6,7},{9,8},{10,11},{13,12},{14,15},{17,16},{18,... | collective-permute-start | bytes 1572872 | tf_op jit(solution)/shard_map/ppermute | solution.py:203
  57.0 8.7 %collective-permute-done.17.refs_1_.refs_5_ = bf16[1024,256]{1,0:T(8,128)(2,1)S(1)} collective-permute-done((bf16[1024,256]{1,0:T(8,128)(2,1)S(1)}, bf16[1024,256]{1,0:T(8,128)(2,1)S(1)}, u32[]{:S(2)}, u32[]{:S(2)}) %collective-permute-start.17) | collective-permute-done | bytes 524320 | tf_op jit(solution)/shard_map/ppermute | solution.py:203
  65.7 0.7 collective-permute-start.18
  66.4 2.5 %collective-permute-start.14 = (bf16[128,256]{1,0:T(8,128)(2,1)S(1)}, bf16[128,256]{1,0:T(8,128)(2,1)S(1)}, u32[]{:S(2)}, u32[]{:S(2)}) collective-permute-start(bf16[128,256]{1,0:T(8,128)(2,1)S(1)} %add_convert_fusion.7), channel_id=1, source_target_pairs={{0,24},{4,28},{8,16},{12,20},{16,8},{20,12},{24,0},{28,4},{1,25},{... | collective-permute-start | bytes 196616 | tf_op jit(solution)/shard_map/ppermute | solution.py:29
  68.9 0.5 collective-permute-start.13
  69.4 0.5 collective-permute-start.12
  70.0 1.7 %collective-permute-done.14 = bf16[128,256]{1,0:T(8,128)(2,1)S(1)} collective-permute-done((bf16[128,256]{1,0:T(8,128)(2,1)S(1)}, bf16[128,256]{1,0:T(8,128)(2,1)S(1)}, u32[]{:S(2)}, u32[]{:S(2)}) %collective-permute-start.14) | collective-permute-done | bytes 65568 | tf_op jit(solution)/shard_map/ppermute | solution.py:29
  71.6 1.6 %collective-permute-done.13 = bf16[128,256]{1,0:T(8,128)(2,1)S(1)} collective-permute-done((bf16[128,256]{1,0:T(8,128)(2,1)S(1)}, bf16[128,256]{1,0:T(8,128)(2,1)S(1)}, u32[]{:S(2)}, u32[]{:S(2)}) %collective-permute-start.13) | collective-permute-done | bytes 65568 | tf_op jit(solution)/shard_map/ppermute | solution.py:29
  73.2 0.5 collective-permute-done.12
  73.8 1.2 %collective-permute-done.15.refs_3_ = bf16[128,256]{1,0:T(8,128)(2,1)S(1)} collective-permute-done((bf16[128,256]{1,0:T(8,128)(2,1)S(1)}, bf16[128,256]{1,0:T(8,128)(2,1)S(1)}, u32[]{:S(2)}, u32[]{:S(2)}) %collective-permute-start.15) | collective-permute-done | bytes 65568 | tf_op jit(solution)/shard_map/ppermute | solution.py:29
  75.1 3.0 %shard_map.39.current_ref = bf16[256,1024]{1,0:T(8,128)(2,1)S(1)} custom-call(bf16[2,1024,1024]{2,1,0:T(8,128)(2,1)S(1)} %copy-done, bf16[256,1024]{1,0:T(8,128)(2,1)S(1)} %bitcast.7, bf16[128,768]{1,0:T(8,128)(2,1)S(1)} %add_convert_fusion.2.refs_0_, bf16[128,768]{1,0:T(8,128)(2,1)S(1)} %collective-permute-done.10.refs_1_, ...), custom_call_target="tpu_custom_call" | custom-call | flops 1073741824 | bytes 4194304 | tf_op jit(solution)/shard_map/pallas_call | solution.py:171
  78.1 1.4 %shard_map.40 = (bf16[128,768]{1,0:T(8,128)(2,1)S(1)}, bf16[128,768]{1,0:T(8,128)(2,1)S(1)}) custom-call(bf16[256,1024]{1,0:T(8,128)(2,1)S(1)} %shard_map.39.current_ref, bf16[1024,256]{1,0:T(8,128)(2,1)S(1)} %slice_bitcast_fusion.refs_0_.refs_4_, bf16[1024,256]{1,0:T(8,128)(2,1)S(1)} %collective-permute-done.17.refs_1_.refs_5_, ...), custom_call_target="tpu_custom_call" | custom-call | flops 402653184 | bytes 1572864 | tf_op jit(solution)/shard_map/pallas_call | solution.py:138
  79.4 0.2 collective-permute-start.19
  79.6 1.3 %collective-permute-start.21 = (bf16[1024,256]{1,0:T(8,128)(2,1)S(1)}, bf16[1024,256]{1,0:T(8,128)(2,1)S(1)}, u32[]{:S(2)}, u32[]{:S(2)}) collective-permute-start(bf16[1024,256]{1,0:T(8,128)(2,1)S(1)} %collective-permute-done.18.refs_0_.refs_8_), channel_id=1, source_target_pairs={{1,0},{2,3},{5,4},{6,7},{9,8},{10,11},{13,12},{14,15},{17,16},{18,... | collective-permute-start | bytes 1572872 | tf_op jit(solution)/shard_map/ppermute | solution.py:203
  81.0 1.6 %collective-permute-start.23 = (bf16[128,768]{1,0:T(8,128)(2,1)S(1)}, bf16[128,768]{1,0:T(8,128)(2,1)S(1)}, u32[]{:S(2)}, u32[]{:S(2)}) collective-permute-start(bf16[128,768]{1,0:T(8,128)(2,1)S(1)} %add_convert_fusion.1), channel_id=1, source_target_pairs={{0,24},{4,28},{8,16},{12,20},{16,8},{20,12},{24,0},{28,4},{1,25},{... | collective-permute-start | bytes 589832 | tf_op jit(solution)/shard_map/ppermute | solution.py:29
  82.6 0.5 collective-permute-start.22
  83.1 1.5 %collective-permute-start.20 = (bf16[128,768]{1,0:T(8,128)(2,1)S(1)}, bf16[128,768]{1,0:T(8,128)(2,1)S(1)}, u32[]{:S(2)}, u32[]{:S(2)}) collective-permute-start(bf16[128,768]{1,0:T(8,128)(2,1)S(1)} %add_convert_fusion.1), channel_id=1, source_target_pairs={{0,8},{4,12},{8,0},{12,4},{16,24},{20,28},{24,16},{28,20},{1,9},{5... | collective-permute-start | bytes 589832 | tf_op jit(solution)/shard_map/ppermute | solution.py:29
  84.6 11.2 %collective-permute-done.21.refs_1_.refs_9_ = bf16[1024,256]{1,0:T(8,128)(2,1)S(1)} collective-permute-done((bf16[1024,256]{1,0:T(8,128)(2,1)S(1)}, bf16[1024,256]{1,0:T(8,128)(2,1)S(1)}, u32[]{:S(2)}, u32[]{:S(2)}) %collective-permute-start.21) | collective-permute-done | bytes 524320 | tf_op jit(solution)/shard_map/ppermute | solution.py:203
  95.7 0.4 shard_map.41
  96.2 1.2 %collective-permute-done.25 = bf16[128,256]{1,0:T(8,128)(2,1)S(1)} collective-permute-done((bf16[128,256]{1,0:T(8,128)(2,1)S(1)}, bf16[128,256]{1,0:T(8,128)(2,1)S(1)}, u32[]{:S(2)}, u32[]{:S(2)}) %collective-permute-start.25) | collective-permute-done | bytes 65568 | tf_op jit(solution)/shard_map/ppermute | solution.py:29
  97.5 1.6 %collective-permute-start.28 = (bf16[128,256]{1,0:T(8,128)(2,1)S(1)}, bf16[128,256]{1,0:T(8,128)(2,1)S(1)}, u32[]{:S(2)}, u32[]{:S(2)}) collective-permute-start(bf16[128,256]{1,0:T(8,128)(2,1)S(1)} %add_convert_fusion.5), channel_id=1, source_target_pairs={{0,24},{4,28},{8,16},{12,20},{16,8},{20,12},{24,0},{28,4},{1,25},{... | collective-permute-start | bytes 196616 | tf_op jit(solution)/shard_map/ppermute | solution.py:29
  99.0 0.5 collective-permute-start.27
  99.5 1.5 %collective-permute-start.26 = (bf16[128,256]{1,0:T(8,128)(2,1)S(1)}, bf16[128,256]{1,0:T(8,128)(2,1)S(1)}, u32[]{:S(2)}, u32[]{:S(2)}) collective-permute-start(bf16[128,256]{1,0:T(8,128)(2,1)S(1)} %add_convert_fusion.5), channel_id=1, source_target_pairs={{0,8},{4,12},{8,0},{12,4},{16,24},{20,28},{24,16},{28,20},{1,9},{5... | collective-permute-start | bytes 196616 | tf_op jit(solution)/shard_map/ppermute | solution.py:29
  101.2 1.6 %collective-permute-done.28 = bf16[128,256]{1,0:T(8,128)(2,1)S(1)} collective-permute-done((bf16[128,256]{1,0:T(8,128)(2,1)S(1)}, bf16[128,256]{1,0:T(8,128)(2,1)S(1)}, u32[]{:S(2)}, u32[]{:S(2)}) %collective-permute-start.28) | collective-permute-done | bytes 65568 | tf_op jit(solution)/shard_map/ppermute | solution.py:29
  102.8 1.2 %collective-permute-done.27 = bf16[128,256]{1,0:T(8,128)(2,1)S(1)} collective-permute-done((bf16[128,256]{1,0:T(8,128)(2,1)S(1)}, bf16[128,256]{1,0:T(8,128)(2,1)S(1)}, u32[]{:S(2)}, u32[]{:S(2)}) %collective-permute-start.27) | collective-permute-done | bytes 65568 | tf_op jit(solution)/shard_map/ppermute | solution.py:29
  104.2 1.2 %collective-permute-done.29.refs_3_ = bf16[128,256]{1,0:T(8,128)(2,1)S(1)} collective-permute-done((bf16[128,256]{1,0:T(8,128)(2,1)S(1)}, bf16[128,256]{1,0:T(8,128)(2,1)S(1)}, u32[]{:S(2)}, u32[]{:S(2)}) %collective-permute-start.29) | collective-permute-done | bytes 65568 | tf_op jit(solution)/shard_map/ppermute | solution.py:29
  105.4 4.0 %shard_map.42 = bf16[1024,256]{1,0:T(8,128)(2,1)} custom-call(bf16[2,1024,1024]{2,1,0:T(8,128)(2,1)S(1)} %copy-done, bf16[256,1024]{1,0:T(8,128)(2,1)S(1)} %shard_map.39.current_ref, bf16[128,768]{1,0:T(8,128)(2,1)S(1)} %add_convert_fusion.refs_0_, bf16[128,768]{1,0:T(8,128)(2,1)S(1)} %collective-permute-done.24.refs_1_, ...), custom_call_target="tpu_custom_call" | custom-call | flops 1073741824 | bytes 4194304 | tf_op jit(solution)/shard_map/pallas_call | solution.py:171
  (31 shorter events, 0.9 us)
Async XLA Ops:
  1.1 15.0 %collective-permute-start.1 = (bf16[1024,256]{1,0:T(8,128)(2,1)S(1)}, bf16[1024,256]{1,0:T(8,128)(2,1)S(1)}, u32[]{:S(2)}, u32[]{:S(2)}) collective-permute-start(bf16[1024,256]{1,0:T(8,128)(2,1)S(1)} %slice_bitcast_fusion.1.refs_0_.refs_4_), channel_id=1, source_target_pairs={{0,1},{1,0},{2,3},{3,2},{4,5},{5,4},{6,7},{7,6},{8,9},{9,8},{10,11... | collective-permute-start | bytes 1572872 | tf_op jit(solution)/shard_map/ppermute | solution.py:203
  4.2 11.9 %collective-permute-start = (bf16[1024,256]{1,0:T(8,128)(2,1)S(1)}, bf16[1024,256]{1,0:T(8,128)(2,1)S(1)}, u32[]{:S(2)}, u32[]{:S(2)}) collective-permute-start(bf16[1024,256]{1,0:T(8,128)(2,1)S(1)} %slice_bitcast_fusion.1.refs_0_.refs_4_), channel_id=1, source_target_pairs={{1,2},{2,1},{5,6},{6,5},{9,10},{10,9},{13,14},{14,13},{17,18},{18,... | collective-permute-start | bytes 1572872 | tf_op jit(solution)/shard_map/ppermute | solution.py:203
  16.1 17.1 %collective-permute-start.2 = (bf16[1024,256]{1,0:T(8,128)(2,1)S(1)}, bf16[1024,256]{1,0:T(8,128)(2,1)S(1)}, u32[]{:S(2)}, u32[]{:S(2)}) collective-permute-start(bf16[1024,256]{1,0:T(8,128)(2,1)S(1)} %collective-permute-done.refs_2_.refs_6_), channel_id=1, source_target_pairs={{1,0},{2,3},{5,4},{6,7},{9,8},{10,11},{13,12},{14,15},{17,16},{18,... | collective-permute-start | bytes 1572872 | tf_op jit(solution)/shard_map/ppermute | solution.py:203
  17.4 15.8 %collective-permute-start.3 = (bf16[1024,256]{1,0:T(8,128)(2,1)S(1)}, bf16[1024,256]{1,0:T(8,128)(2,1)S(1)}, u32[]{:S(2)}, u32[]{:S(2)}) collective-permute-start(bf16[1024,256]{1,0:T(8,128)(2,1)S(1)} %collective-permute-done.1.refs_1_.refs_5_), channel_id=1, source_target_pairs={{1,2},{2,1},{5,6},{6,5},{9,10},{10,9},{13,14},{14,13},{17,18},{18,... | collective-permute-start | bytes 1572872 | tf_op jit(solution)/shard_map/ppermute | solution.py:203
  19.3 55.7 %copy-start = (bf16[2,1024,1024]{2,1,0:T(8,128)(2,1)S(1)}, bf16[2,1024,1024]{2,1,0:T(8,128)(2,1)}, u32[]{:S(2)}) copy-start(bf16[2,1024,1024]{2,1,0:T(8,128)(2,1)} %factors_ref.3) | copy-start | bytes 12582916
  34.5 3.2 %collective-permute-start.4 = (bf16[128,768]{1,0:T(8,128)(2,1)S(1)}, bf16[128,768]{1,0:T(8,128)(2,1)S(1)}, u32[]{:S(2)}, u32[]{:S(2)}) collective-permute-start(bf16[128,768]{1,0:T(8,128)(2,1)S(1)} %get-tuple-element.39), channel_id=1, source_target_pairs={{0,4},{4,0},{8,12},{12,8},{16,20},{20,16},{24,28},{28,24},{1,5},{5... | collective-permute-start | bytes 589832 | tf_op jit(solution)/shard_map/ppermute | solution.py:29
  35.7 17.7 %collective-permute-start.6 = (bf16[1024,256]{1,0:T(8,128)(2,1)S(1)}, bf16[1024,256]{1,0:T(8,128)(2,1)S(1)}, u32[]{:S(2)}, u32[]{:S(2)}) collective-permute-start(bf16[1024,256]{1,0:T(8,128)(2,1)S(1)} %collective-permute-done.3.refs_0_.refs_8_), channel_id=1, source_target_pairs={{1,0},{2,3},{5,4},{6,7},{9,8},{10,11},{13,12},{14,15},{17,16},{18,... | collective-permute-start | bytes 1572872 | tf_op jit(solution)/shard_map/ppermute | solution.py:203
  37.0 16.4 %collective-permute-start.7 = (bf16[1024,256]{1,0:T(8,128)(2,1)S(1)}, bf16[1024,256]{1,0:T(8,128)(2,1)S(1)}, u32[]{:S(2)}, u32[]{:S(2)}) collective-permute-start(bf16[1024,256]{1,0:T(8,128)(2,1)S(1)} %slice_bitcast_fusion.refs_0_.refs_4_), channel_id=1, source_target_pairs={{1,2},{2,1},{5,6},{6,5},{9,10},{10,9},{13,14},{14,13},{17,18},{18,... | collective-permute-start | bytes 1572872 | tf_op jit(solution)/shard_map/ppermute | solution.py:203
  37.8 8.7 %collective-permute-start.9 = (bf16[128,768]{1,0:T(8,128)(2,1)S(1)}, bf16[128,768]{1,0:T(8,128)(2,1)S(1)}, u32[]{:S(2)}, u32[]{:S(2)}) collective-permute-start(bf16[128,768]{1,0:T(8,128)(2,1)S(1)} %add_convert_fusion.3), channel_id=1, source_target_pairs={{0,24},{4,28},{8,16},{12,20},{16,8},{20,12},{24,0},{28,4},{1,25},{... | collective-permute-start | bytes 589832 | tf_op jit(solution)/shard_map/ppermute | solution.py:29
  40.3 13.2 %collective-permute-start.8 = (bf16[128,768]{1,0:T(8,128)(2,1)S(1)}, bf16[128,768]{1,0:T(8,128)(2,1)S(1)}, u32[]{:S(2)}, u32[]{:S(2)}) collective-permute-start(bf16[128,768]{1,0:T(8,128)(2,1)S(1)} %add_convert_fusion.3), channel_id=1, source_target_pairs={{0,16},{4,20},{8,24},{12,28},{16,0},{20,4},{24,8},{28,12},{1,17},{... | collective-permute-start | bytes 589832 | tf_op jit(solution)/shard_map/ppermute | solution.py:29
  40.8 12.7 %collective-permute-start.5 = (bf16[128,768]{1,0:T(8,128)(2,1)S(1)}, bf16[128,768]{1,0:T(8,128)(2,1)S(1)}, u32[]{:S(2)}, u32[]{:S(2)}) collective-permute-start(bf16[128,768]{1,0:T(8,128)(2,1)S(1)} %add_convert_fusion.3), channel_id=1, source_target_pairs={{0,8},{4,12},{8,0},{12,4},{16,24},{20,28},{24,16},{28,20},{1,9},{5... | collective-permute-start | bytes 589832 | tf_op jit(solution)/shard_map/ppermute | solution.py:29
  46.5 19.2 %collective-permute-start.17 = (bf16[1024,256]{1,0:T(8,128)(2,1)S(1)}, bf16[1024,256]{1,0:T(8,128)(2,1)S(1)}, u32[]{:S(2)}, u32[]{:S(2)}) collective-permute-start(bf16[1024,256]{1,0:T(8,128)(2,1)S(1)} %slice_bitcast_fusion.refs_0_.refs_4_), channel_id=1, source_target_pairs={{0,1},{1,0},{2,3},{3,2},{4,5},{5,4},{6,7},{7,6},{8,9},{9,8},{10,11... | collective-permute-start | bytes 1572872 | tf_op jit(solution)/shard_map/ppermute | solution.py:203
  53.5 1.5 %collective-permute-start.10 = (bf16[128,768]{1,0:T(8,128)(2,1)S(1)}, bf16[128,768]{1,0:T(8,128)(2,1)S(1)}, u32[]{:S(2)}, u32[]{:S(2)}) collective-permute-start(bf16[128,768]{1,0:T(8,128)(2,1)S(1)} %add_convert_fusion.2.refs_0_), channel_id=1, source_target_pairs={{0,4},{4,0},{8,12},{12,8},{16,20},{20,16},{24,28},{28,24},{1,5},{5... | collective-permute-start | bytes 589832 | tf_op jit(solution)/shard_map/ppermute | solution.py:29
  55.5 10.9 %collective-permute-start.11 = (bf16[128,256]{1,0:T(8,128)(2,1)S(1)}, bf16[128,256]{1,0:T(8,128)(2,1)S(1)}, u32[]{:S(2)}, u32[]{:S(2)}) collective-permute-start(bf16[128,256]{1,0:T(8,128)(2,1)S(1)} %get-tuple-element.48), channel_id=1, source_target_pairs={{0,4},{4,0},{8,12},{12,8},{16,20},{20,16},{24,28},{28,24},{1,5},{5... | collective-permute-start | bytes 196616 | tf_op jit(solution)/shard_map/ppermute | solution.py:29
  55.7 22.4 %collective-permute-start.16 = (bf16[1024,256]{1,0:T(8,128)(2,1)S(1)}, bf16[1024,256]{1,0:T(8,128)(2,1)S(1)}, u32[]{:S(2)}, u32[]{:S(2)}) collective-permute-start(bf16[1024,256]{1,0:T(8,128)(2,1)S(1)} %collective-permute-done.7.refs_2_.refs_6_), channel_id=1, source_target_pairs={{1,0},{2,3},{5,4},{6,7},{9,8},{10,11},{13,12},{14,15},{17,16},{18,... | collective-permute-start | bytes 1572872 | tf_op jit(solution)/shard_map/ppermute | solution.py:203
  65.7 12.4 %collective-permute-start.18 = (bf16[1024,256]{1,0:T(8,128)(2,1)S(1)}, bf16[1024,256]{1,0:T(8,128)(2,1)S(1)}, u32[]{:S(2)}, u32[]{:S(2)}) collective-permute-start(bf16[1024,256]{1,0:T(8,128)(2,1)S(1)} %collective-permute-done.17.refs_1_.refs_5_), channel_id=1, source_target_pairs={{1,2},{2,1},{5,6},{6,5},{9,10},{10,9},{13,14},{14,13},{17,18},{18,... | collective-permute-start | bytes 1572872 | tf_op jit(solution)/shard_map/ppermute | solution.py:203
  66.4 5.2 %collective-permute-start.14 = (bf16[128,256]{1,0:T(8,128)(2,1)S(1)}, bf16[128,256]{1,0:T(8,128)(2,1)S(1)}, u32[]{:S(2)}, u32[]{:S(2)}) collective-permute-start(bf16[128,256]{1,0:T(8,128)(2,1)S(1)} %add_convert_fusion.7), channel_id=1, source_target_pairs={{0,24},{4,28},{8,16},{12,20},{16,8},{20,12},{24,0},{28,4},{1,25},{... | collective-permute-start | bytes 196616 | tf_op jit(solution)/shard_map/ppermute | solution.py:29
  68.9 4.3 %collective-permute-start.13 = (bf16[128,256]{1,0:T(8,128)(2,1)S(1)}, bf16[128,256]{1,0:T(8,128)(2,1)S(1)}, u32[]{:S(2)}, u32[]{:S(2)}) collective-permute-start(bf16[128,256]{1,0:T(8,128)(2,1)S(1)} %add_convert_fusion.7), channel_id=1, source_target_pairs={{0,16},{4,20},{8,24},{12,28},{16,0},{20,4},{24,8},{28,12},{1,17},{... | collective-permute-start | bytes 196616 | tf_op jit(solution)/shard_map/ppermute | solution.py:29
  69.4 4.3 %collective-permute-start.12 = (bf16[128,256]{1,0:T(8,128)(2,1)S(1)}, bf16[128,256]{1,0:T(8,128)(2,1)S(1)}, u32[]{:S(2)}, u32[]{:S(2)}) collective-permute-start(bf16[128,256]{1,0:T(8,128)(2,1)S(1)} %add_convert_fusion.7), channel_id=1, source_target_pairs={{0,8},{4,12},{8,0},{12,4},{16,24},{20,28},{24,16},{28,20},{1,9},{5... | collective-permute-start | bytes 196616 | tf_op jit(solution)/shard_map/ppermute | solution.py:29
  73.7 1.3 %collective-permute-start.15 = (bf16[128,256]{1,0:T(8,128)(2,1)S(1)}, bf16[128,256]{1,0:T(8,128)(2,1)S(1)}, u32[]{:S(2)}, u32[]{:S(2)}) collective-permute-start(bf16[128,256]{1,0:T(8,128)(2,1)S(1)} %add_convert_fusion.6.refs_2_), channel_id=1, source_target_pairs={{0,4},{4,0},{8,12},{12,8},{16,20},{20,16},{24,28},{28,24},{1,5},{5... | collective-permute-start | bytes 196616 | tf_op jit(solution)/shard_map/ppermute | solution.py:29
  79.4 1.5 %collective-permute-start.19 = (bf16[128,768]{1,0:T(8,128)(2,1)S(1)}, bf16[128,768]{1,0:T(8,128)(2,1)S(1)}, u32[]{:S(2)}, u32[]{:S(2)}) collective-permute-start(bf16[128,768]{1,0:T(8,128)(2,1)S(1)} %get-tuple-element.55), channel_id=1, source_target_pairs={{0,4},{4,0},{8,12},{12,8},{16,20},{20,16},{24,28},{28,24},{1,5},{5... | collective-permute-start | bytes 589832 | tf_op jit(solution)/shard_map/ppermute | solution.py:29
  79.6 16.1 %collective-permute-start.21 = (bf16[1024,256]{1,0:T(8,128)(2,1)S(1)}, bf16[1024,256]{1,0:T(8,128)(2,1)S(1)}, u32[]{:S(2)}, u32[]{:S(2)}) collective-permute-start(bf16[1024,256]{1,0:T(8,128)(2,1)S(1)} %collective-permute-done.18.refs_0_.refs_8_), channel_id=1, source_target_pairs={{1,0},{2,3},{5,4},{6,7},{9,8},{10,11},{13,12},{14,15},{17,16},{18,... | collective-permute-start | bytes 1572872 | tf_op jit(solution)/shard_map/ppermute | solution.py:203
  81.0 15.2 %collective-permute-start.23 = (bf16[128,768]{1,0:T(8,128)(2,1)S(1)}, bf16[128,768]{1,0:T(8,128)(2,1)S(1)}, u32[]{:S(2)}, u32[]{:S(2)}) collective-permute-start(bf16[128,768]{1,0:T(8,128)(2,1)S(1)} %add_convert_fusion.1), channel_id=1, source_target_pairs={{0,24},{4,28},{8,16},{12,20},{16,8},{20,12},{24,0},{28,4},{1,25},{... | collective-permute-start | bytes 589832 | tf_op jit(solution)/shard_map/ppermute | solution.py:29
  82.6 13.7 %collective-permute-start.22 = (bf16[128,768]{1,0:T(8,128)(2,1)S(1)}, bf16[128,768]{1,0:T(8,128)(2,1)S(1)}, u32[]{:S(2)}, u32[]{:S(2)}) collective-permute-start(bf16[128,768]{1,0:T(8,128)(2,1)S(1)} %add_convert_fusion.1), channel_id=1, source_target_pairs={{0,16},{4,20},{8,24},{12,28},{16,0},{20,4},{24,8},{28,12},{1,17},{... | collective-permute-start | bytes 589832 | tf_op jit(solution)/shard_map/ppermute | solution.py:29
  83.1 13.2 %collective-permute-start.20 = (bf16[128,768]{1,0:T(8,128)(2,1)S(1)}, bf16[128,768]{1,0:T(8,128)(2,1)S(1)}, u32[]{:S(2)}, u32[]{:S(2)}) collective-permute-start(bf16[128,768]{1,0:T(8,128)(2,1)S(1)} %add_convert_fusion.1), channel_id=1, source_target_pairs={{0,8},{4,12},{8,0},{12,4},{16,24},{20,28},{24,16},{28,20},{1,9},{5... | collective-permute-start | bytes 589832 | tf_op jit(solution)/shard_map/ppermute | solution.py:29
  96.1 1.3 %collective-permute-start.25 = (bf16[128,256]{1,0:T(8,128)(2,1)S(1)}, bf16[128,256]{1,0:T(8,128)(2,1)S(1)}, u32[]{:S(2)}, u32[]{:S(2)}) collective-permute-start(bf16[128,256]{1,0:T(8,128)(2,1)S(1)} %get-tuple-element.62), channel_id=1, source_target_pairs={{0,4},{4,0},{8,12},{12,8},{16,20},{20,16},{24,28},{28,24},{1,5},{5... | collective-permute-start | bytes 196616 | tf_op jit(solution)/shard_map/ppermute | solution.py:29
  97.5 5.3 %collective-permute-start.28 = (bf16[128,256]{1,0:T(8,128)(2,1)S(1)}, bf16[128,256]{1,0:T(8,128)(2,1)S(1)}, u32[]{:S(2)}, u32[]{:S(2)}) collective-permute-start(bf16[128,256]{1,0:T(8,128)(2,1)S(1)} %add_convert_fusion.5), channel_id=1, source_target_pairs={{0,24},{4,28},{8,16},{12,20},{16,8},{20,12},{24,0},{28,4},{1,25},{... | collective-permute-start | bytes 196616 | tf_op jit(solution)/shard_map/ppermute | solution.py:29
  99.0 5.0 %collective-permute-start.27 = (bf16[128,256]{1,0:T(8,128)(2,1)S(1)}, bf16[128,256]{1,0:T(8,128)(2,1)S(1)}, u32[]{:S(2)}, u32[]{:S(2)}) collective-permute-start(bf16[128,256]{1,0:T(8,128)(2,1)S(1)} %add_convert_fusion.5), channel_id=1, source_target_pairs={{0,16},{4,20},{8,24},{12,28},{16,0},{20,4},{24,8},{28,12},{1,17},{... | collective-permute-start | bytes 196616 | tf_op jit(solution)/shard_map/ppermute | solution.py:29
  99.5 4.5 %collective-permute-start.26 = (bf16[128,256]{1,0:T(8,128)(2,1)S(1)}, bf16[128,256]{1,0:T(8,128)(2,1)S(1)}, u32[]{:S(2)}, u32[]{:S(2)}) collective-permute-start(bf16[128,256]{1,0:T(8,128)(2,1)S(1)} %add_convert_fusion.5), channel_id=1, source_target_pairs={{0,8},{4,12},{8,0},{12,4},{16,24},{20,28},{24,16},{28,20},{1,9},{5... | collective-permute-start | bytes 196616 | tf_op jit(solution)/shard_map/ppermute | solution.py:29
  101.1 4.3 %collective-permute-start.24 = (bf16[128,768]{1,0:T(8,128)(2,1)S(1)}, bf16[128,768]{1,0:T(8,128)(2,1)S(1)}, u32[]{:S(2)}, u32[]{:S(2)}) collective-permute-start(bf16[128,768]{1,0:T(8,128)(2,1)S(1)} %add_convert_fusion.refs_0_), channel_id=1, source_target_pairs={{0,4},{4,0},{8,12},{12,8},{16,20},{20,16},{24,28},{28,24},{1,5},{5... | collective-permute-start | bytes 589832 | tf_op jit(solution)/shard_map/ppermute | solution.py:29
  104.1 1.3 %collective-permute-start.29 = (bf16[128,256]{1,0:T(8,128)(2,1)S(1)}, bf16[128,256]{1,0:T(8,128)(2,1)S(1)}, u32[]{:S(2)}, u32[]{:S(2)}) collective-permute-start(bf16[128,256]{1,0:T(8,128)(2,1)S(1)} %add_convert_fusion.4.refs_2_), channel_id=1, source_target_pairs={{0,4},{4,0},{8,12},{12,8},{16,20},{20,16},{24,28},{28,24},{1,5},{5... | collective-permute-start | bytes 196616 | tf_op jit(solution)/shard_map/ppermute | solution.py:29

commit v3 on v0

v3 whole, which is shorter than its diff:
```python
import functools

import jax
import jax.numpy as jnp
from jax import lax
from jax.experimental import pallas as pl
from jax.experimental.pallas import tpu as pltpu
from jax.sharding import PartitionSpec as P

F32, BF16 = jnp.float32, jnp.bfloat16
VMEM = 16 << 20
ANY = pl.BlockSpec(memory_space=pl.ANY)
IN_VMEM = pl.BlockSpec(memory_space=pltpu.VMEM)


def after(x, *others):
    return lax.optimization_barrier((x,) + others)[0]


def held(*xs):
    return [x for x in xs if x is not None]


def dot(a, b, ca, cb):
    return lax.dot_general(a, b, (((ca,), (cb,)), ((), ())), preferred_element_type=F32)


def swap(x, bit, m):
    return lax.ppermute(x, "rows", [(i, i ^ bit) for i in range(m)])


class Part:
    def __init__(self, arrays, blocks, here=None):
        self.arrays, self.blocks, self.here = arrays, blocks, here
        self.rows, self.width = [x.shape[0] for x in arrays], arrays[0].shape[1]


def start_parts(parts, refs, panels, sems):
    waits, at, column = [], 0, 0
    for k, part in enumerate(parts):
        columns = pl.ds(column, part.width)
        whole = pltpu.make_async_copy(refs[at], panels.at[:, columns], sems.at[k])
        if part.here is None:
            whole.start()
        else:
            here = part.here(lax.axis_index("vecs"))
            pl.when(here)(whole.start)
            row = 0
            for i, rows in enumerate(part.rows[1:]):
                place = panels.at[pl.ds(row, rows), columns]
                piece = pltpu.make_async_copy(refs[at + 1 + i], place, sems.at[k])
                pl.when(jnp.logical_not(here))(piece.start)
                row += rows
        waits.append(whole.wait)
        at += len(part.rows)
        column += part.width
    return waits


def coeff_kernel(parts, current_ref, *refs):
    n = sum(len(part.rows) for part in parts)
    mine_ref, other_ref, current, panels, sems = refs[n:]
    copy = pltpu.make_async_copy(current_ref, current, sems.at[len(parts)])
    copy.start()
    waits = start_parts(parts, refs[:n], panels, sems)
    copy.wait()
    half = current.shape[0] // 2
    odd = lax.axis_index("rows") % 2 == 1
    column = 0
    for part, wait in zip(parts, waits):
        wait()
        at = slice(column, column + part.width)
        total = dot(current[...], panels[:, at], 1, 0)
        mine_ref[:, at] = jnp.where(odd, total[half:], total[:half]).astype(BF16)
        other_ref[:, at] = jnp.where(odd, total[:half], total[half:]).astype(BF16)
        column += part.width


class Copies:
    def __init__(self, sems):
        self.sems, self.count = sems, 0

    def __call__(self, source, target):
        copy = pltpu.make_async_copy(source, target, self.sems.at[self.count])
        self.count += 1
        copy.start()
        return copy.wait


def columns_at(place, width):
    return pl.ds(pl.multiple_of(place(lax.axis_index("vecs")), width), width)


def half_rows(whose, half):
    own = lax.axis_index("rows") % 2
    return pl.ds(pl.multiple_of(jnp.where(own == whose, 0, half), half), half)


def scale_kernel(p, groups, factors_ref, *refs):
    coeff_refs, (out_ref, factor, coeff, sems) = refs[: 2 * len(groups)], refs[2 * len(groups) :]
    size, half = factor.shape[0], coeff.shape[0] // 2
    copy = Copies(sems)
    tiles = []
    for t in reversed(range(0, size, 256)):
        rows, cols = pl.ds(t, 256), pl.ds(t, size - t)
        tiles.append((t, copy(factors_ref.at[p, rows, cols], factor.at[rows, cols])))
    coeff[...] = jnp.zeros_like(coeff)
    waits = []
    for k, ref in enumerate(coeff_refs):
        at = 0
        for part in groups[k // 2]:
            for place, offset, width in part.blocks:
                target = coeff.at[half_rows(k % 2, half), columns_at(place, width)]
                waits.append(copy(ref.at[:, pl.ds(at + offset, width)], target))
            at += part.width
    for wait in waits:
        wait()
    plain = coeff[...].T
    for t, wait in tiles:
        wait()
        out_ref[t : t + 256] = dot(factor[t : t + 256, t:], plain[t:], 1, 0).astype(BF16)


def prepare_kernel(p, last, parts, late, factors_ref, current_ref, scaled_ref, *refs):
    n = sum(len(part.rows) for part in parts)
    rest_ref, across_ref, current, met, panels, sems, panel_sems = refs[n:]
    columns = current.shape[0]
    copy = Copies(sems)
    parts_there = start_parts(parts, refs[:n], panels, panel_sems)
    waits = [copy(current_ref, current)]
    at = 0
    for part in parts:
        for place, offset, width in part.blocks:
            rows, there = pl.ds(at + offset, width), columns_at(place, width)
            waits.append(copy(scaled_ref.at[there], met.at[rows, pl.ds(0, columns)]))
            to = columns
            for other in late:
                for other_place, other_offset, other_width in other.blocks:
                    source = factors_ref.at[p, there, columns_at(other_place, other_width)]
                    waits.append(copy(source, met.at[rows, pl.ds(to + other_offset, other_width)]))
                to += other.width
        at += part.width
    for wait in waits + parts_there:
        wait()
    product = dot(panels[...], met[...], 1, 0)
    across_ref[...] = product[:, columns:].astype(BF16)
    if last:
        rest_ref[...] = current[...].astype(F32).T - product[:, :columns]
    else:
        rest_ref[...] = current[...].astype(F32) - product[:, :columns].T


def finish_kernel(last, rest_ref, across_ref, own_ref, other_ref, out_ref, rest, across, coeff, sems):
    copy = Copies(sems)
    half = coeff.shape[0] // 2
    waits = [copy(rest_ref, rest), copy(across_ref, across)]
    waits += [copy(ref, coeff.at[half_rows(k, half)]) for k, ref in enumerate((own_ref, other_ref))]
    for wait in waits:
        wait()
    product = dot(across[...], coeff[...], 1, 1) if last else dot(coeff[...], across[...], 1, 1)
    out_ref[...] = (rest[...] - product).astype(BF16)


def call(kernel, inputs, outs, scratch, flops):
    return pl.pallas_call(
        kernel,
        in_specs=[ANY] * len(inputs),
        out_specs=[IN_VMEM] * len(outs),
        out_shape=[jax.ShapeDtypeStruct(shape, dtype) for shape, dtype in outs],
        scratch_shapes=scratch,
        compiler_params=pltpu.CompilerParams(vmem_limit_bytes=VMEM),
        cost_estimate=pl.CostEstimate(
            flops=flops, bytes_accessed=sum(x.size * x.dtype.itemsize for x in inputs), transcendentals=0
        ),
    )(*inputs)


def arrays_of(parts):
    return [x for part in parts for x in part.arrays]


def scale(p, factors, groups, coeffs):
    size, columns = factors.shape[1], 2 * coeffs[0].shape[0]
    n_copies = size // 256 + 2 * sum(len(part.blocks) for group in groups for part in group)
    scratch = [
        pltpu.VMEM((size, size), BF16),
        pltpu.VMEM((columns, size), BF16),
        pltpu.SemaphoreType.DMA((n_copies,)),
    ]
    kernel = functools.partial(scale_kernel, p, groups)
    return call(kernel, [factors, *coeffs], [((size, columns), BF16)], scratch, size * size * columns)[0]


def prepare(p, last, factors, current, scaled, parts, late):
    columns, rows = current.shape
    size = factors.shape[1]
    more = sum(part.width for part in late)
    n_copies = 1 + sum(len(part.blocks) for part in parts) * (1 + sum(len(part.blocks) for part in late))
    scratch = [
        pltpu.VMEM((columns, rows), BF16),
        pltpu.VMEM((size, columns + more), BF16),
        pltpu.VMEM((rows, size), BF16),
        pltpu.SemaphoreType.DMA((n_copies,)),
        pltpu.SemaphoreType.DMA((len(parts),)),
    ]
    outs = [((rows, columns) if last else (columns, rows), F32), ((rows, more), BF16)]
    kernel = functools.partial(prepare_kernel, p, last, parts, late)
    inputs = [factors, current, scaled, *arrays_of(parts)]
    return call(kernel, inputs, outs, scratch, 2 * rows * size * (columns + more))


def finish(last, rest, across, coeffs):
    rows, more = across.shape
    columns = rest.size // rows
    scratch = [
        pltpu.VMEM(rest.shape, F32),
        pltpu.VMEM(across.shape, BF16),
        pltpu.VMEM((columns, more), BF16),
        pltpu.SemaphoreType.DMA((4,)),
    ]
    kernel = functools.partial(finish_kernel, last)
    return call(kernel, [rest, across, *coeffs], [(rest.shape, BF16)], scratch, 2 * rows * more * columns)[0]


def coeff(current, parts):
    columns, rows = current.shape
    size = sum(part.width for part in parts)
    arrays = [x for part in parts for x in part.arrays]
    return pl.pallas_call(
        functools.partial(coeff_kernel, parts),
        in_specs=[ANY] * (1 + len(arrays)),
        out_specs=[IN_VMEM] * 2,
        out_shape=[jax.ShapeDtypeStruct((columns // 2, size), BF16)] * 2,
        scratch_shapes=[
            pltpu.VMEM((columns, rows), BF16),
            pltpu.VMEM((rows, size), BF16),
            pltpu.SemaphoreType.DMA((len(parts) + 1,)),
        ],
        compiler_params=pltpu.CompilerParams(vmem_limit_bytes=VMEM),
        cost_estimate=pl.CostEstimate(flops=2 * size * columns * rows, bytes_accessed=2 * rows * size, transcendentals=0),
    )(current, *arrays)


GROUPS = {1: ((0, 1, 2), (3,)), 0: ((0, 1, 2), (3,))}
PIECES = {"O": 1, "F3": 1}
JOINED = "swap"
GATES = {
    "P0": ("p1",),
    "X": ("p1",),
    "E2": ("M1",),
    "M2": ("M1",),
    "E3": ("E2",),
    "N1": ("E2", "M2"),
    "c1.0": ("E3", "N1"),
    "a1.0": ("E2", "M2"),
    "a1.1": ("d1.0", "N1"),
    "N2": ("d1.0", "E3"),
    "F2": ("d1.0", "E3"),
    "F3": ("F2",),
    "a0.0": ("N2", "F2"),
    "c0.0": ("F3",),
}


class Steps:
    def __init__(self, n, m, eigvecs, reflectors, factors):
        self.n, self.m, self.factors = n, m, factors
        self.eigvecs, self.reflectors = eigvecs, reflectors
        self.z = lax.axis_index("vecs")
        self.made = {}

    def __call__(self, name):
        if name not in self.made:
            self.made[name] = None
            self.made[name] = self.make(name)
        if self.made[name] is None:
            raise ValueError("circular gates")
        return self.made[name]

    def gated(self, name, x):
        others = []
        for other in GATES.get(name, ()):
            got = self(other)
            others += list(got) if isinstance(got, (tuple, list)) else [got]
        return after(x, *others) if others else x

    def send(self, name, x, pairs):
        return lax.ppermute(self.gated(name, x), "vecs", pairs)

    def pieces(self, name, x, pairs):
        size = x.shape[0] // PIECES[name]
        return [self.send(name, x[k * size : (k + 1) * size], pairs) for k in range(PIECES[name])]

    def make(self, name):
        n, z = self.n, self.z
        outer = [(i, i ^ 1) for i in range(n)]
        inward, outward = [(0, 1), (n - 1, n - 2)], [(1, 0), (n - 2, n - 1)]
        middle, skip = [(1, 2), (2, 1)], [(2, 0), (n - 3, n - 1)]
        at_end = (z == 0) | (z == n - 1)
        if name == "p1":
            return self.reflectors[1]
        if name == "P0":
            return self.gated(name, self.reflectors)[0]
        if name == "X":
            return self.gated(name, self.eigvecs).T
        if name == "E1":
            return self.send(name, self("p1"), outer)
        if name == "M1":
            return self.send(name, self("p1"), middle)
        if name == "E2":
            if JOINED == "E2":
                return self.send(name, jnp.where(at_end, self("P0"), self("M1")), outer)
            return self.send(name, self("M1"), outward)
        if name == "M2":
            return self.send(name, self("E1"), middle)
        if name == "E3":
            return self.send(name, self("M2"), outward)
        if name == "E3s":
            return self.send(name, self("E1"), skip)
        if name == "I":
            if JOINED == "E2":
                return self("E2")
            return self.send(name, self("P0"), outer if JOINED == "swap" else inward)
        if name == "O":
            return self.pieces(name, self("P0"), outward)
        if name == "N1":
            return self.send(name, self("P0"), middle)
        if name == "N2":
            return self.send(name, self("I"), middle)
        if name == "F2":
            return self.send(name, self("N1"), outward)
        if name == "F3":
            return self.pieces(name, self("N2"), outward)
        step, p = name[0], int(name[1])
        groups = [[self.part(p, g) for g in group] for group in GROUPS[p]]
        late = len(groups) - 1
        if step == "S":
            coeffs = [self(f"{what}{p}.{k}") for k in range(late) for what in "cd"]
            return scale(p, self.gated(name, self.factors), groups[:late], coeffs)
        if step == "Y":
            current = self.gated(name, self("X" if p else "U1"))
            return prepare(p, p == 0, self.factors, current, self(f"S{p}"), sum(groups, []), groups[late])
        if step == "U":
            rest, across = self(f"Y{p}")
            coeffs = [self(f"{what}{p}.{late}") for what in "cd"]
            return finish(p == 0, self.gated(name, rest), across, coeffs)
        k = int(name[3:])
        if step == "a":
            return coeff(self.gated(name, self("U1" if p == 0 else "X")), groups[k])
        if step == "b":
            mine, other = self("a" + name[1:])
            got = self.gated(name, swap(other, 1, self.m))
            return (mine.astype(F32) + got.astype(F32)).astype(BF16)
        if step == "c":
            mine, bit = self("b" + name[1:]), 2
            while bit < self.m:
                got = [swap(mine, s * bit, self.m) for s in range(1, 4) if s * bit < self.m]
                mine = sum([self.gated(name, g).astype(F32) for g in got], mine.astype(F32)).astype(BF16)
                bit *= 4
            return mine
        return swap(self.gated(name, self("c" + name[1:])), 1, self.m)

    def part(self, p, g):
        n, wide = self.n, self.reflectors.shape[2]

        def inner(z):
            return (z > 0) & (z < n - 1)

        places = (
            lambda z: z,
            lambda z: z + 1 - 2 * (z % 2),
            lambda z: jnp.where(inner(z), n - 1 - z, (z + 2) % n),
            lambda z: jnp.where(inner(z), (z + 2) % n, n - 1 - z),
        )
        if p == 1:
            arrays = (["p1"], ["E1"], ["M1", "E2"], ["M2", "E3"])[g]
        else:
            arrays = (["P0"], ["I"] if JOINED == "swap" else ["I", "O"], ["N1", "F2"], ["N2", "F3"])[g]
        found = []
        for name in arrays:
            got = self(name)
            found += got if isinstance(got, list) else [got]
        blocks = [(lambda z: places[g](z) * wide, 0, wide)]
        return Part(found, blocks, inner if len(found) > 1 else None)


def swap_sum(mine, other, m):
    mine = (mine.astype(F32) + swap(other, 1, m).astype(F32)).astype(BF16)
    bit = 2
    while bit < m:
        got = [swap(mine, s * bit, m) for s in range(1, 4) if s * bit < m]
        mine = sum([g.astype(F32) for g in got], mine.astype(F32)).astype(BF16)
        bit *= 4
    return mine, swap(mine, 1, m)


def plain_body(n, m, eigvecs, reflectors, factors):
    current = eigvecs
    for p in (1, 0):
        panel = lax.all_gather(reflectors[p], "vecs", axis=1, tiled=True)
        mine, other = jnp.split(dot(current, panel, 0, 0).astype(BF16), 2)
        odd = lax.axis_index("rows") % 2 == 1
        mine, other = swap_sum(jnp.where(odd, other, mine), jnp.where(odd, mine, other), m)
        total = jnp.where(odd, jnp.concatenate([other, mine]), jnp.concatenate([mine, other]))
        scaled = dot(factors[p], total, 1, 1).astype(BF16)
        current = (current.astype(F32) - dot(panel, scaled, 1, 0)).astype(BF16)
    return current


def solution(mesh):
    n, m = mesh.shape["vecs"], mesh.shape["rows"]

    def local(eigvecs, reflectors, factors):
        wide, columns, size = reflectors.shape[2], eigvecs.shape[1], factors.shape[1]
        fits = n == 4 and wide % 128 == 0 and columns % 32 == 0 and size % 256 == 0
        if fits:
            return Steps(n, m, eigvecs, reflectors, factors)("U0")
        return plain_body(n, m, eigvecs, reflectors, factors)

    in_specs = (P("rows", "vecs"), P(None, "rows", "vecs"), P())
    out_specs = P("rows", "vecs")
    return jax.shard_map(local, mesh=mesh, in_specs=in_specs, out_specs=out_specs, check_vma=False)
```

time: 182 us -> 112 us (0.62)
  blocking collectives: 103 us -> 0 us
  starting transfers between devices: 0.04 us -> 35.3 us
  between operations: 13.4 us -> 0.34 us
  Pallas kernels: 0 us -> 12.8 us
  matrix products: 12.4 us -> 0 us
  waiting for transfers between devices: 48.8 us -> 58.9 us
    psum x2 -> x0, blocking collectives: 103 us -> none  [body(): coeff = lax.psum(partial_value, 'rows').astype(jnp.bfloat16)]
    ppermute x0 -> x30, waiting for transfers between devices: none -> 58.9 us  [the longest x10 45.4 us: send(): return lax.ppermute(self.gated(name, x), 'vecs', pairs)]
    all_gather x2 -> x0, waiting for transfers between devices: 48.1 us -> none  [body(): panel = lax.all_gather(reflectors[which], 'vecs', axis=1, tiled=True)]
    ppermute x0 -> x30, starting transfers between devices: none -> 35.3 us  [the longest x10 20.3 us: send(): return lax.ppermute(self.gated(name, x), 'vecs', pairs)]
    pallas_call x0 -> x10, Pallas kernels: none -> 12.8 us  [the longest x6 9.25 us: call(): pl.pallas_call(kernel, in_specs=[ANY] * len(inputs), out_specs=[IN_VMEM]...]
    dot_general x4 -> x0, matrix products: 12.4 us -> none  [the longest x2 7.44 us: body(): update = jnp.dot(panel, scaled, preferred_element_type=jnp.float32)]
    slice x1 -> x0, local copies, waits for them, and re-layouts: 2.3 us -> none  [body(): panel = lax.all_gather(reflectors[which], 'vecs', axis=1, tiled=True)]
    squeeze x0 -> x2, local copies, waits for them, and re-layouts: none -> 2.15 us  [the longest x1 1.08 us: make(): return self.gated(name, self.reflectors)[0]]
  transfers between devices with their start and end apart: 2 -> 30, of which waited for: 1 -> 16; matrix products, arithmetic and copies ran while one was open for 4% -> 2% of each run, Pallas kernels for 0% -> 8%
where the time goes in v3:
time: 112 us; the launch traced here: 111 us
  waiting for transfers between devices  58.9 us (53%)
  starting transfers between devices  35.3 us (32%)
  Pallas kernels  12.8 us (11%)
  local copies, waits for them, and re-layouts  3.41 us (3%)
    ppermute x10, waiting for transfers between devices, send(): return lax.ppermute(self.gated(name, x), 'vecs', pairs)  45.4 us
    ppermute x10, starting transfers between devices, send(): return lax.ppermute(self.gated(name, x), 'vecs', pairs)  20.3 us
    ppermute x20, starting transfers between devices, swap(): return lax.ppermute(x, 'rows', [(i, i ^ bit) for i in range(m)])  14.9 us
    ppermute x20, waiting for transfers between devices, swap(): return lax.ppermute(x, 'rows', [(i, i ^ bit) for i in range(m)])  13.5 us
    pallas_call x6, Pallas kernels, call(): pl.pallas_call(kernel, in_specs=[ANY] * len(inputs), out_specs=[IN_VMEM]...  9.25 us
    pallas_call x4, Pallas kernels, coeff(): pl.pallas_call(functools.partial(coeff_kernel, parts), in_specs=[ANY] * (...  3.52 us
  transfers between devices with their start and end apart: 30, of which 16 were waited for; matrix products, arithmetic and copies ran while one was open for 2% of the time, Pallas kernels for 8%

profile of v3, /device:TPU:0, one launch (start us, length us, event | category | flops | bytes accessed | tf_op | source)
XLA Modules:
  0.0 111.1 jit_solution(13872649889770565794)
XLA Ops:
  0.0 1.1 slice_bitcast_fusion.1.refs_0_
  1.1 0.7 collective-permute-start
  1.8 5.9 %collective-permute-start.2 = (bf16[1024,256]{1,0:T(8,128)(2,1)S(1)}, bf16[1024,256]{1,0:T(8,128)(2,1)S(1)}, u32[]{:S(2)}, u32[]{:S(2)}) collective-permute-start(bf16[1024,256]{1,0:T(8,128)(2,1)S(1)} %slice_bitcast_fusion.1.refs_0_), channel_id=1, source_target_pairs={{0,1},{1,0},{2,3},{3,2},{4,5},{5,4},{6,7},{7,6},{8,9},{9,8},{10,11... | collective-permute-start | bytes 1572872 | tf_op jit(solution)/shard_map/ppermute | solution.py:288
  7.7 1.3 %collective-permute-start.1 = (bf16[1024,256]{1,0:T(8,128)(2,1)S(1)}, bf16[1024,256]{1,0:T(8,128)(2,1)S(1)}, u32[]{:S(2)}, u32[]{:S(2)}) collective-permute-start(bf16[1024,256]{1,0:T(8,128)(2,1)S(1)} %collective-permute-done.refs_2_), channel_id=1, source_target_pairs={{1,0},{2,3},{5,4},{6,7},{9,8},{10,11},{13,12},{14,15},{17,16},{18,... | collective-permute-start | bytes 1572872 | tf_op jit(solution)/shard_map/ppermute | solution.py:288
  9.0 10.4 %collective-permute-done.2.refs_1_ = bf16[1024,256]{1,0:T(8,128)(2,1)S(1)} collective-permute-done((bf16[1024,256]{1,0:T(8,128)(2,1)S(1)}, bf16[1024,256]{1,0:T(8,128)(2,1)S(1)}, u32[]{:S(2)}, u32[]{:S(2)}) %collective-permute-start.2) | collective-permute-done | bytes 524320 | tf_op jit(solution)/shard_map/ppermute | solution.py:288
  19.3 0.7 collective-permute-start.3
  20.0 1.2 %copy.4 = bf16[1024,256]{0,1:T(8,128)(2,1)S(1)} copy(bf16[1024,256]{1,0:T(8,128)(2,1)} %param.3) | data formatting | bytes 1048576 | tf_op jit(solution)/shard_map/optimization_barrier | solution.py:17
  21.3 10.7 %collective-permute-done.1.refs_3_ = bf16[1024,256]{1,0:T(8,128)(2,1)S(1)} collective-permute-done((bf16[1024,256]{1,0:T(8,128)(2,1)S(1)}, bf16[1024,256]{1,0:T(8,128)(2,1)S(1)}, u32[]{:S(2)}, u32[]{:S(2)}) %collective-permute-start.1) | collective-permute-done | bytes 524320 | tf_op jit(solution)/shard_map/ppermute | solution.py:288
  32.0 1.3 %shard_map.37 = (bf16[128,768]{1,0:T(8,128)(2,1)S(1)}, bf16[128,768]{1,0:T(8,128)(2,1)S(1)}) custom-call(bf16[256,1024]{1,0:T(8,128)(2,1)S(1)} %bitcast.5, bf16[1024,256]{1,0:T(8,128)(2,1)S(1)} %slice_bitcast_fusion.1.refs_0_, bf16[1024,256]{1,0:T(8,128)(2,1)S(1)} %collective-permute-done.2.refs_1_, bf16[1024,256]{1,0:T(8,128)(2,1)S(1)} %collective-permute-done.refs_2_, ...), custom_call_target="tpu_custom_call" | custom-call | flops 402653184 | bytes 1572864 | tf_op jit(solution)/shard_map/pallas_call | solution.py:229
  33.4 1.1 slice_bitcast_fusion.refs_0_
  34.5 1.3 %collective-permute-start.6 = (bf16[1024,256]{1,0:T(8,128)(2,1)S(1)}, bf16[1024,256]{1,0:T(8,128)(2,1)S(1)}, u32[]{:S(2)}, u32[]{:S(2)}) collective-permute-start(bf16[1024,256]{1,0:T(8,128)(2,1)S(1)} %collective-permute-done.3.refs_4_.refs_0_), channel_id=1, source_target_pairs={{1,0},{2,3},{5,4},{6,7},{9,8},{10,11},{13,12},{14,15},{17,16},{18,... | collective-permute-start | bytes 1572872 | tf_op jit(solution)/shard_map/ppermute | solution.py:288
  35.8 0.7 collective-permute-start.7
  36.6 2.5 %collective-permute-start.9 = (bf16[128,768]{1,0:T(8,128)(2,1)S(1)}, bf16[128,768]{1,0:T(8,128)(2,1)S(1)}, u32[]{:S(2)}, u32[]{:S(2)}) collective-permute-start(bf16[128,768]{1,0:T(8,128)(2,1)S(1)} %add_convert_fusion.3), channel_id=1, source_target_pairs={{0,24},{4,28},{8,16},{12,20},{16,8},{20,12},{24,0},{28,4},{1,25},{... | collective-permute-start | bytes 589832 | tf_op jit(solution)/shard_map/ppermute | solution.py:29
  39.1 0.5 collective-permute-start.8
  39.6 0.5 collective-permute-start.5
  40.1 5.1 %collective-permute-done.9 = bf16[128,768]{1,0:T(8,128)(2,1)S(1)} collective-permute-done((bf16[128,768]{1,0:T(8,128)(2,1)S(1)}, bf16[128,768]{1,0:T(8,128)(2,1)S(1)}, u32[]{:S(2)}, u32[]{:S(2)}) %collective-permute-start.9) | collective-permute-done | bytes 196640 | tf_op jit(solution)/shard_map/ppermute | solution.py:29
  45.3 6.6 %collective-permute-start.16 = (bf16[1024,256]{1,0:T(8,128)(2,1)S(1)}, bf16[1024,256]{1,0:T(8,128)(2,1)S(1)}, u32[]{:S(2)}, u32[]{:S(2)}) collective-permute-start(bf16[1024,256]{1,0:T(8,128)(2,1)S(1)} %slice_bitcast_fusion.refs_0_), channel_id=1, source_target_pairs={{0,1},{1,0},{2,3},{3,2},{4,5},{5,4},{6,7},{7,6},{8,9},{9,8},{10,11... | collective-permute-start | bytes 1572872 | tf_op jit(solution)/shard_map/ppermute | solution.py:288
  52.4 1.4 %collective-permute-done.10.refs_1_ = bf16[128,768]{1,0:T(8,128)(2,1)S(1)} collective-permute-done((bf16[128,768]{1,0:T(8,128)(2,1)S(1)}, bf16[128,768]{1,0:T(8,128)(2,1)S(1)}, u32[]{:S(2)}, u32[]{:S(2)}) %collective-permute-start.10) | collective-permute-done | bytes 196640 | tf_op jit(solution)/shard_map/ppermute | solution.py:29
  53.9 0.4 shard_map.40
  54.5 8.8 %collective-permute-done.16.refs_1_ = bf16[1024,256]{1,0:T(8,128)(2,1)S(1)} collective-permute-done((bf16[1024,256]{1,0:T(8,128)(2,1)S(1)}, bf16[1024,256]{1,0:T(8,128)(2,1)S(1)}, u32[]{:S(2)}, u32[]{:S(2)}) %collective-permute-start.16) | collective-permute-done | bytes 524320 | tf_op jit(solution)/shard_map/ppermute | solution.py:288
  63.3 0.7 collective-permute-start.17
  64.0 1.3 %collective-permute-start.18 = (bf16[1024,256]{1,0:T(8,128)(2,1)S(1)}, bf16[1024,256]{1,0:T(8,128)(2,1)S(1)}, u32[]{:S(2)}, u32[]{:S(2)}) collective-permute-start(bf16[1024,256]{1,0:T(8,128)(2,1)S(1)} %collective-permute-done.7.refs_2_), channel_id=1, source_target_pairs={{1,0},{2,3},{5,4},{6,7},{9,8},{10,11},{13,12},{14,15},{17,16},{18,... | collective-permute-start | bytes 1572872 | tf_op jit(solution)/shard_map/ppermute | solution.py:288
  65.3 2.5 %collective-permute-start.14 = (bf16[128,256]{1,0:T(8,128)(2,1)S(1)}, bf16[128,256]{1,0:T(8,128)(2,1)S(1)}, u32[]{:S(2)}, u32[]{:S(2)}) collective-permute-start(bf16[128,256]{1,0:T(8,128)(2,1)S(1)} %add_convert_fusion.7), channel_id=1, source_target_pairs={{0,24},{4,28},{8,16},{12,20},{16,8},{20,12},{24,0},{28,4},{1,25},{... | collective-permute-start | bytes 196616 | tf_op jit(solution)/shard_map/ppermute | solution.py:29
  67.8 0.5 collective-permute-start.13
  68.3 0.5 collective-permute-start.12
  68.9 1.7 %shard_map.38.scaled_ref = bf16[1024,256]{1,0:T(8,128)(2,1)S(1)} custom-call(bf16[2,1024,1024]{2,1,0:T(8,128)(2,1)S(1)} %copy-done, bf16[128,768]{1,0:T(8,128)(2,1)S(1)} %add_convert_fusion.2.refs_0_, bf16[128,768]{1,0:T(8,128)(2,1)S(1)} %collective-permute-done.10.refs_1_), custom_call_target="tpu_custom_call" | custom-call | flops 268435456 | bytes 4587520 | tf_op jit(solution)/shard_map/pallas_call | solution.py:165
  70.5 0.5 collective-permute-done.14
  71.0 1.1 collective-permute-done.13
  72.1 0.5 collective-permute-done.12
  72.7 1.9 %shard_map.39 = (f32[256,1024]{1,0:T(8,128)S(1)}, bf16[1024,256]{1,0:T(8,128)(2,1)S(1)}) custom-call(bf16[2,1024,1024]{2,1,0:T(8,128)(2,1)S(1)} %copy-done, bf16[256,1024]{1,0:T(8,128)(2,1)S(1)} %bitcast.7, bf16[1024,256]{1,0:T(8,128)(2,1)S(1)} %shard_map.38.scaled_ref, bf16[1024,256]{1,0:T(8,128)(2,1)S(1)} %slice_bitcast_fusion.1.refs_0_, ...), custom_call_target="tpu_custom_call" | custom-call | flops 1073741824 | bytes 8388608 | tf_op jit(solution)/shard_map/pallas_call | solution.py:165
  74.6 0.7 shard_map.41.current_ref
  75.3 4.0 %collective-permute-done.18.refs_3_ = bf16[1024,256]{1,0:T(8,128)(2,1)S(1)} collective-permute-done((bf16[1024,256]{1,0:T(8,128)(2,1)S(1)}, bf16[1024,256]{1,0:T(8,128)(2,1)S(1)}, u32[]{:S(2)}, u32[]{:S(2)}) %collective-permute-start.18) | collective-permute-done | bytes 524320 | tf_op jit(solution)/shard_map/ppermute | solution.py:288
  79.3 1.3 %shard_map.42 = (bf16[128,768]{1,0:T(8,128)(2,1)S(1)}, bf16[128,768]{1,0:T(8,128)(2,1)S(1)}) custom-call(bf16[256,1024]{1,0:T(8,128)(2,1)S(1)} %shard_map.41.current_ref, bf16[1024,256]{1,0:T(8,128)(2,1)S(1)} %slice_bitcast_fusion.refs_0_, bf16[1024,256]{1,0:T(8,128)(2,1)S(1)} %collective-permute-done.16.refs_1_, ...), custom_call_target="tpu_custom_call" | custom-call | flops 402653184 | bytes 1572864 | tf_op jit(solution)/shard_map/pallas_call | solution.py:229
  80.7 1.3 %collective-permute-start.21 = (bf16[1024,256]{1,0:T(8,128)(2,1)S(1)}, bf16[1024,256]{1,0:T(8,128)(2,1)S(1)}, u32[]{:S(2)}, u32[]{:S(2)}) collective-permute-start(bf16[1024,256]{1,0:T(8,128)(2,1)S(1)} %collective-permute-done.17.refs_4_.refs_0_), channel_id=1, source_target_pairs={{1,0},{2,3},{5,4},{6,7},{9,8},{10,11},{13,12},{14,15},{17,16},{18,... | collective-permute-start | bytes 1572872 | tf_op jit(solution)/shard_map/ppermute | solution.py:288
  82.2 2.5 %collective-permute-start.23 = (bf16[128,768]{1,0:T(8,128)(2,1)S(1)}, bf16[128,768]{1,0:T(8,128)(2,1)S(1)}, u32[]{:S(2)}, u32[]{:S(2)}) collective-permute-start(bf16[128,768]{1,0:T(8,128)(2,1)S(1)} %add_convert_fusion.1), channel_id=1, source_target_pairs={{0,24},{4,28},{8,16},{12,20},{16,8},{20,12},{24,0},{28,4},{1,25},{... | collective-permute-start | bytes 589832 | tf_op jit(solution)/shard_map/ppermute | solution.py:29
  84.7 0.5 collective-permute-start.22
  85.3 0.5 collective-permute-start.20
  85.8 11.2 %collective-permute-done.21.refs_5_.refs_1_ = bf16[1024,256]{1,0:T(8,128)(2,1)S(1)} collective-permute-done((bf16[1024,256]{1,0:T(8,128)(2,1)S(1)}, bf16[1024,256]{1,0:T(8,128)(2,1)S(1)}, u32[]{:S(2)}, u32[]{:S(2)}) %collective-permute-start.21) | collective-permute-done | bytes 524320 | tf_op jit(solution)/shard_map/ppermute | solution.py:288
  97.5 1.2 %collective-permute-done.25 = bf16[128,256]{1,0:T(8,128)(2,1)S(1)} collective-permute-done((bf16[128,256]{1,0:T(8,128)(2,1)S(1)}, bf16[128,256]{1,0:T(8,128)(2,1)S(1)}, u32[]{:S(2)}, u32[]{:S(2)}) %collective-permute-start.25) | collective-permute-done | bytes 65568 | tf_op jit(solution)/shard_map/ppermute | solution.py:29
  98.7 2.5 %collective-permute-start.28 = (bf16[128,256]{1,0:T(8,128)(2,1)S(1)}, bf16[128,256]{1,0:T(8,128)(2,1)S(1)}, u32[]{:S(2)}, u32[]{:S(2)}) collective-permute-start(bf16[128,256]{1,0:T(8,128)(2,1)S(1)} %add_convert_fusion.5), channel_id=1, source_target_pairs={{0,24},{4,28},{8,16},{12,20},{16,8},{20,12},{24,0},{28,4},{1,25},{... | collective-permute-start | bytes 196616 | tf_op jit(solution)/shard_map/ppermute | solution.py:29
  101.2 0.5 collective-permute-start.27
  101.7 0.5 collective-permute-start.26
  102.4 1.5 %collective-permute-done.28 = bf16[128,256]{1,0:T(8,128)(2,1)S(1)} collective-permute-done((bf16[128,256]{1,0:T(8,128)(2,1)S(1)}, bf16[128,256]{1,0:T(8,128)(2,1)S(1)}, u32[]{:S(2)}, u32[]{:S(2)}) %collective-permute-start.28) | collective-permute-done | bytes 65568 | tf_op jit(solution)/shard_map/ppermute | solution.py:29
  104.0 1.5 %collective-permute-done.27 = bf16[128,256]{1,0:T(8,128)(2,1)S(1)} collective-permute-done((bf16[128,256]{1,0:T(8,128)(2,1)S(1)}, bf16[128,256]{1,0:T(8,128)(2,1)S(1)}, u32[]{:S(2)}, u32[]{:S(2)}) %collective-permute-start.27) | collective-permute-done | bytes 65568 | tf_op jit(solution)/shard_map/ppermute | solution.py:29
  105.5 0.5 collective-permute-done.26
  106.1 1.7 %shard_map.43.scaled_ref = bf16[1024,256]{1,0:T(8,128)(2,1)S(1)} custom-call(bf16[2,1024,1024]{2,1,0:T(8,128)(2,1)S(1)} %copy-done, bf16[128,768]{1,0:T(8,128)(2,1)S(1)} %add_convert_fusion.refs_0_, bf16[128,768]{1,0:T(8,128)(2,1)S(1)} %collective-permute-done.24.refs_1_), custom_call_target="tpu_custom_call" | custom-call | flops 268435456 | bytes 4587520 | tf_op jit(solution)/shard_map/pallas_call | solution.py:165
  107.8 1.8 %shard_map.44 = (f32[1024,256]{1,0:T(8,128)S(1)}, bf16[1024,256]{1,0:T(8,128)(2,1)S(1)}) custom-call(bf16[2,1024,1024]{2,1,0:T(8,128)(2,1)S(1)} %copy-done, bf16[256,1024]{1,0:T(8,128)(2,1)S(1)} %shard_map.41.current_ref, bf16[1024,256]{1,0:T(8,128)(2,1)S(1)} %shard_map.43.scaled_ref, bf16[1024,256]{1,0:T(8,128)(2,1)S(1)} %slice_bitcast_fusion.refs_0_, ...), custom_call_target="tpu_custom_call" | custom-call | flops 1073741824 | bytes 8388608 | tf_op jit(solution)/shard_map/pallas_call | solution.py:165
  109.7 1.5 %shard_map.46 = bf16[1024,256]{1,0:T(8,128)(2,1)} custom-call(f32[1024,256]{1,0:T(8,128)S(1)} %get-tuple-element.61.rest_ref, bf16[1024,256]{1,0:T(8,128)(2,1)S(1)} %get-tuple-element.62.across_ref, bf16[128,256]{1,0:T(8,128)(2,1)S(1)} %add_convert_fusion.4.own_ref, bf16[128,256]{1,0:T(8,128)(2,1)S(1)} %collective-permute-done.29.other_ref), custom_call_target="tpu_custom_call" | custom-call | flops 134217728 | bytes 1703936 | tf_op jit(solution)/shard_map/pallas_call | solution.py:165
  (35 shorter events, 2.1 us)
Async XLA Ops:
  1.1 6.6 %collective-permute-start = (bf16[1024,256]{1,0:T(8,128)(2,1)S(1)}, bf16[1024,256]{1,0:T(8,128)(2,1)S(1)}, u32[]{:S(2)}, u32[]{:S(2)}) collective-permute-start(bf16[1024,256]{1,0:T(8,128)(2,1)S(1)} %slice_bitcast_fusion.1.refs_0_), channel_id=1, source_target_pairs={{1,2},{2,1},{5,6},{6,5},{9,10},{10,9},{13,14},{14,13},{17,18},{18,... | collective-permute-start | bytes 1572872 | tf_op jit(solution)/shard_map/ppermute | solution.py:288
  1.8 17.5 %collective-permute-start.2 = (bf16[1024,256]{1,0:T(8,128)(2,1)S(1)}, bf16[1024,256]{1,0:T(8,128)(2,1)S(1)}, u32[]{:S(2)}, u32[]{:S(2)}) collective-permute-start(bf16[1024,256]{1,0:T(8,128)(2,1)S(1)} %slice_bitcast_fusion.1.refs_0_), channel_id=1, source_target_pairs={{0,1},{1,0},{2,3},{3,2},{4,5},{5,4},{6,7},{7,6},{8,9},{9,8},{10,11... | collective-permute-start | bytes 1572872 | tf_op jit(solution)/shard_map/ppermute | solution.py:288
  7.7 24.3 %collective-permute-start.1 = (bf16[1024,256]{1,0:T(8,128)(2,1)S(1)}, bf16[1024,256]{1,0:T(8,128)(2,1)S(1)}, u32[]{:S(2)}, u32[]{:S(2)}) collective-permute-start(bf16[1024,256]{1,0:T(8,128)(2,1)S(1)} %collective-permute-done.refs_2_), channel_id=1, source_target_pairs={{1,0},{2,3},{5,4},{6,7},{9,8},{10,11},{13,12},{14,15},{17,16},{18,... | collective-permute-start | bytes 1572872 | tf_op jit(solution)/shard_map/ppermute | solution.py:288
  19.3 12.7 %collective-permute-start.3 = (bf16[1024,256]{1,0:T(8,128)(2,1)S(1)}, bf16[1024,256]{1,0:T(8,128)(2,1)S(1)}, u32[]{:S(2)}, u32[]{:S(2)}) collective-permute-start(bf16[1024,256]{1,0:T(8,128)(2,1)S(1)} %collective-permute-done.2.refs_1_), channel_id=1, source_target_pairs={{1,2},{2,1},{5,6},{6,5},{9,10},{10,9},{13,14},{14,13},{17,18},{18,... | collective-permute-start | bytes 1572872 | tf_op jit(solution)/shard_map/ppermute | solution.py:288
  21.2 47.6 %copy-start = (bf16[2,1024,1024]{2,1,0:T(8,128)(2,1)S(1)}, bf16[2,1024,1024]{2,1,0:T(8,128)(2,1)}, u32[]{:S(2)}) copy-start(bf16[2,1024,1024]{2,1,0:T(8,128)(2,1)} %factors_ref.7) | copy-start | bytes 12582916
  33.3 3.2 %collective-permute-start.4 = (bf16[128,768]{1,0:T(8,128)(2,1)S(1)}, bf16[128,768]{1,0:T(8,128)(2,1)S(1)}, u32[]{:S(2)}, u32[]{:S(2)}) collective-permute-start(bf16[128,768]{1,0:T(8,128)(2,1)S(1)} %get-tuple-element.40), channel_id=1, source_target_pairs={{0,4},{4,0},{8,12},{12,8},{16,20},{20,16},{24,28},{28,24},{1,5},{5... | collective-permute-start | bytes 589832 | tf_op jit(solution)/shard_map/ppermute | solution.py:29
  34.5 17.7 %collective-permute-start.6 = (bf16[1024,256]{1,0:T(8,128)(2,1)S(1)}, bf16[1024,256]{1,0:T(8,128)(2,1)S(1)}, u32[]{:S(2)}, u32[]{:S(2)}) collective-permute-start(bf16[1024,256]{1,0:T(8,128)(2,1)S(1)} %collective-permute-done.3.refs_4_.refs_0_), channel_id=1, source_target_pairs={{1,0},{2,3},{5,4},{6,7},{9,8},{10,11},{13,12},{14,15},{17,16},{18,... | collective-permute-start | bytes 1572872 | tf_op jit(solution)/shard_map/ppermute | solution.py:288
  35.8 16.4 %collective-permute-start.7 = (bf16[1024,256]{1,0:T(8,128)(2,1)S(1)}, bf16[1024,256]{1,0:T(8,128)(2,1)S(1)}, u32[]{:S(2)}, u32[]{:S(2)}) collective-permute-start(bf16[1024,256]{1,0:T(8,128)(2,1)S(1)} %slice_bitcast_fusion.refs_0_), channel_id=1, source_target_pairs={{1,2},{2,1},{5,6},{6,5},{9,10},{10,9},{13,14},{14,13},{17,18},{18,... | collective-permute-start | bytes 1572872 | tf_op jit(solution)/shard_map/ppermute | solution.py:288
  36.6 8.7 %collective-permute-start.9 = (bf16[128,768]{1,0:T(8,128)(2,1)S(1)}, bf16[128,768]{1,0:T(8,128)(2,1)S(1)}, u32[]{:S(2)}, u32[]{:S(2)}) collective-permute-start(bf16[128,768]{1,0:T(8,128)(2,1)S(1)} %add_convert_fusion.3), channel_id=1, source_target_pairs={{0,24},{4,28},{8,16},{12,20},{16,8},{20,12},{24,0},{28,4},{1,25},{... | collective-permute-start | bytes 589832 | tf_op jit(solution)/shard_map/ppermute | solution.py:29
  39.1 13.2 %collective-permute-start.8 = (bf16[128,768]{1,0:T(8,128)(2,1)S(1)}, bf16[128,768]{1,0:T(8,128)(2,1)S(1)}, u32[]{:S(2)}, u32[]{:S(2)}) collective-permute-start(bf16[128,768]{1,0:T(8,128)(2,1)S(1)} %add_convert_fusion.3), channel_id=1, source_target_pairs={{0,16},{4,20},{8,24},{12,28},{16,0},{20,4},{24,8},{28,12},{1,17},{... | collective-permute-start | bytes 589832 | tf_op jit(solution)/shard_map/ppermute | solution.py:29
  39.6 12.7 %collective-permute-start.5 = (bf16[128,768]{1,0:T(8,128)(2,1)S(1)}, bf16[128,768]{1,0:T(8,128)(2,1)S(1)}, u32[]{:S(2)}, u32[]{:S(2)}) collective-permute-start(bf16[128,768]{1,0:T(8,128)(2,1)S(1)} %add_convert_fusion.3), channel_id=1, source_target_pairs={{0,8},{4,12},{8,0},{12,4},{16,24},{20,28},{24,16},{28,20},{1,9},{5... | collective-permute-start | bytes 589832 | tf_op jit(solution)/shard_map/ppermute | solution.py:29
  45.3 18.0 %collective-permute-start.16 = (bf16[1024,256]{1,0:T(8,128)(2,1)S(1)}, bf16[1024,256]{1,0:T(8,128)(2,1)S(1)}, u32[]{:S(2)}, u32[]{:S(2)}) collective-permute-start(bf16[1024,256]{1,0:T(8,128)(2,1)S(1)} %slice_bitcast_fusion.refs_0_), channel_id=1, source_target_pairs={{0,1},{1,0},{2,3},{3,2},{4,5},{5,4},{6,7},{7,6},{8,9},{9,8},{10,11... | collective-permute-start | bytes 1572872 | tf_op jit(solution)/shard_map/ppermute | solution.py:288
  52.4 1.5 %collective-permute-start.10 = (bf16[128,768]{1,0:T(8,128)(2,1)S(1)}, bf16[128,768]{1,0:T(8,128)(2,1)S(1)}, u32[]{:S(2)}, u32[]{:S(2)}) collective-permute-start(bf16[128,768]{1,0:T(8,128)(2,1)S(1)} %add_convert_fusion.2.refs_0_), channel_id=1, source_target_pairs={{0,4},{4,0},{8,12},{12,8},{16,20},{20,16},{24,28},{28,24},{1,5},{5... | collective-permute-start | bytes 589832 | tf_op jit(solution)/shard_map/ppermute | solution.py:29
  54.3 11.0 %collective-permute-start.11 = (bf16[128,256]{1,0:T(8,128)(2,1)S(1)}, bf16[128,256]{1,0:T(8,128)(2,1)S(1)}, u32[]{:S(2)}, u32[]{:S(2)}) collective-permute-start(bf16[128,256]{1,0:T(8,128)(2,1)S(1)} %get-tuple-element.51), channel_id=1, source_target_pairs={{0,4},{4,0},{8,12},{12,8},{16,20},{20,16},{24,28},{28,24},{1,5},{5... | collective-permute-start | bytes 196616 | tf_op jit(solution)/shard_map/ppermute | solution.py:29
  63.3 12.0 %collective-permute-start.17 = (bf16[1024,256]{1,0:T(8,128)(2,1)S(1)}, bf16[1024,256]{1,0:T(8,128)(2,1)S(1)}, u32[]{:S(2)}, u32[]{:S(2)}) collective-permute-start(bf16[1024,256]{1,0:T(8,128)(2,1)S(1)} %collective-permute-done.16.refs_1_), channel_id=1, source_target_pairs={{1,2},{2,1},{5,6},{6,5},{9,10},{10,9},{13,14},{14,13},{17,18},{18,... | collective-permute-start | bytes 1572872 | tf_op jit(solution)/shard_map/ppermute | solution.py:288
  64.0 15.3 %collective-permute-start.18 = (bf16[1024,256]{1,0:T(8,128)(2,1)S(1)}, bf16[1024,256]{1,0:T(8,128)(2,1)S(1)}, u32[]{:S(2)}, u32[]{:S(2)}) collective-permute-start(bf16[1024,256]{1,0:T(8,128)(2,1)S(1)} %collective-permute-done.7.refs_2_), channel_id=1, source_target_pairs={{1,0},{2,3},{5,4},{6,7},{9,8},{10,11},{13,12},{14,15},{17,16},{18,... | collective-permute-start | bytes 1572872 | tf_op jit(solution)/shard_map/ppermute | solution.py:288
  65.3 5.7 %collective-permute-start.14 = (bf16[128,256]{1,0:T(8,128)(2,1)S(1)}, bf16[128,256]{1,0:T(8,128)(2,1)S(1)}, u32[]{:S(2)}, u32[]{:S(2)}) collective-permute-start(bf16[128,256]{1,0:T(8,128)(2,1)S(1)} %add_convert_fusion.7), channel_id=1, source_target_pairs={{0,24},{4,28},{8,16},{12,20},{16,8},{20,12},{24,0},{28,4},{1,25},{... | collective-permute-start | bytes 196616 | tf_op jit(solution)/shard_map/ppermute | solution.py:29
  67.8 4.3 %collective-permute-start.13 = (bf16[128,256]{1,0:T(8,128)(2,1)S(1)}, bf16[128,256]{1,0:T(8,128)(2,1)S(1)}, u32[]{:S(2)}, u32[]{:S(2)}) collective-permute-start(bf16[128,256]{1,0:T(8,128)(2,1)S(1)} %add_convert_fusion.7), channel_id=1, source_target_pairs={{0,16},{4,20},{8,24},{12,28},{16,0},{20,4},{24,8},{28,12},{1,17},{... | collective-permute-start | bytes 196616 | tf_op jit(solution)/shard_map/ppermute | solution.py:29
  68.3 4.3 %collective-permute-start.12 = (bf16[128,256]{1,0:T(8,128)(2,1)S(1)}, bf16[128,256]{1,0:T(8,128)(2,1)S(1)}, u32[]{:S(2)}, u32[]{:S(2)}) collective-permute-start(bf16[128,256]{1,0:T(8,128)(2,1)S(1)} %add_convert_fusion.7), channel_id=1, source_target_pairs={{0,8},{4,12},{8,0},{12,4},{16,24},{20,28},{24,16},{28,20},{1,9},{5... | collective-permute-start | bytes 196616 | tf_op jit(solution)/shard_map/ppermute | solution.py:29
  72.6 2.0 %collective-permute-start.15 = (bf16[128,256]{1,0:T(8,128)(2,1)S(1)}, bf16[128,256]{1,0:T(8,128)(2,1)S(1)}, u32[]{:S(2)}, u32[]{:S(2)}) collective-permute-start(bf16[128,256]{1,0:T(8,128)(2,1)S(1)} %add_convert_fusion.6.own_ref), channel_id=1, source_target_pairs={{0,4},{4,0},{8,12},{12,8},{16,20},{20,16},{24,28},{28,24},{1,5},{5... | collective-permute-start | bytes 196616 | tf_op jit(solution)/shard_map/ppermute | solution.py:29
  80.7 1.5 %collective-permute-start.19 = (bf16[128,768]{1,0:T(8,128)(2,1)S(1)}, bf16[128,768]{1,0:T(8,128)(2,1)S(1)}, u32[]{:S(2)}, u32[]{:S(2)}) collective-permute-start(bf16[128,768]{1,0:T(8,128)(2,1)S(1)} %get-tuple-element.56), channel_id=1, source_target_pairs={{0,4},{4,0},{8,12},{12,8},{16,20},{20,16},{24,28},{28,24},{1,5},{5... | collective-permute-start | bytes 589832 | tf_op jit(solution)/shard_map/ppermute | solution.py:29
  80.7 16.2 %collective-permute-start.21 = (bf16[1024,256]{1,0:T(8,128)(2,1)S(1)}, bf16[1024,256]{1,0:T(8,128)(2,1)S(1)}, u32[]{:S(2)}, u32[]{:S(2)}) collective-permute-start(bf16[1024,256]{1,0:T(8,128)(2,1)S(1)} %collective-permute-done.17.refs_4_.refs_0_), channel_id=1, source_target_pairs={{1,0},{2,3},{5,4},{6,7},{9,8},{10,11},{13,12},{14,15},{17,16},{18,... | collective-permute-start | bytes 1572872 | tf_op jit(solution)/shard_map/ppermute | solution.py:288
  82.2 15.2 %collective-permute-start.23 = (bf16[128,768]{1,0:T(8,128)(2,1)S(1)}, bf16[128,768]{1,0:T(8,128)(2,1)S(1)}, u32[]{:S(2)}, u32[]{:S(2)}) collective-permute-start(bf16[128,768]{1,0:T(8,128)(2,1)S(1)} %add_convert_fusion.1), channel_id=1, source_target_pairs={{0,24},{4,28},{8,16},{12,20},{16,8},{20,12},{24,0},{28,4},{1,25},{... | collective-permute-start | bytes 589832 | tf_op jit(solution)/shard_map/ppermute | solution.py:29
  84.7 12.7 %collective-permute-start.22 = (bf16[128,768]{1,0:T(8,128)(2,1)S(1)}, bf16[128,768]{1,0:T(8,128)(2,1)S(1)}, u32[]{:S(2)}, u32[]{:S(2)}) collective-permute-start(bf16[128,768]{1,0:T(8,128)(2,1)S(1)} %add_convert_fusion.1), channel_id=1, source_target_pairs={{0,16},{4,20},{8,24},{12,28},{16,0},{20,4},{24,8},{28,12},{1,17},{... | collective-permute-start | bytes 589832 | tf_op jit(solution)/shard_map/ppermute | solution.py:29
  85.3 12.2 %collective-permute-start.20 = (bf16[128,768]{1,0:T(8,128)(2,1)S(1)}, bf16[128,768]{1,0:T(8,128)(2,1)S(1)}, u32[]{:S(2)}, u32[]{:S(2)}) collective-permute-start(bf16[128,768]{1,0:T(8,128)(2,1)S(1)} %add_convert_fusion.1), channel_id=1, source_target_pairs={{0,8},{4,12},{8,0},{12,4},{16,24},{20,28},{24,16},{28,20},{1,9},{5... | collective-permute-start | bytes 589832 | tf_op jit(solution)/shard_map/ppermute | solution.py:29
  97.4 1.3 %collective-permute-start.25 = (bf16[128,256]{1,0:T(8,128)(2,1)S(1)}, bf16[128,256]{1,0:T(8,128)(2,1)S(1)}, u32[]{:S(2)}, u32[]{:S(2)}) collective-permute-start(bf16[128,256]{1,0:T(8,128)(2,1)S(1)} %get-tuple-element.64), channel_id=1, source_target_pairs={{0,4},{4,0},{8,12},{12,8},{16,20},{20,16},{24,28},{28,24},{1,5},{5... | collective-permute-start | bytes 196616 | tf_op jit(solution)/shard_map/ppermute | solution.py:29
  98.7 5.3 %collective-permute-start.28 = (bf16[128,256]{1,0:T(8,128)(2,1)S(1)}, bf16[128,256]{1,0:T(8,128)(2,1)S(1)}, u32[]{:S(2)}, u32[]{:S(2)}) collective-permute-start(bf16[128,256]{1,0:T(8,128)(2,1)S(1)} %add_convert_fusion.5), channel_id=1, source_target_pairs={{0,24},{4,28},{8,16},{12,20},{16,8},{20,12},{24,0},{28,4},{1,25},{... | collective-permute-start | bytes 196616 | tf_op jit(solution)/shard_map/ppermute | solution.py:29
  101.2 4.3 %collective-permute-start.27 = (bf16[128,256]{1,0:T(8,128)(2,1)S(1)}, bf16[128,256]{1,0:T(8,128)(2,1)S(1)}, u32[]{:S(2)}, u32[]{:S(2)}) collective-permute-start(bf16[128,256]{1,0:T(8,128)(2,1)S(1)} %add_convert_fusion.5), channel_id=1, source_target_pairs={{0,16},{4,20},{8,24},{12,28},{16,0},{20,4},{24,8},{28,12},{1,17},{... | collective-permute-start | bytes 196616 | tf_op jit(solution)/shard_map/ppermute | solution.py:29
  101.7 4.3 %collective-permute-start.26 = (bf16[128,256]{1,0:T(8,128)(2,1)S(1)}, bf16[128,256]{1,0:T(8,128)(2,1)S(1)}, u32[]{:S(2)}, u32[]{:S(2)}) collective-permute-start(bf16[128,256]{1,0:T(8,128)(2,1)S(1)} %add_convert_fusion.5), channel_id=1, source_target_pairs={{0,8},{4,12},{8,0},{12,4},{16,24},{20,28},{24,16},{28,20},{1,9},{5... | collective-permute-start | bytes 196616 | tf_op jit(solution)/shard_map/ppermute | solution.py:29
  102.4 3.7 %collective-permute-start.24 = (bf16[128,768]{1,0:T(8,128)(2,1)S(1)}, bf16[128,768]{1,0:T(8,128)(2,1)S(1)}, u32[]{:S(2)}, u32[]{:S(2)}) collective-permute-start(bf16[128,768]{1,0:T(8,128)(2,1)S(1)} %add_convert_fusion.refs_0_), channel_id=1, source_target_pairs={{0,4},{4,0},{8,12},{12,8},{16,20},{20,16},{24,28},{28,24},{1,5},{5... | collective-permute-start | bytes 589832 | tf_op jit(solution)/shard_map/ppermute | solution.py:29
  106.0 3.6 %collective-permute-start.29 = (bf16[128,256]{1,0:T(8,128)(2,1)S(1)}, bf16[128,256]{1,0:T(8,128)(2,1)S(1)}, u32[]{:S(2)}, u32[]{:S(2)}) collective-permute-start(bf16[128,256]{1,0:T(8,128)(2,1)S(1)} %add_convert_fusion.4.own_ref), channel_id=1, source_target_pairs={{0,4},{4,0},{8,12},{12,8},{16,20},{20,16},{24,28},{28,24},{1,5},{5... | collective-permute-start | bytes 196616 | tf_op jit(solution)/shard_map/ppermute | solution.py:29

commit v4 on v3

--- a/solution.py
+++ b/solution.py
@@ -30,16 +30,18 @@
 
 
 class Part:
-    def __init__(self, arrays, blocks, here=None):
+    def __init__(self, p, arrays, blocks, here=None):
         self.arrays, self.blocks, self.here = arrays, blocks, here
-        self.rows, self.width = [x.shape[0] for x in arrays], arrays[0].shape[1]
+        self.leads = [p if x.ndim == 3 else None for x in arrays]
+        self.rows, self.width = [x.shape[-2] for x in arrays], arrays[0].shape[-1]
 
 
 def start_parts(parts, refs, panels, sems):
     waits, at, column = [], 0, 0
     for k, part in enumerate(parts):
         columns = pl.ds(column, part.width)
-        whole = pltpu.make_async_copy(refs[at], panels.at[:, columns], sems.at[k])
+        own = [ref if p is None else ref.at[p] for ref, p in zip(refs[at : at + len(part.rows)], part.leads)]
+        whole = pltpu.make_async_copy(own[0], panels.at[:, columns], sems.at[k])
         if part.here is None:
             whole.start()
         else:
@@ -48,7 +50,7 @@
             row = 0
             for i, rows in enumerate(part.rows[1:]):
                 place = panels.at[pl.ds(row, rows), columns]
-                piece = pltpu.make_async_copy(refs[at + 1 + i], place, sems.at[k])
+                piece = pltpu.make_async_copy(own[1 + i], place, sems.at[k])
                 pl.when(jnp.logical_not(here))(piece.start)
                 row += rows
         waits.append(whole.wait)
@@ -241,24 +243,20 @@
     )(current, *arrays)
 
 
-GROUPS = {1: ((0, 1, 2), (3,)), 0: ((0, 1, 2), (3,))}
-PIECES = {"O": 1, "F3": 1}
-JOINED = "swap"
+GROUPS = {1: ((0, 1), (2, 3)), 0: ((0, 1, 2), (3,))}
+PIECES = {'O': 1, 'F3': 1}
+JOINED = 'swap'
+WHOLE = ()
+DIRECT = ('0.0', '0.1', '0.2', '1.0', '1.1', '1.2')
+SKIP = ('E3',)
 GATES = {
-    "P0": ("p1",),
-    "X": ("p1",),
-    "E2": ("M1",),
-    "M2": ("M1",),
-    "E3": ("E2",),
-    "N1": ("E2", "M2"),
-    "c1.0": ("E3", "N1"),
-    "a1.0": ("E2", "M2"),
-    "a1.1": ("d1.0", "N1"),
-    "N2": ("d1.0", "E3"),
-    "F2": ("d1.0", "E3"),
-    "F3": ("F2",),
-    "a0.0": ("N2", "F2"),
-    "c0.0": ("F3",),
+    'X': ('p1',),
+    'd1.0': ('I',),
+    'a1.1': ('E3',),
+    'c1.1': ('N2', 'F2', 'Y1'),
+    'c0.1': ('Y0', 'F2'),
+    'U1': ('N2',),
+    'd0.1': ('N1',),
 }
 
 
@@ -303,34 +301,32 @@
             return self.gated(name, self.reflectors)[0]
         if name == "X":
             return self.gated(name, self.eigvecs).T
-        if name == "E1":
-            return self.send(name, self("p1"), outer)
-        if name == "M1":
-            return self.send(name, self("p1"), middle)
-        if name == "E2":
-            if JOINED == "E2":
-                return self.send(name, jnp.where(at_end, self("P0"), self("M1")), outer)
-            return self.send(name, self("M1"), outward)
-        if name == "M2":
-            return self.send(name, self("E1"), middle)
-        if name == "E3":
-            return self.send(name, self("M2"), outward)
-        if name == "E3s":
-            return self.send(name, self("E1"), skip)
+        if name in WHOLE:
+            source = self.reflectors if name[1] == "1" else self({"E2": "M1", "M2": "E1"}[name])
+            return self.send(name, source, middle if name[0] == "M" else outer if name == "E1" else outward)
+        if name in ("E1", "M1", "E2", "M2", "E3"):
+            if name in SKIP:
+                return self.send(name, self.panel(1, "E1"), skip)
+            source = {"E1": "p1", "M1": "p1", "E2": "M1", "M2": "E1", "E3": "M2"}[name]
+            if name == "E2" and JOINED == "E2":
+                return self.send(name, jnp.where(at_end, self("P0"), self.panel(1, "M1")), outer)
+            return self.send(name, self.panel(1, source), {"E1": outer, "M1": middle, "M2": middle}.get(name, outward))
+        twin = {"I": "E1", "N1": "M1", "F2": "E2", "N2": "M2"}.get(name)
+        if twin in WHOLE:
+            return self(twin)
         if name == "I":
             if JOINED == "E2":
                 return self("E2")
             return self.send(name, self("P0"), outer if JOINED == "swap" else inward)
         if name == "O":
             return self.pieces(name, self("P0"), outward)
-        if name == "N1":
-            return self.send(name, self("P0"), middle)
-        if name == "N2":
-            return self.send(name, self("I"), middle)
-        if name == "F2":
-            return self.send(name, self("N1"), outward)
+        if name in ("N1", "N2", "F2"):
+            source = {"N1": "P0", "N2": "I", "F2": "N1"}[name]
+            return self.send(name, self.panel(0, source), outward if name == "F2" else middle)
         if name == "F3":
-            return self.pieces(name, self("N2"), outward)
+            if name in SKIP:
+                return self.pieces(name, self.panel(0, "I"), skip)
+            return self.pieces(name, self.panel(0, "N2"), outward)
         step, p = name[0], int(name[1])
         groups = [[self.part(p, g) for g in group] for group in GROUPS[p]]
         late = len(groups) - 1
@@ -354,11 +350,24 @@
         if step == "c":
             mine, bit = self("b" + name[1:]), 2
             while bit < self.m:
-                got = [swap(mine, s * bit, self.m) for s in range(1, 4) if s * bit < self.m]
-                mine = sum([self.gated(name, g).astype(F32) for g in got], mine.astype(F32)).astype(BF16)
+                if name[1:] in DIRECT or 2 * bit >= self.m:
+                    got = [swap(mine, s * bit, self.m) for s in range(1, 4) if s * bit < self.m]
+                    mine = sum([self.gated(name, g).astype(F32) for g in got], mine.astype(F32)).astype(BF16)
+                else:
+                    halves = jnp.split(mine, 2)
+                    for bits in ((bit, 2 * bit), (2 * bit, bit)):
+                        got = [swap(x, b, self.m) for x, b in zip(halves, bits)]
+                        if bits[0] > bit:
+                            got = [self.gated(name, g) for g in got]
+                        halves = [(x.astype(F32) + g.astype(F32)).astype(BF16) for x, g in zip(halves, got)]
+                    mine = jnp.concatenate(halves)
                 bit *= 4
             return mine
         return swap(self.gated(name, self("c" + name[1:])), 1, self.m)
+
+    def panel(self, p, name):
+        x = self(name)
+        return x[p] if x.ndim == 3 else x
 
     def part(self, p, g):
         n, wide = self.n, self.reflectors.shape[2]
@@ -375,13 +384,16 @@
         if p == 1:
             arrays = (["p1"], ["E1"], ["M1", "E2"], ["M2", "E3"])[g]
         else:
-            arrays = (["P0"], ["I"] if JOINED == "swap" else ["I", "O"], ["N1", "F2"], ["N2", "F3"])[g]
+            together = JOINED == "swap" or "E1" in WHOLE
+            arrays = (["P0"], ["I"] if together else ["I", "O"], ["N1", "F2"], ["N2", "F3"])[g]
+        if g == 0 and "E1" in WHOLE and "M1" in WHOLE:
+            return Part(p, [self.reflectors], [(lambda z: z * wide, 0, wide)])
         found = []
         for name in arrays:
             got = self(name)
             found += got if isinstance(got, list) else [got]
         blocks = [(lambda z: places[g](z) * wide, 0, wide)]
-        return Part(found, blocks, inner if len(found) > 1 else None)
+        return Part(p, found, blocks, inner if len(found) > 1 else None)
 
 
 def swap_sum(mine, other, m):

time: 112 us -> 99.7 us (0.89)
  waiting for transfers between devices: 58.9 us -> 49.2 us
  starting transfers between devices: 35.3 us -> 33 us
    ppermute x10, waiting for transfers between devices: 45.4 us -> 40.1 us  [send(): return lax.ppermute(self.gated(name, x), 'vecs', pairs)]
    ppermute x10, starting transfers between devices: 20.3 us -> 15.4 us  [send(): return lax.ppermute(self.gated(name, x), 'vecs', pairs)]
    ppermute x20, waiting for transfers between devices: 13.5 us -> 9.04 us  [swap(): return lax.ppermute(x, 'rows', [(i, i ^ bit) for i in range(m)])]
    ppermute x20, starting transfers between devices: 14.9 us -> 17.6 us  [swap(): return lax.ppermute(x, 'rows', [(i, i ^ bit) for i in range(m)])]
  transfers between devices with their start and end apart: 30 -> 30, of which waited for: 16 -> 13; matrix products, arithmetic and copies ran while one was open for 2% -> 2% of each run, Pallas kernels for 8% -> 10%
where the time goes in v4:
time: 99.7 us; the launch traced here: 99.3 us
  waiting for transfers between devices  49.2 us (49%)
  starting transfers between devices  33 us (33%)
  Pallas kernels  13.9 us (14%)
  local copies, waits for them, and re-layouts  2.52 us (3%)
    ppermute x10, waiting for transfers between devices, send(): return lax.ppermute(self.gated(name, x), 'vecs', pairs)  40.1 us
    ppermute x20, starting transfers between devices, swap(): return lax.ppermute(x, 'rows', [(i, i ^ bit) for i in range(m)])  17.6 us
    ppermute x10, starting transfers between devices, send(): return lax.ppermute(self.gated(name, x), 'vecs', pairs)  15.4 us
    pallas_call x6, Pallas kernels, call(): pl.pallas_call(kernel, in_specs=[ANY] * len(inputs), out_specs=[IN_VMEM]...  10.1 us
    ppermute x20, waiting for transfers between devices, swap(): return lax.ppermute(x, 'rows', [(i, i ^ bit) for i in range(m)])  9.04 us
    pallas_call x4, Pallas kernels, coeff(): pl.pallas_call(functools.partial(coeff_kernel, parts), in_specs=[ANY] * (...  3.76 us
  transfers between devices with their start and end apart: 30, of which 13 were waited for; matrix products, arithmetic and copies ran while one was open for 2% of the time, Pallas kernels for 10%

profile of v4, /device:TPU:0, one launch (start us, length us, event | category | flops | bytes accessed | tf_op | source)
XLA Modules:
  0.0 99.3 jit_solution(11376268131434462561)
XLA Ops:
  0.0 1.3 %slice_bitcast_fusion = (bf16[1024,256]{1,0:T(8,128)(2,1)S(1)}, bf16[1024,256]{1,0:T(8,128)(2,1)S(1)}) fusion(bf16[2,1024,256]{2,1,0:T(8,128)(2,1)} %param.4), kind=kLoop, calls=%fused_computation | loop fusion | bytes 2097152 | tf_op jit(solution)/shard_map/squeeze | solution.py:301
  1.3 3.1 %collective-permute-start = (bf16[1024,256]{1,0:T(8,128)(2,1)S(1)}, bf16[1024,256]{1,0:T(8,128)(2,1)S(1)}, u32[]{:S(2)}, u32[]{:S(2)}) collective-permute-start(bf16[1024,256]{1,0:T(8,128)(2,1)S(1)} %get-tuple-element.52.refs_0_), channel_id=1, source_target_pairs={{0,1},{1,0},{2,3},{3,2},{4,5},{5,4},{6,7},{7,6},{8,9},{9,8},{10,11... | collective-permute-start | bytes 1572872 | tf_op jit(solution)/shard_map/ppermute | solution.py:286
  4.4 1.4 %collective-permute-start.7 = (bf16[1024,256]{1,0:T(8,128)(2,1)S(1)}, bf16[1024,256]{1,0:T(8,128)(2,1)}, u32[]{:S(2)}, u32[]{:S(2)}) collective-permute-start(bf16[1024,256]{1,0:T(8,128)(2,1)S(1)} %get-tuple-element.52.refs_0_), channel_id=1, source_target_pairs={{1,2},{2,1},{5,6},{6,5},{9,10},{10,9},{13,14},{14,13},{17,18},{18,... | collective-permute-start | bytes 1572872 | tf_op jit(solution)/shard_map/ppermute | solution.py:286
  5.8 3.7 %collective-permute-start.5 = (bf16[1024,256]{1,0:T(8,128)(2,1)S(1)}, bf16[1024,256]{1,0:T(8,128)(2,1)S(1)}, u32[]{:S(2)}, u32[]{:S(2)}) collective-permute-start(bf16[1024,256]{1,0:T(8,128)(2,1)S(1)} %get-tuple-element.51.refs_0_), channel_id=1, source_target_pairs={{0,1},{1,0},{2,3},{3,2},{4,5},{5,4},{6,7},{7,6},{8,9},{9,8},{10,11... | collective-permute-start | bytes 1572872 | tf_op jit(solution)/shard_map/ppermute | solution.py:286
  9.5 0.7 collective-permute-start.14
  10.2 1.2 %copy.4 = bf16[1024,256]{0,1:T(8,128)(2,1)S(1)} copy(bf16[1024,256]{1,0:T(8,128)(2,1)} %param.3) | data formatting | bytes 1048576 | tf_op jit(solution)/shard_map/optimization_barrier | solution.py:17
  11.4 5.7 %collective-permute-done.refs_1_ = bf16[1024,256]{1,0:T(8,128)(2,1)S(1)} collective-permute-done((bf16[1024,256]{1,0:T(8,128)(2,1)S(1)}, bf16[1024,256]{1,0:T(8,128)(2,1)S(1)}, u32[]{:S(2)}, u32[]{:S(2)}) %collective-permute-start) | collective-permute-done | bytes 524320 | tf_op jit(solution)/shard_map/ppermute | solution.py:286
  17.1 1.0 %shard_map.37 = (bf16[128,512]{1,0:T(8,128)(2,1)S(1)}, bf16[128,512]{1,0:T(8,128)(2,1)S(1)}) custom-call(bf16[256,1024]{1,0:T(8,128)(2,1)S(1)} %bitcast.5, bf16[1024,256]{1,0:T(8,128)(2,1)S(1)} %get-tuple-element.52.refs_0_, bf16[1024,256]{1,0:T(8,128)(2,1)S(1)} %collective-permute-done.refs_1_), custom_call_target="tpu_custom_call" | custom-call | flops 268435456 | bytes 1048576 | tf_op jit(solution)/shard_map/pallas_call | solution.py:231
  18.2 1.3 %collective-permute-start.10 = (bf16[1024,256]{1,0:T(8,128)(2,1)S(1)}, bf16[1024,256]{1,0:T(8,128)(2,1)S(1)}, u32[]{:S(2)}, u32[]{:S(2)}) collective-permute-start(bf16[1024,256]{1,0:T(8,128)(2,1)S(1)} %collective-permute-done.refs_1_), channel_id=1, source_target_pairs={{2,0},{1,3},{6,4},{5,7},{10,8},{9,11},{14,12},{13,15},{18,16},{17,... | collective-permute-start | bytes 1572872 | tf_op jit(solution)/shard_map/ppermute | solution.py:286
  19.5 0.7 collective-permute-start.9
  20.2 1.3 %collective-permute-start.8 = (bf16[1024,256]{1,0:T(8,128)(2,1)}, bf16[1024,256]{1,0:T(8,128)(2,1)S(1)}, u32[]{:S(2)}, u32[]{:S(2)}) collective-permute-start(bf16[1024,256]{1,0:T(8,128)(2,1)} %collective-permute-done.7.refs_2_.refs_0_), channel_id=1, source_target_pairs={{1,0},{2,3},{5,4},{6,7},{9,8},{10,11},{13,12},{14,15},{17,16},{18,... | collective-permute-start | bytes 1572872 | tf_op jit(solution)/shard_map/ppermute | solution.py:286
  21.6 6.0 %collective-permute-done.5.refs_1_ = bf16[1024,256]{1,0:T(8,128)(2,1)S(1)} collective-permute-done((bf16[1024,256]{1,0:T(8,128)(2,1)S(1)}, bf16[1024,256]{1,0:T(8,128)(2,1)S(1)}, u32[]{:S(2)}, u32[]{:S(2)}) %collective-permute-start.5) | collective-permute-done | bytes 524320 | tf_op jit(solution)/shard_map/ppermute | solution.py:286
  27.5 1.7 %collective-permute-start.2 = (bf16[128,512]{1,0:T(8,128)(2,1)S(1)}, bf16[128,512]{1,0:T(8,128)(2,1)S(1)}, u32[]{:S(2)}, u32[]{:S(2)}) collective-permute-start(bf16[128,512]{1,0:T(8,128)(2,1)S(1)} %add_convert_fusion.5), channel_id=1, source_target_pairs={{0,8},{4,12},{8,0},{12,4},{16,24},{20,28},{24,16},{28,20},{1,9},{5... | collective-permute-start | bytes 393224 | tf_op jit(solution)/shard_map/ppermute | solution.py:29
  29.2 1.5 %collective-permute-start.3 = (bf16[128,512]{1,0:T(8,128)(2,1)S(1)}, bf16[128,512]{1,0:T(8,128)(2,1)S(1)}, u32[]{:S(2)}, u32[]{:S(2)}) collective-permute-start(bf16[128,512]{1,0:T(8,128)(2,1)S(1)} %add_convert_fusion.5), channel_id=1, source_target_pairs={{0,16},{4,20},{8,24},{12,28},{16,0},{20,4},{24,8},{28,12},{1,17},{... | collective-permute-start | bytes 393224 | tf_op jit(solution)/shard_map/ppermute | solution.py:29
  30.7 1.8 %collective-permute-done.2 = bf16[128,512]{1,0:T(8,128)(2,1)S(1)} collective-permute-done((bf16[128,512]{1,0:T(8,128)(2,1)S(1)}, bf16[128,512]{1,0:T(8,128)(2,1)S(1)}, u32[]{:S(2)}, u32[]{:S(2)}) %collective-permute-start.2) | collective-permute-done | bytes 131104 | tf_op jit(solution)/shard_map/ppermute | solution.py:29
  32.5 2.6 %collective-permute-start.4 = (bf16[128,512]{1,0:T(8,128)(2,1)S(1)}, bf16[128,512]{1,0:T(8,128)(2,1)S(1)}, u32[]{:S(2)}, u32[]{:S(2)}) collective-permute-start(bf16[128,512]{1,0:T(8,128)(2,1)S(1)} %add_convert_fusion.5), channel_id=1, source_target_pairs={{0,24},{4,28},{8,16},{12,20},{16,8},{20,12},{24,0},{28,4},{1,25},{... | collective-permute-start | bytes 393224 | tf_op jit(solution)/shard_map/ppermute | solution.py:29
  35.1 1.3 %collective-permute-start.15 = (bf16[1024,256]{1,0:T(8,128)(2,1)S(1)}, bf16[1024,256]{1,0:T(8,128)(2,1)S(1)}, u32[]{:S(2)}, u32[]{:S(2)}) collective-permute-start(bf16[1024,256]{1,0:T(8,128)(2,1)S(1)} %collective-permute-done.14.refs_2_), channel_id=1, source_target_pairs={{1,0},{2,3},{5,4},{6,7},{9,8},{10,11},{13,12},{14,15},{17,16},{18,... | collective-permute-start | bytes 1572872 | tf_op jit(solution)/shard_map/ppermute | solution.py:286
  36.4 2.0 %collective-permute-done.4 = bf16[128,512]{1,0:T(8,128)(2,1)S(1)} collective-permute-done((bf16[128,512]{1,0:T(8,128)(2,1)S(1)}, bf16[128,512]{1,0:T(8,128)(2,1)S(1)}, u32[]{:S(2)}, u32[]{:S(2)}) %collective-permute-start.4) | collective-permute-done | bytes 131104 | tf_op jit(solution)/shard_map/ppermute | solution.py:29
  38.4 0.7 collective-permute-start.11
  39.1 5.0 %collective-permute-done.10.refs_5_.refs_3_ = bf16[1024,256]{1,0:T(8,128)(2,1)S(1)} collective-permute-done((bf16[1024,256]{1,0:T(8,128)(2,1)S(1)}, bf16[1024,256]{1,0:T(8,128)(2,1)S(1)}, u32[]{:S(2)}, u32[]{:S(2)}) %collective-permute-start.10) | collective-permute-done | bytes 524320 | tf_op jit(solution)/shard_map/ppermute | solution.py:286
  44.2 8.0 %collective-permute-done.8.refs_3_.refs_1_ = bf16[1024,256]{1,0:T(8,128)(2,1)S(1)} collective-permute-done((bf16[1024,256]{1,0:T(8,128)(2,1)}, bf16[1024,256]{1,0:T(8,128)(2,1)S(1)}, u32[]{:S(2)}, u32[]{:S(2)}) %collective-permute-start.8) | collective-permute-done | bytes 524320 | tf_op jit(solution)/shard_map/ppermute | solution.py:286
  52.2 1.0 %shard_map.40 = (bf16[128,512]{1,0:T(8,128)(2,1)S(1)}, bf16[128,512]{1,0:T(8,128)(2,1)S(1)}) custom-call(bf16[256,1024]{1,0:T(8,128)(2,1)S(1)} %bitcast.6, bf16[1024,256]{1,0:T(8,128)(2,1)} %collective-permute-done.7.refs_2_.refs_0_, bf16[1024,256]{1,0:T(8,128)(2,1)S(1)} %collective-permute-done.8.refs_3_.refs_1_, ...), custom_call_target="tpu_custom_call" | custom-call | flops 268435456 | bytes 1048576 | tf_op jit(solution)/shard_map/pallas_call | solution.py:231
  53.3 1.6 %shard_map.38.scaled_ref = bf16[1024,256]{1,0:T(8,128)(2,1)S(1)} custom-call(bf16[2,1024,1024]{2,1,0:T(8,128)(2,1)S(1)} %copy-done, bf16[128,512]{1,0:T(8,128)(2,1)S(1)} %add_convert_fusion.4.refs_0_, bf16[128,512]{1,0:T(8,128)(2,1)S(1)} %collective-permute-done.6.refs_1_), custom_call_target="tpu_custom_call" | custom-call | flops 268435456 | bytes 4456448 | tf_op jit(solution)/shard_map/pallas_call | solution.py:167
  55.0 1.6 %collective-permute-start.13 = (bf16[128,512]{1,0:T(8,128)(2,1)S(1)}, bf16[128,512]{1,0:T(8,128)(2,1)S(1)}, u32[]{:S(2)}, u32[]{:S(2)}) collective-permute-start(bf16[128,512]{1,0:T(8,128)(2,1)S(1)} %add_convert_fusion.3), channel_id=1, source_target_pairs={{0,8},{4,12},{8,0},{12,4},{16,24},{20,28},{24,16},{28,20},{1,9},{5... | collective-permute-start | bytes 393224 | tf_op jit(solution)/shard_map/ppermute | solution.py:29
  56.5 1.5 %collective-permute-start.16 = (bf16[128,512]{1,0:T(8,128)(2,1)S(1)}, bf16[128,512]{1,0:T(8,128)(2,1)S(1)}, u32[]{:S(2)}, u32[]{:S(2)}) collective-permute-start(bf16[128,512]{1,0:T(8,128)(2,1)S(1)} %add_convert_fusion.3), channel_id=1, source_target_pairs={{0,16},{4,20},{8,24},{12,28},{16,0},{20,4},{24,8},{28,12},{1,17},{... | collective-permute-start | bytes 393224 | tf_op jit(solution)/shard_map/ppermute | solution.py:29
  58.0 0.5 collective-permute-start.17
  58.5 2.5 %shard_map.39 = (f32[256,1024]{1,0:T(8,128)S(1)}, bf16[1024,512]{1,0:T(8,128)(2,1)S(1)}) custom-call(bf16[2,1024,1024]{2,1,0:T(8,128)(2,1)S(1)} %copy-done, bf16[256,1024]{1,0:T(8,128)(2,1)S(1)} %bitcast.7, bf16[1024,256]{1,0:T(8,128)(2,1)S(1)} %shard_map.38.scaled_ref, bf16[1024,256]{1,0:T(8,128)(2,1)S(1)} %get-tuple-element.52.refs_0_, ...), custom_call_target="tpu_custom_call" | custom-call | flops 1610612736 | bytes 8388608 | tf_op jit(solution)/shard_map/pallas_call | solution.py:167
  61.0 1.9 %collective-permute-done.15.refs_3_ = bf16[1024,256]{1,0:T(8,128)(2,1)S(1)} collective-permute-done((bf16[1024,256]{1,0:T(8,128)(2,1)S(1)}, bf16[1024,256]{1,0:T(8,128)(2,1)S(1)}, u32[]{:S(2)}, u32[]{:S(2)}) %collective-permute-start.15) | collective-permute-done | bytes 524320 | tf_op jit(solution)/shard_map/ppermute | solution.py:286
  63.0 1.9 %collective-permute-done.16 = bf16[128,512]{1,0:T(8,128)(2,1)S(1)} collective-permute-done((bf16[128,512]{1,0:T(8,128)(2,1)S(1)}, bf16[128,512]{1,0:T(8,128)(2,1)S(1)}, u32[]{:S(2)}, u32[]{:S(2)}) %collective-permute-start.16) | collective-permute-done | bytes 131104 | tf_op jit(solution)/shard_map/ppermute | solution.py:29
  65.1 1.3 %collective-permute-done.18.other_ref = bf16[128,512]{1,0:T(8,128)(2,1)S(1)} collective-permute-done((bf16[128,512]{1,0:T(8,128)(2,1)S(1)}, bf16[128,512]{1,0:T(8,128)(2,1)S(1)}, u32[]{:S(2)}, u32[]{:S(2)}) %collective-permute-start.18) | collective-permute-done | bytes 131104 | tf_op jit(solution)/shard_map/ppermute | solution.py:29
  66.4 1.0 %shard_map.41.current_ref = bf16[256,1024]{1,0:T(8,128)(2,1)S(1)} custom-call(f32[256,1024]{1,0:T(8,128)S(1)} %get-tuple-element.33.rest_ref, bf16[1024,512]{1,0:T(8,128)(2,1)S(1)} %get-tuple-element.34.across_ref, bf16[128,512]{1,0:T(8,128)(2,1)S(1)} %add_convert_fusion.2.own_ref, bf16[128,512]{1,0:T(8,128)(2,1)S(1)} %collective-permute-done.18.other_ref), custom_call_target="tpu_custom_call" | custom-call | flops 268435456 | bytes 2359296 | tf_op jit(solution)/shard_map/pallas_call | solution.py:167
  67.4 1.4 %shard_map.42 = (bf16[128,768]{1,0:T(8,128)(2,1)S(1)}, bf16[128,768]{1,0:T(8,128)(2,1)S(1)}) custom-call(bf16[256,1024]{1,0:T(8,128)(2,1)S(1)} %shard_map.41.current_ref, bf16[1024,256]{1,0:T(8,128)(2,1)S(1)} %get-tuple-element.51.refs_0_, bf16[1024,256]{1,0:T(8,128)(2,1)S(1)} %collective-permute-done.5.refs_1_, ...), custom_call_target="tpu_custom_call" | custom-call | flops 402653184 | bytes 1572864 | tf_op jit(solution)/shard_map/pallas_call | solution.py:231
  68.8 0.2 collective-permute-start.19
  69.0 1.3 %collective-permute-start.24 = (bf16[1024,256]{1,0:T(8,128)(2,1)S(1)}, bf16[1024,256]{1,0:T(8,128)(2,1)S(1)}, u32[]{:S(2)}, u32[]{:S(2)}) collective-permute-start(bf16[1024,256]{1,0:T(8,128)(2,1)S(1)} %collective-permute-done.11.refs_4_.refs_0_), channel_id=1, source_target_pairs={{1,0},{2,3},{5,4},{6,7},{9,8},{10,11},{13,12},{14,15},{17,16},{18,... | collective-permute-start | bytes 1572872 | tf_op jit(solution)/shard_map/ppermute | solution.py:286
  70.4 1.3 %collective-permute-start.20 = (bf16[128,768]{1,0:T(8,128)(2,1)S(1)}, bf16[128,768]{1,0:T(8,128)(2,1)S(1)}, u32[]{:S(2)}, u32[]{:S(2)}) collective-permute-start(bf16[128,768]{1,0:T(8,128)(2,1)S(1)} %add_convert_fusion.1), channel_id=1, source_target_pairs={{0,8},{4,12},{8,0},{12,4},{16,24},{20,28},{24,16},{28,20},{1,9},{5... | collective-permute-start | bytes 589832 | tf_op jit(solution)/shard_map/ppermute | solution.py:29
  71.7 0.8 collective-permute-start.21
  72.5 1.4 %collective-permute-start.22 = (bf16[128,768]{1,0:T(8,128)(2,1)S(1)}, bf16[128,768]{1,0:T(8,128)(2,1)S(1)}, u32[]{:S(2)}, u32[]{:S(2)}) collective-permute-start(bf16[128,768]{1,0:T(8,128)(2,1)S(1)} %add_convert_fusion.1), channel_id=1, source_target_pairs={{0,24},{4,28},{8,16},{12,20},{16,8},{20,12},{24,0},{28,4},{1,25},{... | collective-permute-start | bytes 589832 | tf_op jit(solution)/shard_map/ppermute | solution.py:29
  73.9 13.5 %collective-permute-done.24.refs_5_.refs_1_ = bf16[1024,256]{1,0:T(8,128)(2,1)S(1)} collective-permute-done((bf16[1024,256]{1,0:T(8,128)(2,1)S(1)}, bf16[1024,256]{1,0:T(8,128)(2,1)S(1)}, u32[]{:S(2)}, u32[]{:S(2)}) %collective-permute-start.24) | collective-permute-done | bytes 524320 | tf_op jit(solution)/shard_map/ppermute | solution.py:286
  87.5 0.4 shard_map.45
  88.1 0.5 collective-permute-start.23
  88.6 0.6 collective-permute-done.25
  89.2 1.3 %collective-permute-start.26 = (bf16[128,256]{1,0:T(8,128)(2,1)S(1)}, bf16[128,256]{1,0:T(8,128)(2,1)S(1)}, u32[]{:S(2)}, u32[]{:S(2)}) collective-permute-start(bf16[128,256]{1,0:T(8,128)(2,1)S(1)} %add_convert_fusion.7), channel_id=1, source_target_pairs={{0,8},{4,12},{8,0},{12,4},{16,24},{20,28},{24,16},{28,20},{1,9},{5... | collective-permute-start | bytes 196616 | tf_op jit(solution)/shard_map/ppermute | solution.py:29
  90.5 0.8 collective-permute-start.27
  91.3 1.4 %collective-permute-start.28 = (bf16[128,256]{1,0:T(8,128)(2,1)S(1)}, bf16[128,256]{1,0:T(8,128)(2,1)S(1)}, u32[]{:S(2)}, u32[]{:S(2)}) collective-permute-start(bf16[128,256]{1,0:T(8,128)(2,1)S(1)} %add_convert_fusion.7), channel_id=1, source_target_pairs={{0,24},{4,28},{8,16},{12,20},{16,8},{20,12},{24,0},{28,4},{1,25},{... | collective-permute-start | bytes 196616 | tf_op jit(solution)/shard_map/ppermute | solution.py:29
  92.8 1.7 %shard_map.43.scaled_ref = bf16[1024,256]{1,0:T(8,128)(2,1)S(1)} custom-call(bf16[2,1024,1024]{2,1,0:T(8,128)(2,1)S(1)} %copy-done, bf16[128,768]{1,0:T(8,128)(2,1)S(1)} %add_convert_fusion.refs_0_, bf16[128,768]{1,0:T(8,128)(2,1)S(1)} %collective-permute-done.23.refs_1_), custom_call_target="tpu_custom_call" | custom-call | flops 268435456 | bytes 4587520 | tf_op jit(solution)/shard_map/pallas_call | solution.py:167
  94.5 1.8 %shard_map.44 = (f32[1024,256]{1,0:T(8,128)S(1)}, bf16[1024,256]{1,0:T(8,128)(2,1)S(1)}) custom-call(bf16[2,1024,1024]{2,1,0:T(8,128)(2,1)S(1)} %copy-done, bf16[256,1024]{1,0:T(8,128)(2,1)S(1)} %shard_map.41.current_ref, bf16[1024,256]{1,0:T(8,128)(2,1)S(1)} %shard_map.43.scaled_ref, bf16[1024,256]{1,0:T(8,128)(2,1)S(1)} %get-tuple-element.51.refs_0_, ...), custom_call_target="tpu_custom_call" | custom-call | flops 1073741824 | bytes 8388608 | tf_op jit(solution)/shard_map/pallas_call | solution.py:167
  96.6 1.2 %collective-permute-done.29.other_ref = bf16[128,256]{1,0:T(8,128)(2,1)S(1)} collective-permute-done((bf16[128,256]{1,0:T(8,128)(2,1)S(1)}, bf16[128,256]{1,0:T(8,128)(2,1)S(1)}, u32[]{:S(2)}, u32[]{:S(2)}) %collective-permute-start.29) | collective-permute-done | bytes 65568 | tf_op jit(solution)/shard_map/ppermute | solution.py:29
  97.9 1.5 %shard_map.46 = bf16[1024,256]{1,0:T(8,128)(2,1)} custom-call(f32[1024,256]{1,0:T(8,128)S(1)} %get-tuple-element.43.rest_ref, bf16[1024,256]{1,0:T(8,128)(2,1)S(1)} %get-tuple-element.44.across_ref, bf16[128,256]{1,0:T(8,128)(2,1)S(1)} %add_convert_fusion.6.own_ref, bf16[128,256]{1,0:T(8,128)(2,1)S(1)} %collective-permute-done.29.other_ref), custom_call_target="tpu_custom_call" | custom-call | flops 134217728 | bytes 1703936 | tf_op jit(solution)/shard_map/pallas_call | solution.py:167
  (34 shorter events, 1.0 us)
Async XLA Ops:
  1.3 15.8 %collective-permute-start = (bf16[1024,256]{1,0:T(8,128)(2,1)S(1)}, bf16[1024,256]{1,0:T(8,128)(2,1)S(1)}, u32[]{:S(2)}, u32[]{:S(2)}) collective-permute-start(bf16[1024,256]{1,0:T(8,128)(2,1)S(1)} %get-tuple-element.52.refs_0_), channel_id=1, source_target_pairs={{0,1},{1,0},{2,3},{3,2},{4,5},{5,4},{6,7},{7,6},{8,9},{9,8},{10,11... | collective-permute-start | bytes 1572872 | tf_op jit(solution)/shard_map/ppermute | solution.py:286
  4.4 15.1 %collective-permute-start.7 = (bf16[1024,256]{1,0:T(8,128)(2,1)S(1)}, bf16[1024,256]{1,0:T(8,128)(2,1)}, u32[]{:S(2)}, u32[]{:S(2)}) collective-permute-start(bf16[1024,256]{1,0:T(8,128)(2,1)S(1)} %get-tuple-element.52.refs_0_), channel_id=1, source_target_pairs={{1,2},{2,1},{5,6},{6,5},{9,10},{10,9},{13,14},{14,13},{17,18},{18,... | collective-permute-start | bytes 1572872 | tf_op jit(solution)/shard_map/ppermute | solution.py:286
  5.8 21.7 %collective-permute-start.5 = (bf16[1024,256]{1,0:T(8,128)(2,1)S(1)}, bf16[1024,256]{1,0:T(8,128)(2,1)S(1)}, u32[]{:S(2)}, u32[]{:S(2)}) collective-permute-start(bf16[1024,256]{1,0:T(8,128)(2,1)S(1)} %get-tuple-element.51.refs_0_), channel_id=1, source_target_pairs={{0,1},{1,0},{2,3},{3,2},{4,5},{5,4},{6,7},{7,6},{8,9},{9,8},{10,11... | collective-permute-start | bytes 1572872 | tf_op jit(solution)/shard_map/ppermute | solution.py:286
  9.5 19.7 %collective-permute-start.14 = (bf16[1024,256]{1,0:T(8,128)(2,1)S(1)}, bf16[1024,256]{1,0:T(8,128)(2,1)S(1)}, u32[]{:S(2)}, u32[]{:S(2)}) collective-permute-start(bf16[1024,256]{1,0:T(8,128)(2,1)S(1)} %get-tuple-element.51.refs_0_), channel_id=1, source_target_pairs={{1,2},{2,1},{5,6},{6,5},{9,10},{10,9},{13,14},{14,13},{17,18},{18,... | collective-permute-start | bytes 1572872 | tf_op jit(solution)/shard_map/ppermute | solution.py:286
  11.4 41.8 %copy-start = (bf16[2,1024,1024]{2,1,0:T(8,128)(2,1)S(1)}, bf16[2,1024,1024]{2,1,0:T(8,128)(2,1)}, u32[]{:S(2)}) copy-start(bf16[2,1024,1024]{2,1,0:T(8,128)(2,1)} %factors_ref.7) | copy-start | bytes 12582916
  18.1 2.1 %collective-permute-start.1 = (bf16[128,512]{1,0:T(8,128)(2,1)S(1)}, bf16[128,512]{1,0:T(8,128)(2,1)S(1)}, u32[]{:S(2)}, u32[]{:S(2)}) collective-permute-start(bf16[128,512]{1,0:T(8,128)(2,1)S(1)} %get-tuple-element.30), channel_id=1, source_target_pairs={{0,4},{4,0},{8,12},{12,8},{16,20},{20,16},{24,28},{28,24},{1,5},{5... | collective-permute-start | bytes 393224 | tf_op jit(solution)/shard_map/ppermute | solution.py:29
  18.2 25.9 %collective-permute-start.10 = (bf16[1024,256]{1,0:T(8,128)(2,1)S(1)}, bf16[1024,256]{1,0:T(8,128)(2,1)S(1)}, u32[]{:S(2)}, u32[]{:S(2)}) collective-permute-start(bf16[1024,256]{1,0:T(8,128)(2,1)S(1)} %collective-permute-done.refs_1_), channel_id=1, source_target_pairs={{2,0},{1,3},{6,4},{5,7},{10,8},{9,11},{14,12},{13,15},{18,16},{17,... | collective-permute-start | bytes 1572872 | tf_op jit(solution)/shard_map/ppermute | solution.py:286
  19.5 24.6 %collective-permute-start.9 = (bf16[1024,256]{1,0:T(8,128)(2,1)S(1)}, bf16[1024,256]{1,0:T(8,128)(2,1)S(1)}, u32[]{:S(2)}, u32[]{:S(2)}) collective-permute-start(bf16[1024,256]{1,0:T(8,128)(2,1)S(1)} %collective-permute-done.refs_1_), channel_id=1, source_target_pairs={{1,2},{2,1},{5,6},{6,5},{9,10},{10,9},{13,14},{14,13},{17,18},{18,... | collective-permute-start | bytes 1572872 | tf_op jit(solution)/shard_map/ppermute | solution.py:286
  20.2 31.9 %collective-permute-start.8 = (bf16[1024,256]{1,0:T(8,128)(2,1)}, bf16[1024,256]{1,0:T(8,128)(2,1)S(1)}, u32[]{:S(2)}, u32[]{:S(2)}) collective-permute-start(bf16[1024,256]{1,0:T(8,128)(2,1)} %collective-permute-done.7.refs_2_.refs_0_), channel_id=1, source_target_pairs={{1,0},{2,3},{5,4},{6,7},{9,8},{10,11},{13,12},{14,15},{17,16},{18,... | collective-permute-start | bytes 1572872 | tf_op jit(solution)/shard_map/ppermute | solution.py:286
  27.5 5.0 %collective-permute-start.2 = (bf16[128,512]{1,0:T(8,128)(2,1)S(1)}, bf16[128,512]{1,0:T(8,128)(2,1)S(1)}, u32[]{:S(2)}, u32[]{:S(2)}) collective-permute-start(bf16[128,512]{1,0:T(8,128)(2,1)S(1)} %add_convert_fusion.5), channel_id=1, source_target_pairs={{0,8},{4,12},{8,0},{12,4},{16,24},{20,28},{24,16},{28,20},{1,9},{5... | collective-permute-start | bytes 393224 | tf_op jit(solution)/shard_map/ppermute | solution.py:29
  29.2 5.9 %collective-permute-start.3 = (bf16[128,512]{1,0:T(8,128)(2,1)S(1)}, bf16[128,512]{1,0:T(8,128)(2,1)S(1)}, u32[]{:S(2)}, u32[]{:S(2)}) collective-permute-start(bf16[128,512]{1,0:T(8,128)(2,1)S(1)} %add_convert_fusion.5), channel_id=1, source_target_pairs={{0,16},{4,20},{8,24},{12,28},{16,0},{20,4},{24,8},{28,12},{1,17},{... | collective-permute-start | bytes 393224 | tf_op jit(solution)/shard_map/ppermute | solution.py:29
  32.5 5.9 %collective-permute-start.4 = (bf16[128,512]{1,0:T(8,128)(2,1)S(1)}, bf16[128,512]{1,0:T(8,128)(2,1)S(1)}, u32[]{:S(2)}, u32[]{:S(2)}) collective-permute-start(bf16[128,512]{1,0:T(8,128)(2,1)S(1)} %add_convert_fusion.5), channel_id=1, source_target_pairs={{0,24},{4,28},{8,16},{12,20},{16,8},{20,12},{24,0},{28,4},{1,25},{... | collective-permute-start | bytes 393224 | tf_op jit(solution)/shard_map/ppermute | solution.py:29
  35.1 27.9 %collective-permute-start.15 = (bf16[1024,256]{1,0:T(8,128)(2,1)S(1)}, bf16[1024,256]{1,0:T(8,128)(2,1)S(1)}, u32[]{:S(2)}, u32[]{:S(2)}) collective-permute-start(bf16[1024,256]{1,0:T(8,128)(2,1)S(1)} %collective-permute-done.14.refs_2_), channel_id=1, source_target_pairs={{1,0},{2,3},{5,4},{6,7},{9,8},{10,11},{13,12},{14,15},{17,16},{18,... | collective-permute-start | bytes 1572872 | tf_op jit(solution)/shard_map/ppermute | solution.py:286
  38.4 24.6 %collective-permute-start.11 = (bf16[1024,256]{1,0:T(8,128)(2,1)S(1)}, bf16[1024,256]{1,0:T(8,128)(2,1)S(1)}, u32[]{:S(2)}, u32[]{:S(2)}) collective-permute-start(bf16[1024,256]{1,0:T(8,128)(2,1)S(1)} %collective-permute-done.5.refs_1_), channel_id=1, source_target_pairs={{1,2},{2,1},{5,6},{6,5},{9,10},{10,9},{13,14},{14,13},{17,18},{18,... | collective-permute-start | bytes 1572872 | tf_op jit(solution)/shard_map/ppermute | solution.py:286
  44.1 9.1 %collective-permute-start.6 = (bf16[128,512]{1,0:T(8,128)(2,1)S(1)}, bf16[128,512]{1,0:T(8,128)(2,1)S(1)}, u32[]{:S(2)}, u32[]{:S(2)}) collective-permute-start(bf16[128,512]{1,0:T(8,128)(2,1)S(1)} %add_convert_fusion.4.refs_0_), channel_id=1, source_target_pairs={{0,4},{4,0},{8,12},{12,8},{16,20},{20,16},{24,28},{28,24},{1,5},{5... | collective-permute-start | bytes 393224 | tf_op jit(solution)/shard_map/ppermute | solution.py:29
  53.2 1.7 %collective-permute-start.12 = (bf16[128,512]{1,0:T(8,128)(2,1)S(1)}, bf16[128,512]{1,0:T(8,128)(2,1)S(1)}, u32[]{:S(2)}, u32[]{:S(2)}) collective-permute-start(bf16[128,512]{1,0:T(8,128)(2,1)S(1)} %get-tuple-element.37), channel_id=1, source_target_pairs={{0,4},{4,0},{8,12},{12,8},{16,20},{20,16},{24,28},{28,24},{1,5},{5... | collective-permute-start | bytes 393224 | tf_op jit(solution)/shard_map/ppermute | solution.py:29
  55.0 8.0 %collective-permute-start.13 = (bf16[128,512]{1,0:T(8,128)(2,1)S(1)}, bf16[128,512]{1,0:T(8,128)(2,1)S(1)}, u32[]{:S(2)}, u32[]{:S(2)}) collective-permute-start(bf16[128,512]{1,0:T(8,128)(2,1)S(1)} %add_convert_fusion.3), channel_id=1, source_target_pairs={{0,8},{4,12},{8,0},{12,4},{16,24},{20,28},{24,16},{28,20},{1,9},{5... | collective-permute-start | bytes 393224 | tf_op jit(solution)/shard_map/ppermute | solution.py:29
  56.5 8.4 %collective-permute-start.16 = (bf16[128,512]{1,0:T(8,128)(2,1)S(1)}, bf16[128,512]{1,0:T(8,128)(2,1)S(1)}, u32[]{:S(2)}, u32[]{:S(2)}) collective-permute-start(bf16[128,512]{1,0:T(8,128)(2,1)S(1)} %add_convert_fusion.3), channel_id=1, source_target_pairs={{0,16},{4,20},{8,24},{12,28},{16,0},{20,4},{24,8},{28,12},{1,17},{... | collective-permute-start | bytes 393224 | tf_op jit(solution)/shard_map/ppermute | solution.py:29
  58.0 6.9 %collective-permute-start.17 = (bf16[128,512]{1,0:T(8,128)(2,1)S(1)}, bf16[128,512]{1,0:T(8,128)(2,1)S(1)}, u32[]{:S(2)}, u32[]{:S(2)}) collective-permute-start(bf16[128,512]{1,0:T(8,128)(2,1)S(1)} %add_convert_fusion.3), channel_id=1, source_target_pairs={{0,24},{4,28},{8,16},{12,20},{16,8},{20,12},{24,0},{28,4},{1,25},{... | collective-permute-start | bytes 393224 | tf_op jit(solution)/shard_map/ppermute | solution.py:29
  65.0 1.4 %collective-permute-start.18 = (bf16[128,512]{1,0:T(8,128)(2,1)S(1)}, bf16[128,512]{1,0:T(8,128)(2,1)S(1)}, u32[]{:S(2)}, u32[]{:S(2)}) collective-permute-start(bf16[128,512]{1,0:T(8,128)(2,1)S(1)} %add_convert_fusion.2.own_ref), channel_id=1, source_target_pairs={{0,4},{4,0},{8,12},{12,8},{16,20},{20,16},{24,28},{28,24},{1,5},{5... | collective-permute-start | bytes 393224 | tf_op jit(solution)/shard_map/ppermute | solution.py:29
  68.8 1.5 %collective-permute-start.19 = (bf16[128,768]{1,0:T(8,128)(2,1)S(1)}, bf16[128,768]{1,0:T(8,128)(2,1)S(1)}, u32[]{:S(2)}, u32[]{:S(2)}) collective-permute-start(bf16[128,768]{1,0:T(8,128)(2,1)S(1)} %get-tuple-element.42), channel_id=1, source_target_pairs={{0,4},{4,0},{8,12},{12,8},{16,20},{20,16},{24,28},{28,24},{1,5},{5... | collective-permute-start | bytes 589832 | tf_op jit(solution)/shard_map/ppermute | solution.py:29
  69.0 18.4 %collective-permute-start.24 = (bf16[1024,256]{1,0:T(8,128)(2,1)S(1)}, bf16[1024,256]{1,0:T(8,128)(2,1)S(1)}, u32[]{:S(2)}, u32[]{:S(2)}) collective-permute-start(bf16[1024,256]{1,0:T(8,128)(2,1)S(1)} %collective-permute-done.11.refs_4_.refs_0_), channel_id=1, source_target_pairs={{1,0},{2,3},{5,4},{6,7},{9,8},{10,11},{13,12},{14,15},{17,16},{18,... | collective-permute-start | bytes 1572872 | tf_op jit(solution)/shard_map/ppermute | solution.py:286
  70.4 17.6 %collective-permute-start.20 = (bf16[128,768]{1,0:T(8,128)(2,1)S(1)}, bf16[128,768]{1,0:T(8,128)(2,1)S(1)}, u32[]{:S(2)}, u32[]{:S(2)}) collective-permute-start(bf16[128,768]{1,0:T(8,128)(2,1)S(1)} %add_convert_fusion.1), channel_id=1, source_target_pairs={{0,8},{4,12},{8,0},{12,4},{16,24},{20,28},{24,16},{28,20},{1,9},{5... | collective-permute-start | bytes 589832 | tf_op jit(solution)/shard_map/ppermute | solution.py:29
  71.7 16.3 %collective-permute-start.21 = (bf16[128,768]{1,0:T(8,128)(2,1)S(1)}, bf16[128,768]{1,0:T(8,128)(2,1)S(1)}, u32[]{:S(2)}, u32[]{:S(2)}) collective-permute-start(bf16[128,768]{1,0:T(8,128)(2,1)S(1)} %add_convert_fusion.1), channel_id=1, source_target_pairs={{0,16},{4,20},{8,24},{12,28},{16,0},{20,4},{24,8},{28,12},{1,17},{... | collective-permute-start | bytes 589832 | tf_op jit(solution)/shard_map/ppermute | solution.py:29
  72.5 15.5 %collective-permute-start.22 = (bf16[128,768]{1,0:T(8,128)(2,1)S(1)}, bf16[128,768]{1,0:T(8,128)(2,1)S(1)}, u32[]{:S(2)}, u32[]{:S(2)}) collective-permute-start(bf16[128,768]{1,0:T(8,128)(2,1)S(1)} %add_convert_fusion.1), channel_id=1, source_target_pairs={{0,24},{4,28},{8,16},{12,20},{16,8},{20,12},{24,0},{28,4},{1,25},{... | collective-permute-start | bytes 589832 | tf_op jit(solution)/shard_map/ppermute | solution.py:29
  87.9 1.3 %collective-permute-start.25 = (bf16[128,256]{1,0:T(8,128)(2,1)S(1)}, bf16[128,256]{1,0:T(8,128)(2,1)S(1)}, u32[]{:S(2)}, u32[]{:S(2)}) collective-permute-start(bf16[128,256]{1,0:T(8,128)(2,1)S(1)} %get-tuple-element.46), channel_id=1, source_target_pairs={{0,4},{4,0},{8,12},{12,8},{16,20},{20,16},{24,28},{28,24},{1,5},{5... | collective-permute-start | bytes 196616 | tf_op jit(solution)/shard_map/ppermute | solution.py:29
  88.1 4.7 %collective-permute-start.23 = (bf16[128,768]{1,0:T(8,128)(2,1)S(1)}, bf16[128,768]{1,0:T(8,128)(2,1)S(1)}, u32[]{:S(2)}, u32[]{:S(2)}) collective-permute-start(bf16[128,768]{1,0:T(8,128)(2,1)S(1)} %add_convert_fusion.refs_0_), channel_id=1, source_target_pairs={{0,4},{4,0},{8,12},{12,8},{16,20},{20,16},{24,28},{28,24},{1,5},{5... | collective-permute-start | bytes 589832 | tf_op jit(solution)/shard_map/ppermute | solution.py:29
  89.2 7.1 %collective-permute-start.26 = (bf16[128,256]{1,0:T(8,128)(2,1)S(1)}, bf16[128,256]{1,0:T(8,128)(2,1)S(1)}, u32[]{:S(2)}, u32[]{:S(2)}) collective-permute-start(bf16[128,256]{1,0:T(8,128)(2,1)S(1)} %add_convert_fusion.7), channel_id=1, source_target_pairs={{0,8},{4,12},{8,0},{12,4},{16,24},{20,28},{24,16},{28,20},{1,9},{5... | collective-permute-start | bytes 196616 | tf_op jit(solution)/shard_map/ppermute | solution.py:29
  90.5 5.8 %collective-permute-start.27 = (bf16[128,256]{1,0:T(8,128)(2,1)S(1)}, bf16[128,256]{1,0:T(8,128)(2,1)S(1)}, u32[]{:S(2)}, u32[]{:S(2)}) collective-permute-start(bf16[128,256]{1,0:T(8,128)(2,1)S(1)} %add_convert_fusion.7), channel_id=1, source_target_pairs={{0,16},{4,20},{8,24},{12,28},{16,0},{20,4},{24,8},{28,12},{1,17},{... | collective-permute-start | bytes 196616 | tf_op jit(solution)/shard_map/ppermute | solution.py:29
  91.3 5.2 %collective-permute-start.28 = (bf16[128,256]{1,0:T(8,128)(2,1)S(1)}, bf16[128,256]{1,0:T(8,128)(2,1)S(1)}, u32[]{:S(2)}, u32[]{:S(2)}) collective-permute-start(bf16[128,256]{1,0:T(8,128)(2,1)S(1)} %add_convert_fusion.7), channel_id=1, source_target_pairs={{0,24},{4,28},{8,16},{12,20},{16,8},{20,12},{24,0},{28,4},{1,25},{... | collective-permute-start | bytes 196616 | tf_op jit(solution)/shard_map/ppermute | solution.py:29
  96.5 1.3 %collective-permute-start.29 = (bf16[128,256]{1,0:T(8,128)(2,1)S(1)}, bf16[128,256]{1,0:T(8,128)(2,1)S(1)}, u32[]{:S(2)}, u32[]{:S(2)}) collective-permute-start(bf16[128,256]{1,0:T(8,128)(2,1)S(1)} %add_convert_fusion.6.own_ref), channel_id=1, source_target_pairs={{0,4},{4,0},{8,12},{12,8},{16,20},{20,16},{24,28},{28,24},{1,5},{5... | collective-permute-start | bytes 196616 | tf_op jit(solution)/shard_map/ppermute | solution.py:29

commit v5 on v4

--- a/solution.py
+++ b/solution.py
@@ -239,7 +239,9 @@
             pltpu.SemaphoreType.DMA((len(parts) + 1,)),
         ],
         compiler_params=pltpu.CompilerParams(vmem_limit_bytes=VMEM),
-        cost_estimate=pl.CostEstimate(flops=2 * size * columns * rows, bytes_accessed=2 * rows * size, transcendentals=0),
+        cost_estimate=pl.CostEstimate(
+            flops=WEIGHT * 2 * size * columns * rows, bytes_accessed=WEIGHT * 2 * rows * size, transcendentals=0
+        ),
     )(current, *arrays)
 
 
@@ -247,6 +249,7 @@
 PIECES = {'O': 1, 'F3': 1}
 JOINED = 'swap'
 WHOLE = ()
+WEIGHT = 16
 DIRECT = ('0.0', '0.1', '0.2', '1.0', '1.1', '1.2')
 SKIP = ('E3',)
 GATES = {
@@ -351,7 +354,7 @@
             mine, bit = self("b" + name[1:]), 2
             while bit < self.m:
                 if name[1:] in DIRECT or 2 * bit >= self.m:
-                    got = [swap(mine, s * bit, self.m) for s in range(1, 4) if s * bit < self.m]
+                    got = [swap(mine, s * bit, self.m) for s in (3, 1, 2) if s * bit < self.m]
                     mine = sum([self.gated(name, g).astype(F32) for g in got], mine.astype(F32)).astype(BF16)
                 else:
                     halves = jnp.split(mine, 2)

time: 99.7 us -> 95.8 us (0.961)
  waiting for transfers between devices: 49.2 us -> 46.1 us
  starting transfers between devices: 33 us -> 32 us
    ppermute x10, waiting for transfers between devices: 40.1 us -> 35 us  [send(): return lax.ppermute(self.gated(name, x), 'vecs', pairs)]
    ppermute x20, waiting for transfers between devices: 9.04 us -> 11.1 us  [swap(): return lax.ppermute(x, 'rows', [(i, i ^ bit) for i in range(m)])]
    ppermute x20, starting transfers between devices: 17.6 us -> 16.6 us  [swap(): return lax.ppermute(x, 'rows', [(i, i ^ bit) for i in range(m)])]
  transfers between devices with their start and end apart: 30 -> 30, of which waited for: 13 -> 13; matrix products, arithmetic and copies ran while one was open for 2% -> 2% of each run, Pallas kernels for 10% -> 13%
where the time goes in v5:
time: 95.8 us; the launch traced here: 95.3 us
  waiting for transfers between devices  46.1 us (48%)
  starting transfers between devices  32 us (33%)
  Pallas kernels  13.9 us (15%)
  local copies, waits for them, and re-layouts  2.52 us (3%)
    ppermute x10, waiting for transfers between devices, send(): return lax.ppermute(self.gated(name, x), 'vecs', pairs)  35 us
    ppermute x20, starting transfers between devices, swap(): return lax.ppermute(x, 'rows', [(i, i ^ bit) for i in range(m)])  16.6 us
    ppermute x10, starting transfers between devices, send(): return lax.ppermute(self.gated(name, x), 'vecs', pairs)  15.4 us
    ppermute x20, waiting for transfers between devices, swap(): return lax.ppermute(x, 'rows', [(i, i ^ bit) for i in range(m)])  11.1 us
    pallas_call x6, Pallas kernels, call(): pl.pallas_call(kernel, in_specs=[ANY] * len(inputs), out_specs=[IN_VMEM]...  10.1 us
    pallas_call x4, Pallas kernels, coeff(): pl.pallas_call(functools.partial(coeff_kernel, parts), in_specs=[ANY] * (...  3.76 us
  transfers between devices with their start and end apart: 30, of which 13 were waited for; matrix products, arithmetic and copies ran while one was open for 2% of the time, Pallas kernels for 13%

profile of v5, /device:TPU:0, one launch (start us, length us, event | category | flops | bytes accessed | tf_op | source)
XLA Modules:
  0.0 95.3 jit_solution(791723500124860442)
XLA Ops:
  0.0 1.3 %slice_bitcast_fusion = (bf16[1024,256]{1,0:T(8,128)(2,1)S(1)}, bf16[1024,256]{1,0:T(8,128)(2,1)S(1)}) fusion(bf16[2,1024,256]{2,1,0:T(8,128)(2,1)} %param.4), kind=kLoop, calls=%fused_computation | loop fusion | bytes 2097152 | tf_op jit(solution)/shard_map/squeeze | solution.py:304
  1.3 3.1 %collective-permute-start = (bf16[1024,256]{1,0:T(8,128)(2,1)S(1)}, bf16[1024,256]{1,0:T(8,128)(2,1)S(1)}, u32[]{:S(2)}, u32[]{:S(2)}) collective-permute-start(bf16[1024,256]{1,0:T(8,128)(2,1)S(1)} %get-tuple-element.52.refs_0_), channel_id=1, source_target_pairs={{0,1},{1,0},{2,3},{3,2},{4,5},{5,4},{6,7},{7,6},{8,9},{9,8},{10,11... | collective-permute-start | bytes 1572872 | tf_op jit(solution)/shard_map/ppermute | solution.py:289
  4.4 1.4 %collective-permute-start.7 = (bf16[1024,256]{1,0:T(8,128)(2,1)S(1)}, bf16[1024,256]{1,0:T(8,128)(2,1)}, u32[]{:S(2)}, u32[]{:S(2)}) collective-permute-start(bf16[1024,256]{1,0:T(8,128)(2,1)S(1)} %get-tuple-element.52.refs_0_), channel_id=1, source_target_pairs={{1,2},{2,1},{5,6},{6,5},{9,10},{10,9},{13,14},{14,13},{17,18},{18,... | collective-permute-start | bytes 1572872 | tf_op jit(solution)/shard_map/ppermute | solution.py:289
  5.8 3.7 %collective-permute-start.5 = (bf16[1024,256]{1,0:T(8,128)(2,1)S(1)}, bf16[1024,256]{1,0:T(8,128)(2,1)S(1)}, u32[]{:S(2)}, u32[]{:S(2)}) collective-permute-start(bf16[1024,256]{1,0:T(8,128)(2,1)S(1)} %get-tuple-element.51.refs_0_), channel_id=1, source_target_pairs={{0,1},{1,0},{2,3},{3,2},{4,5},{5,4},{6,7},{7,6},{8,9},{9,8},{10,11... | collective-permute-start | bytes 1572872 | tf_op jit(solution)/shard_map/ppermute | solution.py:289
  9.5 0.7 collective-permute-start.14
  10.2 1.2 %copy.4 = bf16[1024,256]{0,1:T(8,128)(2,1)S(1)} copy(bf16[1024,256]{1,0:T(8,128)(2,1)} %param.3) | data formatting | bytes 1048576 | tf_op jit(solution)/shard_map/optimization_barrier | solution.py:17
  11.4 5.7 %collective-permute-done.refs_1_ = bf16[1024,256]{1,0:T(8,128)(2,1)S(1)} collective-permute-done((bf16[1024,256]{1,0:T(8,128)(2,1)S(1)}, bf16[1024,256]{1,0:T(8,128)(2,1)S(1)}, u32[]{:S(2)}, u32[]{:S(2)}) %collective-permute-start) | collective-permute-done | bytes 524320 | tf_op jit(solution)/shard_map/ppermute | solution.py:289
  17.1 1.0 %shard_map.37 = (bf16[128,512]{1,0:T(8,128)(2,1)S(1)}, bf16[128,512]{1,0:T(8,128)(2,1)S(1)}) custom-call(bf16[256,1024]{1,0:T(8,128)(2,1)S(1)} %bitcast.5, bf16[1024,256]{1,0:T(8,128)(2,1)S(1)} %get-tuple-element.52.refs_0_, bf16[1024,256]{1,0:T(8,128)(2,1)S(1)} %collective-permute-done.refs_1_), custom_call_target="tpu_custom_call" | custom-call | flops 4294967296 | bytes 16777216 | tf_op jit(solution)/shard_map/pallas_call | solution.py:231
  18.2 1.3 %collective-permute-start.10 = (bf16[1024,256]{1,0:T(8,128)(2,1)S(1)}, bf16[1024,256]{1,0:T(8,128)(2,1)S(1)}, u32[]{:S(2)}, u32[]{:S(2)}) collective-permute-start(bf16[1024,256]{1,0:T(8,128)(2,1)S(1)} %collective-permute-done.refs_1_), channel_id=1, source_target_pairs={{2,0},{1,3},{6,4},{5,7},{10,8},{9,11},{14,12},{13,15},{18,16},{17,... | collective-permute-start | bytes 1572872 | tf_op jit(solution)/shard_map/ppermute | solution.py:289
  19.5 0.7 collective-permute-start.9
  20.2 1.3 %collective-permute-start.8 = (bf16[1024,256]{1,0:T(8,128)(2,1)}, bf16[1024,256]{1,0:T(8,128)(2,1)S(1)}, u32[]{:S(2)}, u32[]{:S(2)}) collective-permute-start(bf16[1024,256]{1,0:T(8,128)(2,1)} %collective-permute-done.7.refs_2_.refs_0_), channel_id=1, source_target_pairs={{1,0},{2,3},{5,4},{6,7},{9,8},{10,11},{13,12},{14,15},{17,16},{18,... | collective-permute-start | bytes 1572872 | tf_op jit(solution)/shard_map/ppermute | solution.py:289
  21.6 6.0 %collective-permute-done.5.refs_1_ = bf16[1024,256]{1,0:T(8,128)(2,1)S(1)} collective-permute-done((bf16[1024,256]{1,0:T(8,128)(2,1)S(1)}, bf16[1024,256]{1,0:T(8,128)(2,1)S(1)}, u32[]{:S(2)}, u32[]{:S(2)}) %collective-permute-start.5) | collective-permute-done | bytes 524320 | tf_op jit(solution)/shard_map/ppermute | solution.py:289
  27.5 2.6 %collective-permute-start.2 = (bf16[128,512]{1,0:T(8,128)(2,1)S(1)}, bf16[128,512]{1,0:T(8,128)(2,1)S(1)}, u32[]{:S(2)}, u32[]{:S(2)}) collective-permute-start(bf16[128,512]{1,0:T(8,128)(2,1)S(1)} %add_convert_fusion.5), channel_id=1, source_target_pairs={{0,24},{4,28},{8,16},{12,20},{16,8},{20,12},{24,0},{28,4},{1,25},{... | collective-permute-start | bytes 393224 | tf_op jit(solution)/shard_map/ppermute | solution.py:29
  30.1 0.5 collective-permute-start.3
  30.7 3.9 %collective-permute-done.2 = bf16[128,512]{1,0:T(8,128)(2,1)S(1)} collective-permute-done((bf16[128,512]{1,0:T(8,128)(2,1)S(1)}, bf16[128,512]{1,0:T(8,128)(2,1)S(1)}, u32[]{:S(2)}, u32[]{:S(2)}) %collective-permute-start.2) | collective-permute-done | bytes 131104 | tf_op jit(solution)/shard_map/ppermute | solution.py:29
  34.6 1.3 %collective-permute-start.4 = (bf16[128,512]{1,0:T(8,128)(2,1)S(1)}, bf16[128,512]{1,0:T(8,128)(2,1)S(1)}, u32[]{:S(2)}, u32[]{:S(2)}) collective-permute-start(bf16[128,512]{1,0:T(8,128)(2,1)S(1)} %add_convert_fusion.5), channel_id=1, source_target_pairs={{0,16},{4,20},{8,24},{12,28},{16,0},{20,4},{24,8},{28,12},{1,17},{... | collective-permute-start | bytes 393224 | tf_op jit(solution)/shard_map/ppermute | solution.py:29
  35.9 1.3 %collective-permute-start.15 = (bf16[1024,256]{1,0:T(8,128)(2,1)S(1)}, bf16[1024,256]{1,0:T(8,128)(2,1)S(1)}, u32[]{:S(2)}, u32[]{:S(2)}) collective-permute-start(bf16[1024,256]{1,0:T(8,128)(2,1)S(1)} %collective-permute-done.14.refs_2_), channel_id=1, source_target_pairs={{1,0},{2,3},{5,4},{6,7},{9,8},{10,11},{13,12},{14,15},{17,16},{18,... | collective-permute-start | bytes 1572872 | tf_op jit(solution)/shard_map/ppermute | solution.py:289
  37.2 2.4 %collective-permute-done.4 = bf16[128,512]{1,0:T(8,128)(2,1)S(1)} collective-permute-done((bf16[128,512]{1,0:T(8,128)(2,1)S(1)}, bf16[128,512]{1,0:T(8,128)(2,1)S(1)}, u32[]{:S(2)}, u32[]{:S(2)}) %collective-permute-start.4) | collective-permute-done | bytes 131104 | tf_op jit(solution)/shard_map/ppermute | solution.py:29
  39.6 0.7 collective-permute-start.11
  40.4 3.8 %collective-permute-done.10.refs_5_.refs_3_ = bf16[1024,256]{1,0:T(8,128)(2,1)S(1)} collective-permute-done((bf16[1024,256]{1,0:T(8,128)(2,1)S(1)}, bf16[1024,256]{1,0:T(8,128)(2,1)S(1)}, u32[]{:S(2)}, u32[]{:S(2)}) %collective-permute-start.10) | collective-permute-done | bytes 524320 | tf_op jit(solution)/shard_map/ppermute | solution.py:289
  44.2 8.0 %collective-permute-done.8.refs_3_.refs_1_ = bf16[1024,256]{1,0:T(8,128)(2,1)S(1)} collective-permute-done((bf16[1024,256]{1,0:T(8,128)(2,1)}, bf16[1024,256]{1,0:T(8,128)(2,1)S(1)}, u32[]{:S(2)}, u32[]{:S(2)}) %collective-permute-start.8) | collective-permute-done | bytes 524320 | tf_op jit(solution)/shard_map/ppermute | solution.py:289
  52.2 1.0 %shard_map.40 = (bf16[128,512]{1,0:T(8,128)(2,1)S(1)}, bf16[128,512]{1,0:T(8,128)(2,1)S(1)}) custom-call(bf16[256,1024]{1,0:T(8,128)(2,1)S(1)} %bitcast.6, bf16[1024,256]{1,0:T(8,128)(2,1)} %collective-permute-done.7.refs_2_.refs_0_, bf16[1024,256]{1,0:T(8,128)(2,1)S(1)} %collective-permute-done.8.refs_3_.refs_1_, ...), custom_call_target="tpu_custom_call" | custom-call | flops 4294967296 | bytes 16777216 | tf_op jit(solution)/shard_map/pallas_call | solution.py:231
  53.3 1.6 %shard_map.38.scaled_ref = bf16[1024,256]{1,0:T(8,128)(2,1)S(1)} custom-call(bf16[2,1024,1024]{2,1,0:T(8,128)(2,1)S(1)} %copy-done, bf16[128,512]{1,0:T(8,128)(2,1)S(1)} %add_convert_fusion.4.refs_0_, bf16[128,512]{1,0:T(8,128)(2,1)S(1)} %collective-permute-done.6.refs_1_), custom_call_target="tpu_custom_call" | custom-call | flops 268435456 | bytes 4456448 | tf_op jit(solution)/shard_map/pallas_call | solution.py:167
  55.0 2.5 %collective-permute-start.13 = (bf16[128,512]{1,0:T(8,128)(2,1)S(1)}, bf16[128,512]{1,0:T(8,128)(2,1)S(1)}, u32[]{:S(2)}, u32[]{:S(2)}) collective-permute-start(bf16[128,512]{1,0:T(8,128)(2,1)S(1)} %add_convert_fusion.3), channel_id=1, source_target_pairs={{0,24},{4,28},{8,16},{12,20},{16,8},{20,12},{24,0},{28,4},{1,25},{... | collective-permute-start | bytes 393224 | tf_op jit(solution)/shard_map/ppermute | solution.py:29
  57.5 0.5 collective-permute-start.16
  58.0 0.5 collective-permute-start.17
  58.5 2.5 %shard_map.39 = (f32[256,1024]{1,0:T(8,128)S(1)}, bf16[1024,512]{1,0:T(8,128)(2,1)S(1)}) custom-call(bf16[2,1024,1024]{2,1,0:T(8,128)(2,1)S(1)} %copy-done, bf16[256,1024]{1,0:T(8,128)(2,1)S(1)} %bitcast.7, bf16[1024,256]{1,0:T(8,128)(2,1)S(1)} %shard_map.38.scaled_ref, bf16[1024,256]{1,0:T(8,128)(2,1)S(1)} %get-tuple-element.52.refs_0_, ...), custom_call_target="tpu_custom_call" | custom-call | flops 1610612736 | bytes 8388608 | tf_op jit(solution)/shard_map/pallas_call | solution.py:167
  61.0 1.9 %collective-permute-done.15.refs_3_ = bf16[1024,256]{1,0:T(8,128)(2,1)S(1)} collective-permute-done((bf16[1024,256]{1,0:T(8,128)(2,1)S(1)}, bf16[1024,256]{1,0:T(8,128)(2,1)S(1)}, u32[]{:S(2)}, u32[]{:S(2)}) %collective-permute-start.15) | collective-permute-done | bytes 524320 | tf_op jit(solution)/shard_map/ppermute | solution.py:289
  63.0 1.7 %collective-permute-done.16 = bf16[128,512]{1,0:T(8,128)(2,1)S(1)} collective-permute-done((bf16[128,512]{1,0:T(8,128)(2,1)S(1)}, bf16[128,512]{1,0:T(8,128)(2,1)S(1)}, u32[]{:S(2)}, u32[]{:S(2)}) %collective-permute-start.16) | collective-permute-done | bytes 131104 | tf_op jit(solution)/shard_map/ppermute | solution.py:29
  64.9 1.3 %collective-permute-start.24 = (bf16[1024,256]{1,0:T(8,128)(2,1)S(1)}, bf16[1024,256]{1,0:T(8,128)(2,1)S(1)}, u32[]{:S(2)}, u32[]{:S(2)}) collective-permute-start(bf16[1024,256]{1,0:T(8,128)(2,1)S(1)} %collective-permute-done.11.refs_4_.refs_0_), channel_id=1, source_target_pairs={{1,0},{2,3},{5,4},{6,7},{9,8},{10,11},{13,12},{14,15},{17,16},{18,... | collective-permute-start | bytes 1572872 | tf_op jit(solution)/shard_map/ppermute | solution.py:289
  66.2 1.0 %shard_map.41.current_ref = bf16[256,1024]{1,0:T(8,128)(2,1)S(1)} custom-call(f32[256,1024]{1,0:T(8,128)S(1)} %get-tuple-element.33.rest_ref, bf16[1024,512]{1,0:T(8,128)(2,1)S(1)} %get-tuple-element.34.across_ref, bf16[128,512]{1,0:T(8,128)(2,1)S(1)} %add_convert_fusion.2.own_ref, bf16[128,512]{1,0:T(8,128)(2,1)S(1)} %collective-permute-done.18.other_ref), custom_call_target="tpu_custom_call" | custom-call | flops 268435456 | bytes 2359296 | tf_op jit(solution)/shard_map/pallas_call | solution.py:167
  67.2 1.4 %shard_map.42 = (bf16[128,768]{1,0:T(8,128)(2,1)S(1)}, bf16[128,768]{1,0:T(8,128)(2,1)S(1)}) custom-call(bf16[256,1024]{1,0:T(8,128)(2,1)S(1)} %shard_map.41.current_ref, bf16[1024,256]{1,0:T(8,128)(2,1)S(1)} %get-tuple-element.51.refs_0_, bf16[1024,256]{1,0:T(8,128)(2,1)S(1)} %collective-permute-done.5.refs_1_, ...), custom_call_target="tpu_custom_call" | custom-call | flops 6442450944 | bytes 25165824 | tf_op jit(solution)/shard_map/pallas_call | solution.py:231
  68.6 0.5 collective-permute-start.19
  69.1 1.1 %collective-permute-done.19 = bf16[128,768]{1,0:T(8,128)(2,1)S(1)} collective-permute-done((bf16[128,768]{1,0:T(8,128)(2,1)S(1)}, bf16[128,768]{1,0:T(8,128)(2,1)S(1)}, u32[]{:S(2)}, u32[]{:S(2)}) %collective-permute-start.19) | collective-permute-done | bytes 196640 | tf_op jit(solution)/shard_map/ppermute | solution.py:29
  70.2 2.4 %collective-permute-start.20 = (bf16[128,768]{1,0:T(8,128)(2,1)S(1)}, bf16[128,768]{1,0:T(8,128)(2,1)S(1)}, u32[]{:S(2)}, u32[]{:S(2)}) collective-permute-start(bf16[128,768]{1,0:T(8,128)(2,1)S(1)} %add_convert_fusion.1), channel_id=1, source_target_pairs={{0,24},{4,28},{8,16},{12,20},{16,8},{20,12},{24,0},{28,4},{1,25},{... | collective-permute-start | bytes 589832 | tf_op jit(solution)/shard_map/ppermute | solution.py:29
  72.7 0.5 collective-permute-start.21
  73.2 0.6 collective-permute-start.22
  73.8 9.7 %collective-permute-done.24.refs_5_.refs_1_ = bf16[1024,256]{1,0:T(8,128)(2,1)S(1)} collective-permute-done((bf16[1024,256]{1,0:T(8,128)(2,1)S(1)}, bf16[1024,256]{1,0:T(8,128)(2,1)S(1)}, u32[]{:S(2)}, u32[]{:S(2)}) %collective-permute-start.24) | collective-permute-done | bytes 524320 | tf_op jit(solution)/shard_map/ppermute | solution.py:289
  83.5 0.4 shard_map.45
  84.1 0.5 collective-permute-start.23
  84.6 0.6 collective-permute-done.25
  85.2 2.4 %collective-permute-start.26 = (bf16[128,256]{1,0:T(8,128)(2,1)S(1)}, bf16[128,256]{1,0:T(8,128)(2,1)S(1)}, u32[]{:S(2)}, u32[]{:S(2)}) collective-permute-start(bf16[128,256]{1,0:T(8,128)(2,1)S(1)} %add_convert_fusion.7), channel_id=1, source_target_pairs={{0,24},{4,28},{8,16},{12,20},{16,8},{20,12},{24,0},{28,4},{1,25},{... | collective-permute-start | bytes 196616 | tf_op jit(solution)/shard_map/ppermute | solution.py:29
  87.6 0.5 collective-permute-start.27
  88.2 0.6 collective-permute-start.28
  88.8 1.7 %shard_map.43.scaled_ref = bf16[1024,256]{1,0:T(8,128)(2,1)S(1)} custom-call(bf16[2,1024,1024]{2,1,0:T(8,128)(2,1)S(1)} %copy-done, bf16[128,768]{1,0:T(8,128)(2,1)S(1)} %add_convert_fusion.refs_0_, bf16[128,768]{1,0:T(8,128)(2,1)S(1)} %collective-permute-done.23.refs_1_), custom_call_target="tpu_custom_call" | custom-call | flops 268435456 | bytes 4587520 | tf_op jit(solution)/shard_map/pallas_call | solution.py:167
  90.5 1.8 %shard_map.44 = (f32[1024,256]{1,0:T(8,128)S(1)}, bf16[1024,256]{1,0:T(8,128)(2,1)S(1)}) custom-call(bf16[2,1024,1024]{2,1,0:T(8,128)(2,1)S(1)} %copy-done, bf16[256,1024]{1,0:T(8,128)(2,1)S(1)} %shard_map.41.current_ref, bf16[1024,256]{1,0:T(8,128)(2,1)S(1)} %shard_map.43.scaled_ref, bf16[1024,256]{1,0:T(8,128)(2,1)S(1)} %get-tuple-element.51.refs_0_, ...), custom_call_target="tpu_custom_call" | custom-call | flops 1073741824 | bytes 8388608 | tf_op jit(solution)/shard_map/pallas_call | solution.py:167
  92.6 1.2 %collective-permute-done.29.other_ref = bf16[128,256]{1,0:T(8,128)(2,1)S(1)} collective-permute-done((bf16[128,256]{1,0:T(8,128)(2,1)S(1)}, bf16[128,256]{1,0:T(8,128)(2,1)S(1)}, u32[]{:S(2)}, u32[]{:S(2)}) %collective-permute-start.29) | collective-permute-done | bytes 65568 | tf_op jit(solution)/shard_map/ppermute | solution.py:29
  93.8 1.5 %shard_map.46 = bf16[1024,256]{1,0:T(8,128)(2,1)} custom-call(f32[1024,256]{1,0:T(8,128)S(1)} %get-tuple-element.43.rest_ref, bf16[1024,256]{1,0:T(8,128)(2,1)S(1)} %get-tuple-element.44.across_ref, bf16[128,256]{1,0:T(8,128)(2,1)S(1)} %add_convert_fusion.6.own_ref, bf16[128,256]{1,0:T(8,128)(2,1)S(1)} %collective-permute-done.29.other_ref), custom_call_target="tpu_custom_call" | custom-call | flops 134217728 | bytes 1703936 | tf_op jit(solution)/shard_map/pallas_call | solution.py:167
  (34 shorter events, 0.9 us)
Async XLA Ops:
  1.3 15.8 %collective-permute-start = (bf16[1024,256]{1,0:T(8,128)(2,1)S(1)}, bf16[1024,256]{1,0:T(8,128)(2,1)S(1)}, u32[]{:S(2)}, u32[]{:S(2)}) collective-permute-start(bf16[1024,256]{1,0:T(8,128)(2,1)S(1)} %get-tuple-element.52.refs_0_), channel_id=1, source_target_pairs={{0,1},{1,0},{2,3},{3,2},{4,5},{5,4},{6,7},{7,6},{8,9},{9,8},{10,11... | collective-permute-start | bytes 1572872 | tf_op jit(solution)/shard_map/ppermute | solution.py:289
  4.4 15.1 %collective-permute-start.7 = (bf16[1024,256]{1,0:T(8,128)(2,1)S(1)}, bf16[1024,256]{1,0:T(8,128)(2,1)}, u32[]{:S(2)}, u32[]{:S(2)}) collective-permute-start(bf16[1024,256]{1,0:T(8,128)(2,1)S(1)} %get-tuple-element.52.refs_0_), channel_id=1, source_target_pairs={{1,2},{2,1},{5,6},{6,5},{9,10},{10,9},{13,14},{14,13},{17,18},{18,... | collective-permute-start | bytes 1572872 | tf_op jit(solution)/shard_map/ppermute | solution.py:289
  5.8 21.7 %collective-permute-start.5 = (bf16[1024,256]{1,0:T(8,128)(2,1)S(1)}, bf16[1024,256]{1,0:T(8,128)(2,1)S(1)}, u32[]{:S(2)}, u32[]{:S(2)}) collective-permute-start(bf16[1024,256]{1,0:T(8,128)(2,1)S(1)} %get-tuple-element.51.refs_0_), channel_id=1, source_target_pairs={{0,1},{1,0},{2,3},{3,2},{4,5},{5,4},{6,7},{7,6},{8,9},{9,8},{10,11... | collective-permute-start | bytes 1572872 | tf_op jit(solution)/shard_map/ppermute | solution.py:289
  9.5 20.6 %collective-permute-start.14 = (bf16[1024,256]{1,0:T(8,128)(2,1)S(1)}, bf16[1024,256]{1,0:T(8,128)(2,1)S(1)}, u32[]{:S(2)}, u32[]{:S(2)}) collective-permute-start(bf16[1024,256]{1,0:T(8,128)(2,1)S(1)} %get-tuple-element.51.refs_0_), channel_id=1, source_target_pairs={{1,2},{2,1},{5,6},{6,5},{9,10},{10,9},{13,14},{14,13},{17,18},{18,... | collective-permute-start | bytes 1572872 | tf_op jit(solution)/shard_map/ppermute | solution.py:289
  18.1 2.1 %collective-permute-start.1 = (bf16[128,512]{1,0:T(8,128)(2,1)S(1)}, bf16[128,512]{1,0:T(8,128)(2,1)S(1)}, u32[]{:S(2)}, u32[]{:S(2)}) collective-permute-start(bf16[128,512]{1,0:T(8,128)(2,1)S(1)} %get-tuple-element.30), channel_id=1, source_target_pairs={{0,4},{4,0},{8,12},{12,8},{16,20},{20,16},{24,28},{28,24},{1,5},{5... | collective-permute-start | bytes 393224 | tf_op jit(solution)/shard_map/ppermute | solution.py:29
  18.2 25.9 %collective-permute-start.10 = (bf16[1024,256]{1,0:T(8,128)(2,1)S(1)}, bf16[1024,256]{1,0:T(8,128)(2,1)S(1)}, u32[]{:S(2)}, u32[]{:S(2)}) collective-permute-start(bf16[1024,256]{1,0:T(8,128)(2,1)S(1)} %collective-permute-done.refs_1_), channel_id=1, source_target_pairs={{2,0},{1,3},{6,4},{5,7},{10,8},{9,11},{14,12},{13,15},{18,16},{17,... | collective-permute-start | bytes 1572872 | tf_op jit(solution)/shard_map/ppermute | solution.py:289
  19.5 24.6 %collective-permute-start.9 = (bf16[1024,256]{1,0:T(8,128)(2,1)S(1)}, bf16[1024,256]{1,0:T(8,128)(2,1)S(1)}, u32[]{:S(2)}, u32[]{:S(2)}) collective-permute-start(bf16[1024,256]{1,0:T(8,128)(2,1)S(1)} %collective-permute-done.refs_1_), channel_id=1, source_target_pairs={{1,2},{2,1},{5,6},{6,5},{9,10},{10,9},{13,14},{14,13},{17,18},{18,... | collective-permute-start | bytes 1572872 | tf_op jit(solution)/shard_map/ppermute | solution.py:289
  20.2 31.9 %collective-permute-start.8 = (bf16[1024,256]{1,0:T(8,128)(2,1)}, bf16[1024,256]{1,0:T(8,128)(2,1)S(1)}, u32[]{:S(2)}, u32[]{:S(2)}) collective-permute-start(bf16[1024,256]{1,0:T(8,128)(2,1)} %collective-permute-done.7.refs_2_.refs_0_), channel_id=1, source_target_pairs={{1,0},{2,3},{5,4},{6,7},{9,8},{10,11},{13,12},{14,15},{17,16},{18,... | collective-permute-start | bytes 1572872 | tf_op jit(solution)/shard_map/ppermute | solution.py:289
  27.5 7.1 %collective-permute-start.2 = (bf16[128,512]{1,0:T(8,128)(2,1)S(1)}, bf16[128,512]{1,0:T(8,128)(2,1)S(1)}, u32[]{:S(2)}, u32[]{:S(2)}) collective-permute-start(bf16[128,512]{1,0:T(8,128)(2,1)S(1)} %add_convert_fusion.5), channel_id=1, source_target_pairs={{0,24},{4,28},{8,16},{12,20},{16,8},{20,12},{24,0},{28,4},{1,25},{... | collective-permute-start | bytes 393224 | tf_op jit(solution)/shard_map/ppermute | solution.py:29
  30.1 5.8 %collective-permute-start.3 = (bf16[128,512]{1,0:T(8,128)(2,1)S(1)}, bf16[128,512]{1,0:T(8,128)(2,1)S(1)}, u32[]{:S(2)}, u32[]{:S(2)}) collective-permute-start(bf16[128,512]{1,0:T(8,128)(2,1)S(1)} %add_convert_fusion.5), channel_id=1, source_target_pairs={{0,8},{4,12},{8,0},{12,4},{16,24},{20,28},{24,16},{28,20},{1,9},{5... | collective-permute-start | bytes 393224 | tf_op jit(solution)/shard_map/ppermute | solution.py:29
  34.6 5.0 %collective-permute-start.4 = (bf16[128,512]{1,0:T(8,128)(2,1)S(1)}, bf16[128,512]{1,0:T(8,128)(2,1)S(1)}, u32[]{:S(2)}, u32[]{:S(2)}) collective-permute-start(bf16[128,512]{1,0:T(8,128)(2,1)S(1)} %add_convert_fusion.5), channel_id=1, source_target_pairs={{0,16},{4,20},{8,24},{12,28},{16,0},{20,4},{24,8},{28,12},{1,17},{... | collective-permute-start | bytes 393224 | tf_op jit(solution)/shard_map/ppermute | solution.py:29
  35.9 27.1 %collective-permute-start.15 = (bf16[1024,256]{1,0:T(8,128)(2,1)S(1)}, bf16[1024,256]{1,0:T(8,128)(2,1)S(1)}, u32[]{:S(2)}, u32[]{:S(2)}) collective-permute-start(bf16[1024,256]{1,0:T(8,128)(2,1)S(1)} %collective-permute-done.14.refs_2_), channel_id=1, source_target_pairs={{1,0},{2,3},{5,4},{6,7},{9,8},{10,11},{13,12},{14,15},{17,16},{18,... | collective-permute-start | bytes 1572872 | tf_op jit(solution)/shard_map/ppermute | solution.py:289
  39.6 23.4 %collective-permute-start.11 = (bf16[1024,256]{1,0:T(8,128)(2,1)S(1)}, bf16[1024,256]{1,0:T(8,128)(2,1)S(1)}, u32[]{:S(2)}, u32[]{:S(2)}) collective-permute-start(bf16[1024,256]{1,0:T(8,128)(2,1)S(1)} %collective-permute-done.5.refs_1_), channel_id=1, source_target_pairs={{1,2},{2,1},{5,6},{6,5},{9,10},{10,9},{13,14},{14,13},{17,18},{18,... | collective-permute-start | bytes 1572872 | tf_op jit(solution)/shard_map/ppermute | solution.py:289
  40.3 12.9 %copy-start = (bf16[2,1024,1024]{2,1,0:T(8,128)(2,1)S(1)}, bf16[2,1024,1024]{2,1,0:T(8,128)(2,1)}, u32[]{:S(2)}) copy-start(bf16[2,1024,1024]{2,1,0:T(8,128)(2,1)} %factors_ref.7) | copy-start | bytes 12582916
  44.1 9.1 %collective-permute-start.6 = (bf16[128,512]{1,0:T(8,128)(2,1)S(1)}, bf16[128,512]{1,0:T(8,128)(2,1)S(1)}, u32[]{:S(2)}, u32[]{:S(2)}) collective-permute-start(bf16[128,512]{1,0:T(8,128)(2,1)S(1)} %add_convert_fusion.4.refs_0_), channel_id=1, source_target_pairs={{0,4},{4,0},{8,12},{12,8},{16,20},{20,16},{24,28},{28,24},{1,5},{5... | collective-permute-start | bytes 393224 | tf_op jit(solution)/shard_map/ppermute | solution.py:29
  53.2 1.7 %collective-permute-start.12 = (bf16[128,512]{1,0:T(8,128)(2,1)S(1)}, bf16[128,512]{1,0:T(8,128)(2,1)S(1)}, u32[]{:S(2)}, u32[]{:S(2)}) collective-permute-start(bf16[128,512]{1,0:T(8,128)(2,1)S(1)} %get-tuple-element.37), channel_id=1, source_target_pairs={{0,4},{4,0},{8,12},{12,8},{16,20},{20,16},{24,28},{28,24},{1,5},{5... | collective-permute-start | bytes 393224 | tf_op jit(solution)/shard_map/ppermute | solution.py:29
  55.0 8.0 %collective-permute-start.13 = (bf16[128,512]{1,0:T(8,128)(2,1)S(1)}, bf16[128,512]{1,0:T(8,128)(2,1)S(1)}, u32[]{:S(2)}, u32[]{:S(2)}) collective-permute-start(bf16[128,512]{1,0:T(8,128)(2,1)S(1)} %add_convert_fusion.3), channel_id=1, source_target_pairs={{0,24},{4,28},{8,16},{12,20},{16,8},{20,12},{24,0},{28,4},{1,25},{... | collective-permute-start | bytes 393224 | tf_op jit(solution)/shard_map/ppermute | solution.py:29
  57.5 7.2 %collective-permute-start.16 = (bf16[128,512]{1,0:T(8,128)(2,1)S(1)}, bf16[128,512]{1,0:T(8,128)(2,1)S(1)}, u32[]{:S(2)}, u32[]{:S(2)}) collective-permute-start(bf16[128,512]{1,0:T(8,128)(2,1)S(1)} %add_convert_fusion.3), channel_id=1, source_target_pairs={{0,8},{4,12},{8,0},{12,4},{16,24},{20,28},{24,16},{28,20},{1,9},{5... | collective-permute-start | bytes 393224 | tf_op jit(solution)/shard_map/ppermute | solution.py:29
  58.0 6.7 %collective-permute-start.17 = (bf16[128,512]{1,0:T(8,128)(2,1)S(1)}, bf16[128,512]{1,0:T(8,128)(2,1)S(1)}, u32[]{:S(2)}, u32[]{:S(2)}) collective-permute-start(bf16[128,512]{1,0:T(8,128)(2,1)S(1)} %add_convert_fusion.3), channel_id=1, source_target_pairs={{0,16},{4,20},{8,24},{12,28},{16,0},{20,4},{24,8},{28,12},{1,17},{... | collective-permute-start | bytes 393224 | tf_op jit(solution)/shard_map/ppermute | solution.py:29
  64.8 1.4 %collective-permute-start.18 = (bf16[128,512]{1,0:T(8,128)(2,1)S(1)}, bf16[128,512]{1,0:T(8,128)(2,1)S(1)}, u32[]{:S(2)}, u32[]{:S(2)}) collective-permute-start(bf16[128,512]{1,0:T(8,128)(2,1)S(1)} %add_convert_fusion.2.own_ref), channel_id=1, source_target_pairs={{0,4},{4,0},{8,12},{12,8},{16,20},{20,16},{24,28},{28,24},{1,5},{5... | collective-permute-start | bytes 393224 | tf_op jit(solution)/shard_map/ppermute | solution.py:29
  64.9 18.6 %collective-permute-start.24 = (bf16[1024,256]{1,0:T(8,128)(2,1)S(1)}, bf16[1024,256]{1,0:T(8,128)(2,1)S(1)}, u32[]{:S(2)}, u32[]{:S(2)}) collective-permute-start(bf16[1024,256]{1,0:T(8,128)(2,1)S(1)} %collective-permute-done.11.refs_4_.refs_0_), channel_id=1, source_target_pairs={{1,0},{2,3},{5,4},{6,7},{9,8},{10,11},{13,12},{14,15},{17,16},{18,... | collective-permute-start | bytes 1572872 | tf_op jit(solution)/shard_map/ppermute | solution.py:289
  68.6 1.6 %collective-permute-start.19 = (bf16[128,768]{1,0:T(8,128)(2,1)S(1)}, bf16[128,768]{1,0:T(8,128)(2,1)S(1)}, u32[]{:S(2)}, u32[]{:S(2)}) collective-permute-start(bf16[128,768]{1,0:T(8,128)(2,1)S(1)} %get-tuple-element.42), channel_id=1, source_target_pairs={{0,4},{4,0},{8,12},{12,8},{16,20},{20,16},{24,28},{28,24},{1,5},{5... | collective-permute-start | bytes 589832 | tf_op jit(solution)/shard_map/ppermute | solution.py:29
  70.2 13.7 %collective-permute-start.20 = (bf16[128,768]{1,0:T(8,128)(2,1)S(1)}, bf16[128,768]{1,0:T(8,128)(2,1)S(1)}, u32[]{:S(2)}, u32[]{:S(2)}) collective-permute-start(bf16[128,768]{1,0:T(8,128)(2,1)S(1)} %add_convert_fusion.1), channel_id=1, source_target_pairs={{0,24},{4,28},{8,16},{12,20},{16,8},{20,12},{24,0},{28,4},{1,25},{... | collective-permute-start | bytes 589832 | tf_op jit(solution)/shard_map/ppermute | solution.py:29
  72.7 11.3 %collective-permute-start.21 = (bf16[128,768]{1,0:T(8,128)(2,1)S(1)}, bf16[128,768]{1,0:T(8,128)(2,1)S(1)}, u32[]{:S(2)}, u32[]{:S(2)}) collective-permute-start(bf16[128,768]{1,0:T(8,128)(2,1)S(1)} %add_convert_fusion.1), channel_id=1, source_target_pairs={{0,8},{4,12},{8,0},{12,4},{16,24},{20,28},{24,16},{28,20},{1,9},{5... | collective-permute-start | bytes 589832 | tf_op jit(solution)/shard_map/ppermute | solution.py:29
  73.2 10.8 %collective-permute-start.22 = (bf16[128,768]{1,0:T(8,128)(2,1)S(1)}, bf16[128,768]{1,0:T(8,128)(2,1)S(1)}, u32[]{:S(2)}, u32[]{:S(2)}) collective-permute-start(bf16[128,768]{1,0:T(8,128)(2,1)S(1)} %add_convert_fusion.1), channel_id=1, source_target_pairs={{0,16},{4,20},{8,24},{12,28},{16,0},{20,4},{24,8},{28,12},{1,17},{... | collective-permute-start | bytes 589832 | tf_op jit(solution)/shard_map/ppermute | solution.py:29
  83.9 1.3 %collective-permute-start.25 = (bf16[128,256]{1,0:T(8,128)(2,1)S(1)}, bf16[128,256]{1,0:T(8,128)(2,1)S(1)}, u32[]{:S(2)}, u32[]{:S(2)}) collective-permute-start(bf16[128,256]{1,0:T(8,128)(2,1)S(1)} %get-tuple-element.46), channel_id=1, source_target_pairs={{0,4},{4,0},{8,12},{12,8},{16,20},{20,16},{24,28},{28,24},{1,5},{5... | collective-permute-start | bytes 196616 | tf_op jit(solution)/shard_map/ppermute | solution.py:29
  84.1 4.7 %collective-permute-start.23 = (bf16[128,768]{1,0:T(8,128)(2,1)S(1)}, bf16[128,768]{1,0:T(8,128)(2,1)S(1)}, u32[]{:S(2)}, u32[]{:S(2)}) collective-permute-start(bf16[128,768]{1,0:T(8,128)(2,1)S(1)} %add_convert_fusion.refs_0_), channel_id=1, source_target_pairs={{0,4},{4,0},{8,12},{12,8},{16,20},{20,16},{24,28},{28,24},{1,5},{5... | collective-permute-start | bytes 589832 | tf_op jit(solution)/shard_map/ppermute | solution.py:29
  85.2 7.1 %collective-permute-start.26 = (bf16[128,256]{1,0:T(8,128)(2,1)S(1)}, bf16[128,256]{1,0:T(8,128)(2,1)S(1)}, u32[]{:S(2)}, u32[]{:S(2)}) collective-permute-start(bf16[128,256]{1,0:T(8,128)(2,1)S(1)} %add_convert_fusion.7), channel_id=1, source_target_pairs={{0,24},{4,28},{8,16},{12,20},{16,8},{20,12},{24,0},{28,4},{1,25},{... | collective-permute-start | bytes 196616 | tf_op jit(solution)/shard_map/ppermute | solution.py:29
  87.6 4.7 %collective-permute-start.27 = (bf16[128,256]{1,0:T(8,128)(2,1)S(1)}, bf16[128,256]{1,0:T(8,128)(2,1)S(1)}, u32[]{:S(2)}, u32[]{:S(2)}) collective-permute-start(bf16[128,256]{1,0:T(8,128)(2,1)S(1)} %add_convert_fusion.7), channel_id=1, source_target_pairs={{0,8},{4,12},{8,0},{12,4},{16,24},{20,28},{24,16},{28,20},{1,9},{5... | collective-permute-start | bytes 196616 | tf_op jit(solution)/shard_map/ppermute | solution.py:29
  88.2 4.3 %collective-permute-start.28 = (bf16[128,256]{1,0:T(8,128)(2,1)S(1)}, bf16[128,256]{1,0:T(8,128)(2,1)S(1)}, u32[]{:S(2)}, u32[]{:S(2)}) collective-permute-start(bf16[128,256]{1,0:T(8,128)(2,1)S(1)} %add_convert_fusion.7), channel_id=1, source_target_pairs={{0,16},{4,20},{8,24},{12,28},{16,0},{20,4},{24,8},{28,12},{1,17},{... | collective-permute-start | bytes 196616 | tf_op jit(solution)/shard_map/ppermute | solution.py:29
  92.5 1.3 %collective-permute-start.29 = (bf16[128,256]{1,0:T(8,128)(2,1)S(1)}, bf16[128,256]{1,0:T(8,128)(2,1)S(1)}, u32[]{:S(2)}, u32[]{:S(2)}) collective-permute-start(bf16[128,256]{1,0:T(8,128)(2,1)S(1)} %add_convert_fusion.6.own_ref), channel_id=1, source_target_pairs={{0,4},{4,0},{8,12},{12,8},{16,20},{20,16},{24,28},{28,24},{1,5},{5... | collective-permute-start | bytes 196616 | tf_op jit(solution)/shard_map/ppermute | solution.py:29

commit v6 on v5

--- a/solution.py
+++ b/solution.py
@@ -224,7 +224,7 @@
     return call(kernel, [rest, across, *coeffs], [(rest.shape, BF16)], scratch, 2 * rows * more * columns)[0]
 
 
-def coeff(current, parts):
+def coeff(current, parts, weight):
     columns, rows = current.shape
     size = sum(part.width for part in parts)
     arrays = [x for part in parts for x in part.arrays]
@@ -240,7 +240,7 @@
         ],
         compiler_params=pltpu.CompilerParams(vmem_limit_bytes=VMEM),
         cost_estimate=pl.CostEstimate(
-            flops=WEIGHT * 2 * size * columns * rows, bytes_accessed=WEIGHT * 2 * rows * size, transcendentals=0
+            flops=weight * 2 * size * columns * rows, bytes_accessed=weight * 2 * rows * size, transcendentals=0
         ),
     )(current, *arrays)
 
@@ -249,7 +249,7 @@
 PIECES = {'O': 1, 'F3': 1}
 JOINED = 'swap'
 WHOLE = ()
-WEIGHT = 16
+WEIGHT = {'1.0': 64, '1.1': 1, '0.0': 16, '0.1': 16}
 DIRECT = ('0.0', '0.1', '0.2', '1.0', '1.1', '1.2')
 SKIP = ('E3',)
 GATES = {
@@ -345,7 +345,7 @@
             return finish(p == 0, self.gated(name, rest), across, coeffs)
         k = int(name[3:])
         if step == "a":
-            return coeff(self.gated(name, self("U1" if p == 0 else "X")), groups[k])
+            return coeff(self.gated(name, self("U1" if p == 0 else "X")), groups[k], WEIGHT[name[1:]])
         if step == "b":
             mine, other = self("a" + name[1:])
             got = self.gated(name, swap(other, 1, self.m))

time: 95.8 us -> 94.8 us (0.990)
  waiting for transfers between devices: 46.1 us -> 44.1 us
  Pallas kernels: 13.9 us -> 15.2 us
    ppermute x10, waiting for transfers between devices: 35 us -> 32.8 us  [send(): return lax.ppermute(self.gated(name, x), 'vecs', pairs)]
  transfers between devices with their start and end apart: 30 -> 30, of which waited for: 13 -> 14; matrix products, arithmetic and copies ran while one was open for 2% -> 2% of each run, Pallas kernels for 13% -> 15%
where the time goes in v6:
time: 94.8 us; the launch traced here: 94.3 us
  waiting for transfers between devices  44.1 us (47%)
  starting transfers between devices  31.8 us (34%)
  Pallas kernels  15.2 us (16%)
  local copies, waits for them, and re-layouts  2.52 us (3%)
    ppermute x10, waiting for transfers between devices, send(): return lax.ppermute(self.gated(name, x), 'vecs', pairs)  32.8 us
    ppermute x20, starting transfers between devices, swap(): return lax.ppermute(x, 'rows', [(i, i ^ bit) for i in range(m)])  16.4 us
    ppermute x10, starting transfers between devices, send(): return lax.ppermute(self.gated(name, x), 'vecs', pairs)  15.4 us
    ppermute x20, waiting for transfers between devices, swap(): return lax.ppermute(x, 'rows', [(i, i ^ bit) for i in range(m)])  11.2 us
    pallas_call x6, Pallas kernels, call(): pl.pallas_call(kernel, in_specs=[ANY] * len(inputs), out_specs=[IN_VMEM]...  10.7 us
    pallas_call x4, Pallas kernels, coeff(): pl.pallas_call(functools.partial(coeff_kernel, parts), in_specs=[ANY] * (...  4.48 us
  transfers between devices with their start and end apart: 30, of which 14 were waited for; matrix products, arithmetic and copies ran while one was open for 2% of the time, Pallas kernels for 15%

profile of v6, /device:TPU:0, one launch (start us, length us, event | category | flops | bytes accessed | tf_op | source)
XLA Modules:
  0.0 94.3 jit_solution(15336456846730365737)
XLA Ops:
  0.0 1.3 %slice_bitcast_fusion = (bf16[1024,256]{1,0:T(8,128)(2,1)S(1)}, bf16[1024,256]{1,0:T(8,128)(2,1)S(1)}) fusion(bf16[2,1024,256]{2,1,0:T(8,128)(2,1)} %param.4), kind=kLoop, calls=%fused_computation | loop fusion | bytes 2097152 | tf_op jit(solution)/shard_map/squeeze | solution.py:304
  1.3 3.1 %collective-permute-start = (bf16[1024,256]{1,0:T(8,128)(2,1)S(1)}, bf16[1024,256]{1,0:T(8,128)(2,1)}, u32[]{:S(2)}, u32[]{:S(2)}) collective-permute-start(bf16[1024,256]{1,0:T(8,128)(2,1)S(1)} %get-tuple-element.52.refs_0_), channel_id=1, source_target_pairs={{0,1},{1,0},{2,3},{3,2},{4,5},{5,4},{6,7},{7,6},{8,9},{9,8},{10,11... | collective-permute-start | bytes 1572872 | tf_op jit(solution)/shard_map/ppermute | solution.py:289
  4.4 0.7 collective-permute-start.7
  5.1 4.4 %collective-permute-start.5 = (bf16[1024,256]{1,0:T(8,128)(2,1)S(1)}, bf16[1024,256]{1,0:T(8,128)(2,1)S(1)}, u32[]{:S(2)}, u32[]{:S(2)}) collective-permute-start(bf16[1024,256]{1,0:T(8,128)(2,1)S(1)} %get-tuple-element.51.refs_0_), channel_id=1, source_target_pairs={{0,1},{1,0},{2,3},{3,2},{4,5},{5,4},{6,7},{7,6},{8,9},{9,8},{10,11... | collective-permute-start | bytes 1572872 | tf_op jit(solution)/shard_map/ppermute | solution.py:289
  9.5 0.7 collective-permute-start.14
  10.2 1.2 %copy.4 = bf16[1024,256]{0,1:T(8,128)(2,1)S(1)} copy(bf16[1024,256]{1,0:T(8,128)(2,1)} %param.3) | data formatting | bytes 1048576 | tf_op jit(solution)/shard_map/optimization_barrier | solution.py:17
  11.4 5.8 %collective-permute-done.refs_1_ = bf16[1024,256]{1,0:T(8,128)(2,1)} collective-permute-done((bf16[1024,256]{1,0:T(8,128)(2,1)S(1)}, bf16[1024,256]{1,0:T(8,128)(2,1)}, u32[]{:S(2)}, u32[]{:S(2)}) %collective-permute-start) | collective-permute-done | bytes 524320 | tf_op jit(solution)/shard_map/ppermute | solution.py:289
  17.2 1.7 %shard_map.37 = (bf16[128,512]{1,0:T(8,128)(2,1)S(1)}, bf16[128,512]{1,0:T(8,128)(2,1)S(1)}) custom-call(bf16[256,1024]{1,0:T(8,128)(2,1)S(1)} %bitcast.5, bf16[1024,256]{1,0:T(8,128)(2,1)S(1)} %get-tuple-element.52.refs_0_, bf16[1024,256]{1,0:T(8,128)(2,1)} %collective-permute-done.refs_1_), custom_call_target="tpu_custom_call" | custom-call | flops 17179869184 | bytes 67108864 | tf_op jit(solution)/shard_map/pallas_call | solution.py:231
  19.0 1.3 %collective-permute-start.10 = (bf16[1024,256]{1,0:T(8,128)(2,1)}, bf16[1024,256]{1,0:T(8,128)(2,1)S(1)}, u32[]{:S(2)}, u32[]{:S(2)}) collective-permute-start(bf16[1024,256]{1,0:T(8,128)(2,1)} %collective-permute-done.refs_1_), channel_id=1, source_target_pairs={{2,0},{1,3},{6,4},{5,7},{10,8},{9,11},{14,12},{13,15},{18,16},{17,... | collective-permute-start | bytes 1572872 | tf_op jit(solution)/shard_map/ppermute | solution.py:289
  20.3 0.7 collective-permute-start.9
  21.0 1.3 %collective-permute-start.8 = (bf16[1024,256]{1,0:T(8,128)(2,1)S(1)}, bf16[1024,256]{1,0:T(8,128)(2,1)S(1)}, u32[]{:S(2)}, u32[]{:S(2)}) collective-permute-start(bf16[1024,256]{1,0:T(8,128)(2,1)S(1)} %collective-permute-done.7.refs_2_.refs_0_), channel_id=1, source_target_pairs={{1,0},{2,3},{5,4},{6,7},{9,8},{10,11},{13,12},{14,15},{17,16},{18,... | collective-permute-start | bytes 1572872 | tf_op jit(solution)/shard_map/ppermute | solution.py:289
  22.4 5.1 %collective-permute-done.5.refs_1_ = bf16[1024,256]{1,0:T(8,128)(2,1)S(1)} collective-permute-done((bf16[1024,256]{1,0:T(8,128)(2,1)S(1)}, bf16[1024,256]{1,0:T(8,128)(2,1)S(1)}, u32[]{:S(2)}, u32[]{:S(2)}) %collective-permute-start.5) | collective-permute-done | bytes 524320 | tf_op jit(solution)/shard_map/ppermute | solution.py:289
  27.5 2.6 %collective-permute-start.2 = (bf16[128,512]{1,0:T(8,128)(2,1)S(1)}, bf16[128,512]{1,0:T(8,128)(2,1)S(1)}, u32[]{:S(2)}, u32[]{:S(2)}) collective-permute-start(bf16[128,512]{1,0:T(8,128)(2,1)S(1)} %add_convert_fusion.5), channel_id=1, source_target_pairs={{0,24},{4,28},{8,16},{12,20},{16,8},{20,12},{24,0},{28,4},{1,25},{... | collective-permute-start | bytes 393224 | tf_op jit(solution)/shard_map/ppermute | solution.py:29
  30.1 0.5 collective-permute-start.3
  30.7 3.9 %collective-permute-done.2 = bf16[128,512]{1,0:T(8,128)(2,1)S(1)} collective-permute-done((bf16[128,512]{1,0:T(8,128)(2,1)S(1)}, bf16[128,512]{1,0:T(8,128)(2,1)S(1)}, u32[]{:S(2)}, u32[]{:S(2)}) %collective-permute-start.2) | collective-permute-done | bytes 131104 | tf_op jit(solution)/shard_map/ppermute | solution.py:29
  34.6 1.3 %collective-permute-start.4 = (bf16[128,512]{1,0:T(8,128)(2,1)S(1)}, bf16[128,512]{1,0:T(8,128)(2,1)S(1)}, u32[]{:S(2)}, u32[]{:S(2)}) collective-permute-start(bf16[128,512]{1,0:T(8,128)(2,1)S(1)} %add_convert_fusion.5), channel_id=1, source_target_pairs={{0,16},{4,20},{8,24},{12,28},{16,0},{20,4},{24,8},{28,12},{1,17},{... | collective-permute-start | bytes 393224 | tf_op jit(solution)/shard_map/ppermute | solution.py:29
  35.9 1.3 %collective-permute-start.15 = (bf16[1024,256]{1,0:T(8,128)(2,1)S(1)}, bf16[1024,256]{1,0:T(8,128)(2,1)S(1)}, u32[]{:S(2)}, u32[]{:S(2)}) collective-permute-start(bf16[1024,256]{1,0:T(8,128)(2,1)S(1)} %collective-permute-done.14.refs_2_), channel_id=1, source_target_pairs={{1,0},{2,3},{5,4},{6,7},{9,8},{10,11},{13,12},{14,15},{17,16},{18,... | collective-permute-start | bytes 1572872 | tf_op jit(solution)/shard_map/ppermute | solution.py:289
  37.2 2.4 %collective-permute-done.4 = bf16[128,512]{1,0:T(8,128)(2,1)S(1)} collective-permute-done((bf16[128,512]{1,0:T(8,128)(2,1)S(1)}, bf16[128,512]{1,0:T(8,128)(2,1)S(1)}, u32[]{:S(2)}, u32[]{:S(2)}) %collective-permute-start.4) | collective-permute-done | bytes 131104 | tf_op jit(solution)/shard_map/ppermute | solution.py:29
  39.6 0.7 collective-permute-start.11
  40.3 3.8 %collective-permute-done.10.refs_5_.refs_3_ = bf16[1024,256]{1,0:T(8,128)(2,1)S(1)} collective-permute-done((bf16[1024,256]{1,0:T(8,128)(2,1)}, bf16[1024,256]{1,0:T(8,128)(2,1)S(1)}, u32[]{:S(2)}, u32[]{:S(2)}) %collective-permute-start.10) | collective-permute-done | bytes 524320 | tf_op jit(solution)/shard_map/ppermute | solution.py:289
  44.2 8.6 %collective-permute-done.8.refs_3_.refs_1_ = bf16[1024,256]{1,0:T(8,128)(2,1)S(1)} collective-permute-done((bf16[1024,256]{1,0:T(8,128)(2,1)S(1)}, bf16[1024,256]{1,0:T(8,128)(2,1)S(1)}, u32[]{:S(2)}, u32[]{:S(2)}) %collective-permute-start.8) | collective-permute-done | bytes 524320 | tf_op jit(solution)/shard_map/ppermute | solution.py:289
  52.8 1.0 %shard_map.40 = (bf16[128,512]{1,0:T(8,128)(2,1)S(1)}, bf16[128,512]{1,0:T(8,128)(2,1)S(1)}) custom-call(bf16[256,1024]{1,0:T(8,128)(2,1)S(1)} %bitcast.6, bf16[1024,256]{1,0:T(8,128)(2,1)S(1)} %collective-permute-done.7.refs_2_.refs_0_, bf16[1024,256]{1,0:T(8,128)(2,1)S(1)} %collective-permute-done.8.refs_3_.refs_1_, ...), custom_call_target="tpu_custom_call" | custom-call | flops 268435456 | bytes 1048576 | tf_op jit(solution)/shard_map/pallas_call | solution.py:231
  53.9 1.6 %shard_map.38.scaled_ref = bf16[1024,256]{1,0:T(8,128)(2,1)S(1)} custom-call(bf16[2,1024,1024]{2,1,0:T(8,128)(2,1)S(1)} %copy-done, bf16[128,512]{1,0:T(8,128)(2,1)S(1)} %add_convert_fusion.4.refs_0_, bf16[128,512]{1,0:T(8,128)(2,1)S(1)} %collective-permute-done.6.refs_1_), custom_call_target="tpu_custom_call" | custom-call | flops 268435456 | bytes 4456448 | tf_op jit(solution)/shard_map/pallas_call | solution.py:167
  55.6 2.5 %collective-permute-start.13 = (bf16[128,512]{1,0:T(8,128)(2,1)S(1)}, bf16[128,512]{1,0:T(8,128)(2,1)S(1)}, u32[]{:S(2)}, u32[]{:S(2)}) collective-permute-start(bf16[128,512]{1,0:T(8,128)(2,1)S(1)} %add_convert_fusion.3), channel_id=1, source_target_pairs={{0,24},{4,28},{8,16},{12,20},{16,8},{20,12},{24,0},{28,4},{1,25},{... | collective-permute-start | bytes 393224 | tf_op jit(solution)/shard_map/ppermute | solution.py:29
  58.1 0.5 collective-permute-start.16
  58.6 0.5 collective-permute-start.17
  59.1 3.1 %shard_map.39 = (f32[256,1024]{1,0:T(8,128)S(1)}, bf16[1024,512]{1,0:T(8,128)(2,1)S(1)}) custom-call(bf16[2,1024,1024]{2,1,0:T(8,128)(2,1)S(1)} %copy-done, bf16[256,1024]{1,0:T(8,128)(2,1)S(1)} %bitcast.7, bf16[1024,256]{1,0:T(8,128)(2,1)S(1)} %shard_map.38.scaled_ref, bf16[1024,256]{1,0:T(8,128)(2,1)S(1)} %get-tuple-element.52.refs_0_, ...), custom_call_target="tpu_custom_call" | custom-call | flops 1610612736 | bytes 8388608 | tf_op jit(solution)/shard_map/pallas_call | solution.py:167
  62.2 1.4 %collective-permute-done.15.refs_3_ = bf16[1024,256]{1,0:T(8,128)(2,1)S(1)} collective-permute-done((bf16[1024,256]{1,0:T(8,128)(2,1)S(1)}, bf16[1024,256]{1,0:T(8,128)(2,1)S(1)}, u32[]{:S(2)}, u32[]{:S(2)}) %collective-permute-start.15) | collective-permute-done | bytes 524320 | tf_op jit(solution)/shard_map/ppermute | solution.py:289
  63.6 1.7 %collective-permute-done.16 = bf16[128,512]{1,0:T(8,128)(2,1)S(1)} collective-permute-done((bf16[128,512]{1,0:T(8,128)(2,1)S(1)}, bf16[128,512]{1,0:T(8,128)(2,1)S(1)}, u32[]{:S(2)}, u32[]{:S(2)}) %collective-permute-start.16) | collective-permute-done | bytes 131104 | tf_op jit(solution)/shard_map/ppermute | solution.py:29
  65.5 1.3 %collective-permute-start.24 = (bf16[1024,256]{1,0:T(8,128)(2,1)S(1)}, bf16[1024,256]{1,0:T(8,128)(2,1)S(1)}, u32[]{:S(2)}, u32[]{:S(2)}) collective-permute-start(bf16[1024,256]{1,0:T(8,128)(2,1)S(1)} %collective-permute-done.11.refs_4_.refs_0_), channel_id=1, source_target_pairs={{1,0},{2,3},{5,4},{6,7},{9,8},{10,11},{13,12},{14,15},{17,16},{18,... | collective-permute-start | bytes 1572872 | tf_op jit(solution)/shard_map/ppermute | solution.py:289
  66.8 1.0 %shard_map.41.current_ref = bf16[256,1024]{1,0:T(8,128)(2,1)S(1)} custom-call(f32[256,1024]{1,0:T(8,128)S(1)} %get-tuple-element.33.rest_ref, bf16[1024,512]{1,0:T(8,128)(2,1)S(1)} %get-tuple-element.34.across_ref, bf16[128,512]{1,0:T(8,128)(2,1)S(1)} %add_convert_fusion.2.own_ref, bf16[128,512]{1,0:T(8,128)(2,1)S(1)} %collective-permute-done.18.other_ref), custom_call_target="tpu_custom_call" | custom-call | flops 268435456 | bytes 2359296 | tf_op jit(solution)/shard_map/pallas_call | solution.py:167
  67.8 1.4 %shard_map.42 = (bf16[128,768]{1,0:T(8,128)(2,1)S(1)}, bf16[128,768]{1,0:T(8,128)(2,1)S(1)}) custom-call(bf16[256,1024]{1,0:T(8,128)(2,1)S(1)} %shard_map.41.current_ref, bf16[1024,256]{1,0:T(8,128)(2,1)S(1)} %get-tuple-element.51.refs_0_, bf16[1024,256]{1,0:T(8,128)(2,1)S(1)} %collective-permute-done.5.refs_1_, ...), custom_call_target="tpu_custom_call" | custom-call | flops 6442450944 | bytes 25165824 | tf_op jit(solution)/shard_map/pallas_call | solution.py:231
  69.2 0.5 collective-permute-start.19
  69.7 1.1 %collective-permute-done.19 = bf16[128,768]{1,0:T(8,128)(2,1)S(1)} collective-permute-done((bf16[128,768]{1,0:T(8,128)(2,1)S(1)}, bf16[128,768]{1,0:T(8,128)(2,1)S(1)}, u32[]{:S(2)}, u32[]{:S(2)}) %collective-permute-start.19) | collective-permute-done | bytes 196640 | tf_op jit(solution)/shard_map/ppermute | solution.py:29
  70.8 2.4 %collective-permute-start.20 = (bf16[128,768]{1,0:T(8,128)(2,1)S(1)}, bf16[128,768]{1,0:T(8,128)(2,1)S(1)}, u32[]{:S(2)}, u32[]{:S(2)}) collective-permute-start(bf16[128,768]{1,0:T(8,128)(2,1)S(1)} %add_convert_fusion.1), channel_id=1, source_target_pairs={{0,24},{4,28},{8,16},{12,20},{16,8},{20,12},{24,0},{28,4},{1,25},{... | collective-permute-start | bytes 589832 | tf_op jit(solution)/shard_map/ppermute | solution.py:29
  73.3 0.5 collective-permute-start.21
  73.8 0.6 collective-permute-start.22
  74.4 8.1 %collective-permute-done.24.refs_5_.refs_1_ = bf16[1024,256]{1,0:T(8,128)(2,1)S(1)} collective-permute-done((bf16[1024,256]{1,0:T(8,128)(2,1)S(1)}, bf16[1024,256]{1,0:T(8,128)(2,1)S(1)}, u32[]{:S(2)}, u32[]{:S(2)}) %collective-permute-start.24) | collective-permute-done | bytes 524320 | tf_op jit(solution)/shard_map/ppermute | solution.py:289
  82.5 0.4 shard_map.45
  83.3 0.4 collective-permute-start.23
  83.7 0.6 collective-permute-done.25
  84.3 2.4 %collective-permute-start.26 = (bf16[128,256]{1,0:T(8,128)(2,1)S(1)}, bf16[128,256]{1,0:T(8,128)(2,1)S(1)}, u32[]{:S(2)}, u32[]{:S(2)}) collective-permute-start(bf16[128,256]{1,0:T(8,128)(2,1)S(1)} %add_convert_fusion.7), channel_id=1, source_target_pairs={{0,24},{4,28},{8,16},{12,20},{16,8},{20,12},{24,0},{28,4},{1,25},{... | collective-permute-start | bytes 196616 | tf_op jit(solution)/shard_map/ppermute | solution.py:29
  86.7 0.5 collective-permute-start.27
  87.2 0.6 collective-permute-start.28
  87.8 1.7 %shard_map.43.scaled_ref = bf16[1024,256]{1,0:T(8,128)(2,1)S(1)} custom-call(bf16[2,1024,1024]{2,1,0:T(8,128)(2,1)S(1)} %copy-done, bf16[128,768]{1,0:T(8,128)(2,1)S(1)} %add_convert_fusion.refs_0_, bf16[128,768]{1,0:T(8,128)(2,1)S(1)} %collective-permute-done.23.refs_1_), custom_call_target="tpu_custom_call" | custom-call | flops 268435456 | bytes 4587520 | tf_op jit(solution)/shard_map/pallas_call | solution.py:167
  89.5 1.9 %shard_map.44 = (f32[1024,256]{1,0:T(8,128)S(1)}, bf16[1024,256]{1,0:T(8,128)(2,1)S(1)}) custom-call(bf16[2,1024,1024]{2,1,0:T(8,128)(2,1)S(1)} %copy-done, bf16[256,1024]{1,0:T(8,128)(2,1)S(1)} %shard_map.41.current_ref, bf16[1024,256]{1,0:T(8,128)(2,1)S(1)} %shard_map.43.scaled_ref, bf16[1024,256]{1,0:T(8,128)(2,1)S(1)} %get-tuple-element.51.refs_0_, ...), custom_call_target="tpu_custom_call" | custom-call | flops 1073741824 | bytes 8388608 | tf_op jit(solution)/shard_map/pallas_call | solution.py:167
  91.6 1.2 %collective-permute-done.29.other_ref = bf16[128,256]{1,0:T(8,128)(2,1)S(1)} collective-permute-done((bf16[128,256]{1,0:T(8,128)(2,1)S(1)}, bf16[128,256]{1,0:T(8,128)(2,1)S(1)}, u32[]{:S(2)}, u32[]{:S(2)}) %collective-permute-start.29) | collective-permute-done | bytes 65568 | tf_op jit(solution)/shard_map/ppermute | solution.py:29
  92.8 1.5 %shard_map.46 = bf16[1024,256]{1,0:T(8,128)(2,1)} custom-call(f32[1024,256]{1,0:T(8,128)S(1)} %get-tuple-element.43.rest_ref, bf16[1024,256]{1,0:T(8,128)(2,1)S(1)} %get-tuple-element.44.across_ref, bf16[128,256]{1,0:T(8,128)(2,1)S(1)} %add_convert_fusion.6.own_ref, bf16[128,256]{1,0:T(8,128)(2,1)S(1)} %collective-permute-done.29.other_ref), custom_call_target="tpu_custom_call" | custom-call | flops 134217728 | bytes 1703936 | tf_op jit(solution)/shard_map/pallas_call | solution.py:167
  (34 shorter events, 1.1 us)
Async XLA Ops:
  1.3 15.9 %collective-permute-start = (bf16[1024,256]{1,0:T(8,128)(2,1)S(1)}, bf16[1024,256]{1,0:T(8,128)(2,1)}, u32[]{:S(2)}, u32[]{:S(2)}) collective-permute-start(bf16[1024,256]{1,0:T(8,128)(2,1)S(1)} %get-tuple-element.52.refs_0_), channel_id=1, source_target_pairs={{0,1},{1,0},{2,3},{3,2},{4,5},{5,4},{6,7},{7,6},{8,9},{9,8},{10,11... | collective-permute-start | bytes 1572872 | tf_op jit(solution)/shard_map/ppermute | solution.py:289
  4.4 16.0 %collective-permute-start.7 = (bf16[1024,256]{1,0:T(8,128)(2,1)S(1)}, bf16[1024,256]{1,0:T(8,128)(2,1)S(1)}, u32[]{:S(2)}, u32[]{:S(2)}) collective-permute-start(bf16[1024,256]{1,0:T(8,128)(2,1)S(1)} %get-tuple-element.52.refs_0_), channel_id=1, source_target_pairs={{1,2},{2,1},{5,6},{6,5},{9,10},{10,9},{13,14},{14,13},{17,18},{18,... | collective-permute-start | bytes 1572872 | tf_op jit(solution)/shard_map/ppermute | solution.py:289
  5.1 22.5 %collective-permute-start.5 = (bf16[1024,256]{1,0:T(8,128)(2,1)S(1)}, bf16[1024,256]{1,0:T(8,128)(2,1)S(1)}, u32[]{:S(2)}, u32[]{:S(2)}) collective-permute-start(bf16[1024,256]{1,0:T(8,128)(2,1)S(1)} %get-tuple-element.51.refs_0_), channel_id=1, source_target_pairs={{0,1},{1,0},{2,3},{3,2},{4,5},{5,4},{6,7},{7,6},{8,9},{9,8},{10,11... | collective-permute-start | bytes 1572872 | tf_op jit(solution)/shard_map/ppermute | solution.py:289
  9.5 20.6 %collective-permute-start.14 = (bf16[1024,256]{1,0:T(8,128)(2,1)S(1)}, bf16[1024,256]{1,0:T(8,128)(2,1)S(1)}, u32[]{:S(2)}, u32[]{:S(2)}) collective-permute-start(bf16[1024,256]{1,0:T(8,128)(2,1)S(1)} %get-tuple-element.51.refs_0_), channel_id=1, source_target_pairs={{1,2},{2,1},{5,6},{6,5},{9,10},{10,9},{13,14},{14,13},{17,18},{18,... | collective-permute-start | bytes 1572872 | tf_op jit(solution)/shard_map/ppermute | solution.py:289
  17.2 36.6 %copy-start = (bf16[2,1024,1024]{2,1,0:T(8,128)(2,1)S(1)}, bf16[2,1024,1024]{2,1,0:T(8,128)(2,1)}, u32[]{:S(2)}) copy-start(bf16[2,1024,1024]{2,1,0:T(8,128)(2,1)} %factors_ref.7) | copy-start | bytes 12582916
  18.9 2.1 %collective-permute-start.1 = (bf16[128,512]{1,0:T(8,128)(2,1)S(1)}, bf16[128,512]{1,0:T(8,128)(2,1)S(1)}, u32[]{:S(2)}, u32[]{:S(2)}) collective-permute-start(bf16[128,512]{1,0:T(8,128)(2,1)S(1)} %get-tuple-element.30), channel_id=1, source_target_pairs={{0,4},{4,0},{8,12},{12,8},{16,20},{20,16},{24,28},{28,24},{1,5},{5... | collective-permute-start | bytes 393224 | tf_op jit(solution)/shard_map/ppermute | solution.py:29
  19.0 25.1 %collective-permute-start.10 = (bf16[1024,256]{1,0:T(8,128)(2,1)}, bf16[1024,256]{1,0:T(8,128)(2,1)S(1)}, u32[]{:S(2)}, u32[]{:S(2)}) collective-permute-start(bf16[1024,256]{1,0:T(8,128)(2,1)} %collective-permute-done.refs_1_), channel_id=1, source_target_pairs={{2,0},{1,3},{6,4},{5,7},{10,8},{9,11},{14,12},{13,15},{18,16},{17,... | collective-permute-start | bytes 1572872 | tf_op jit(solution)/shard_map/ppermute | solution.py:289
  20.3 23.8 %collective-permute-start.9 = (bf16[1024,256]{1,0:T(8,128)(2,1)}, bf16[1024,256]{1,0:T(8,128)(2,1)S(1)}, u32[]{:S(2)}, u32[]{:S(2)}) collective-permute-start(bf16[1024,256]{1,0:T(8,128)(2,1)} %collective-permute-done.refs_1_), channel_id=1, source_target_pairs={{1,2},{2,1},{5,6},{6,5},{9,10},{10,9},{13,14},{14,13},{17,18},{18,... | collective-permute-start | bytes 1572872 | tf_op jit(solution)/shard_map/ppermute | solution.py:289
  21.0 31.7 %collective-permute-start.8 = (bf16[1024,256]{1,0:T(8,128)(2,1)S(1)}, bf16[1024,256]{1,0:T(8,128)(2,1)S(1)}, u32[]{:S(2)}, u32[]{:S(2)}) collective-permute-start(bf16[1024,256]{1,0:T(8,128)(2,1)S(1)} %collective-permute-done.7.refs_2_.refs_0_), channel_id=1, source_target_pairs={{1,0},{2,3},{5,4},{6,7},{9,8},{10,11},{13,12},{14,15},{17,16},{18,... | collective-permute-start | bytes 1572872 | tf_op jit(solution)/shard_map/ppermute | solution.py:289
  27.5 7.1 %collective-permute-start.2 = (bf16[128,512]{1,0:T(8,128)(2,1)S(1)}, bf16[128,512]{1,0:T(8,128)(2,1)S(1)}, u32[]{:S(2)}, u32[]{:S(2)}) collective-permute-start(bf16[128,512]{1,0:T(8,128)(2,1)S(1)} %add_convert_fusion.5), channel_id=1, source_target_pairs={{0,24},{4,28},{8,16},{12,20},{16,8},{20,12},{24,0},{28,4},{1,25},{... | collective-permute-start | bytes 393224 | tf_op jit(solution)/shard_map/ppermute | solution.py:29
  30.1 5.8 %collective-permute-start.3 = (bf16[128,512]{1,0:T(8,128)(2,1)S(1)}, bf16[128,512]{1,0:T(8,128)(2,1)S(1)}, u32[]{:S(2)}, u32[]{:S(2)}) collective-permute-start(bf16[128,512]{1,0:T(8,128)(2,1)S(1)} %add_convert_fusion.5), channel_id=1, source_target_pairs={{0,8},{4,12},{8,0},{12,4},{16,24},{20,28},{24,16},{28,20},{1,9},{5... | collective-permute-start | bytes 393224 | tf_op jit(solution)/shard_map/ppermute | solution.py:29
  34.6 5.0 %collective-permute-start.4 = (bf16[128,512]{1,0:T(8,128)(2,1)S(1)}, bf16[128,512]{1,0:T(8,128)(2,1)S(1)}, u32[]{:S(2)}, u32[]{:S(2)}) collective-permute-start(bf16[128,512]{1,0:T(8,128)(2,1)S(1)} %add_convert_fusion.5), channel_id=1, source_target_pairs={{0,16},{4,20},{8,24},{12,28},{16,0},{20,4},{24,8},{28,12},{1,17},{... | collective-permute-start | bytes 393224 | tf_op jit(solution)/shard_map/ppermute | solution.py:29
  35.9 27.7 %collective-permute-start.15 = (bf16[1024,256]{1,0:T(8,128)(2,1)S(1)}, bf16[1024,256]{1,0:T(8,128)(2,1)S(1)}, u32[]{:S(2)}, u32[]{:S(2)}) collective-permute-start(bf16[1024,256]{1,0:T(8,128)(2,1)S(1)} %collective-permute-done.14.refs_2_), channel_id=1, source_target_pairs={{1,0},{2,3},{5,4},{6,7},{9,8},{10,11},{13,12},{14,15},{17,16},{18,... | collective-permute-start | bytes 1572872 | tf_op jit(solution)/shard_map/ppermute | solution.py:289
  39.6 24.0 %collective-permute-start.11 = (bf16[1024,256]{1,0:T(8,128)(2,1)S(1)}, bf16[1024,256]{1,0:T(8,128)(2,1)S(1)}, u32[]{:S(2)}, u32[]{:S(2)}) collective-permute-start(bf16[1024,256]{1,0:T(8,128)(2,1)S(1)} %collective-permute-done.5.refs_1_), channel_id=1, source_target_pairs={{1,2},{2,1},{5,6},{6,5},{9,10},{10,9},{13,14},{14,13},{17,18},{18,... | collective-permute-start | bytes 1572872 | tf_op jit(solution)/shard_map/ppermute | solution.py:289
  44.1 9.7 %collective-permute-start.6 = (bf16[128,512]{1,0:T(8,128)(2,1)S(1)}, bf16[128,512]{1,0:T(8,128)(2,1)S(1)}, u32[]{:S(2)}, u32[]{:S(2)}) collective-permute-start(bf16[128,512]{1,0:T(8,128)(2,1)S(1)} %add_convert_fusion.4.refs_0_), channel_id=1, source_target_pairs={{0,4},{4,0},{8,12},{12,8},{16,20},{20,16},{24,28},{28,24},{1,5},{5... | collective-permute-start | bytes 393224 | tf_op jit(solution)/shard_map/ppermute | solution.py:29
  53.8 1.7 %collective-permute-start.12 = (bf16[128,512]{1,0:T(8,128)(2,1)S(1)}, bf16[128,512]{1,0:T(8,128)(2,1)S(1)}, u32[]{:S(2)}, u32[]{:S(2)}) collective-permute-start(bf16[128,512]{1,0:T(8,128)(2,1)S(1)} %get-tuple-element.37), channel_id=1, source_target_pairs={{0,4},{4,0},{8,12},{12,8},{16,20},{20,16},{24,28},{28,24},{1,5},{5... | collective-permute-start | bytes 393224 | tf_op jit(solution)/shard_map/ppermute | solution.py:29
  55.6 8.0 %collective-permute-start.13 = (bf16[128,512]{1,0:T(8,128)(2,1)S(1)}, bf16[128,512]{1,0:T(8,128)(2,1)S(1)}, u32[]{:S(2)}, u32[]{:S(2)}) collective-permute-start(bf16[128,512]{1,0:T(8,128)(2,1)S(1)} %add_convert_fusion.3), channel_id=1, source_target_pairs={{0,24},{4,28},{8,16},{12,20},{16,8},{20,12},{24,0},{28,4},{1,25},{... | collective-permute-start | bytes 393224 | tf_op jit(solution)/shard_map/ppermute | solution.py:29
  58.1 7.2 %collective-permute-start.16 = (bf16[128,512]{1,0:T(8,128)(2,1)S(1)}, bf16[128,512]{1,0:T(8,128)(2,1)S(1)}, u32[]{:S(2)}, u32[]{:S(2)}) collective-permute-start(bf16[128,512]{1,0:T(8,128)(2,1)S(1)} %add_convert_fusion.3), channel_id=1, source_target_pairs={{0,8},{4,12},{8,0},{12,4},{16,24},{20,28},{24,16},{28,20},{1,9},{5... | collective-permute-start | bytes 393224 | tf_op jit(solution)/shard_map/ppermute | solution.py:29
  58.6 6.7 %collective-permute-start.17 = (bf16[128,512]{1,0:T(8,128)(2,1)S(1)}, bf16[128,512]{1,0:T(8,128)(2,1)S(1)}, u32[]{:S(2)}, u32[]{:S(2)}) collective-permute-start(bf16[128,512]{1,0:T(8,128)(2,1)S(1)} %add_convert_fusion.3), channel_id=1, source_target_pairs={{0,16},{4,20},{8,24},{12,28},{16,0},{20,4},{24,8},{28,12},{1,17},{... | collective-permute-start | bytes 393224 | tf_op jit(solution)/shard_map/ppermute | solution.py:29
  65.4 1.4 %collective-permute-start.18 = (bf16[128,512]{1,0:T(8,128)(2,1)S(1)}, bf16[128,512]{1,0:T(8,128)(2,1)S(1)}, u32[]{:S(2)}, u32[]{:S(2)}) collective-permute-start(bf16[128,512]{1,0:T(8,128)(2,1)S(1)} %add_convert_fusion.2.own_ref), channel_id=1, source_target_pairs={{0,4},{4,0},{8,12},{12,8},{16,20},{20,16},{24,28},{28,24},{1,5},{5... | collective-permute-start | bytes 393224 | tf_op jit(solution)/shard_map/ppermute | solution.py:29
  65.5 17.0 %collective-permute-start.24 = (bf16[1024,256]{1,0:T(8,128)(2,1)S(1)}, bf16[1024,256]{1,0:T(8,128)(2,1)S(1)}, u32[]{:S(2)}, u32[]{:S(2)}) collective-permute-start(bf16[1024,256]{1,0:T(8,128)(2,1)S(1)} %collective-permute-done.11.refs_4_.refs_0_), channel_id=1, source_target_pairs={{1,0},{2,3},{5,4},{6,7},{9,8},{10,11},{13,12},{14,15},{17,16},{18,... | collective-permute-start | bytes 1572872 | tf_op jit(solution)/shard_map/ppermute | solution.py:289
  69.2 1.6 %collective-permute-start.19 = (bf16[128,768]{1,0:T(8,128)(2,1)S(1)}, bf16[128,768]{1,0:T(8,128)(2,1)S(1)}, u32[]{:S(2)}, u32[]{:S(2)}) collective-permute-start(bf16[128,768]{1,0:T(8,128)(2,1)S(1)} %get-tuple-element.42), channel_id=1, source_target_pairs={{0,4},{4,0},{8,12},{12,8},{16,20},{20,16},{24,28},{28,24},{1,5},{5... | collective-permute-start | bytes 589832 | tf_op jit(solution)/shard_map/ppermute | solution.py:29
  70.8 12.2 %collective-permute-start.20 = (bf16[128,768]{1,0:T(8,128)(2,1)S(1)}, bf16[128,768]{1,0:T(8,128)(2,1)S(1)}, u32[]{:S(2)}, u32[]{:S(2)}) collective-permute-start(bf16[128,768]{1,0:T(8,128)(2,1)S(1)} %add_convert_fusion.1), channel_id=1, source_target_pairs={{0,24},{4,28},{8,16},{12,20},{16,8},{20,12},{24,0},{28,4},{1,25},{... | collective-permute-start | bytes 589832 | tf_op jit(solution)/shard_map/ppermute | solution.py:29
  73.3 9.9 %collective-permute-start.21 = (bf16[128,768]{1,0:T(8,128)(2,1)S(1)}, bf16[128,768]{1,0:T(8,128)(2,1)S(1)}, u32[]{:S(2)}, u32[]{:S(2)}) collective-permute-start(bf16[128,768]{1,0:T(8,128)(2,1)S(1)} %add_convert_fusion.1), channel_id=1, source_target_pairs={{0,8},{4,12},{8,0},{12,4},{16,24},{20,28},{24,16},{28,20},{1,9},{5... | collective-permute-start | bytes 589832 | tf_op jit(solution)/shard_map/ppermute | solution.py:29
  73.8 9.4 %collective-permute-start.22 = (bf16[128,768]{1,0:T(8,128)(2,1)S(1)}, bf16[128,768]{1,0:T(8,128)(2,1)S(1)}, u32[]{:S(2)}, u32[]{:S(2)}) collective-permute-start(bf16[128,768]{1,0:T(8,128)(2,1)S(1)} %add_convert_fusion.1), channel_id=1, source_target_pairs={{0,16},{4,20},{8,24},{12,28},{16,0},{20,4},{24,8},{28,12},{1,17},{... | collective-permute-start | bytes 589832 | tf_op jit(solution)/shard_map/ppermute | solution.py:29
  82.9 1.3 %collective-permute-start.25 = (bf16[128,256]{1,0:T(8,128)(2,1)S(1)}, bf16[128,256]{1,0:T(8,128)(2,1)S(1)}, u32[]{:S(2)}, u32[]{:S(2)}) collective-permute-start(bf16[128,256]{1,0:T(8,128)(2,1)S(1)} %get-tuple-element.46), channel_id=1, source_target_pairs={{0,4},{4,0},{8,12},{12,8},{16,20},{20,16},{24,28},{28,24},{1,5},{5... | collective-permute-start | bytes 196616 | tf_op jit(solution)/shard_map/ppermute | solution.py:29
  83.3 4.5 %collective-permute-start.23 = (bf16[128,768]{1,0:T(8,128)(2,1)S(1)}, bf16[128,768]{1,0:T(8,128)(2,1)S(1)}, u32[]{:S(2)}, u32[]{:S(2)}) collective-permute-start(bf16[128,768]{1,0:T(8,128)(2,1)S(1)} %add_convert_fusion.refs_0_), channel_id=1, source_target_pairs={{0,4},{4,0},{8,12},{12,8},{16,20},{20,16},{24,28},{28,24},{1,5},{5... | collective-permute-start | bytes 589832 | tf_op jit(solution)/shard_map/ppermute | solution.py:29
  84.3 7.1 %collective-permute-start.26 = (bf16[128,256]{1,0:T(8,128)(2,1)S(1)}, bf16[128,256]{1,0:T(8,128)(2,1)S(1)}, u32[]{:S(2)}, u32[]{:S(2)}) collective-permute-start(bf16[128,256]{1,0:T(8,128)(2,1)S(1)} %add_convert_fusion.7), channel_id=1, source_target_pairs={{0,24},{4,28},{8,16},{12,20},{16,8},{20,12},{24,0},{28,4},{1,25},{... | collective-permute-start | bytes 196616 | tf_op jit(solution)/shard_map/ppermute | solution.py:29
  86.7 4.7 %collective-permute-start.27 = (bf16[128,256]{1,0:T(8,128)(2,1)S(1)}, bf16[128,256]{1,0:T(8,128)(2,1)S(1)}, u32[]{:S(2)}, u32[]{:S(2)}) collective-permute-start(bf16[128,256]{1,0:T(8,128)(2,1)S(1)} %add_convert_fusion.7), channel_id=1, source_target_pairs={{0,8},{4,12},{8,0},{12,4},{16,24},{20,28},{24,16},{28,20},{1,9},{5... | collective-permute-start | bytes 196616 | tf_op jit(solution)/shard_map/ppermute | solution.py:29
  87.2 4.3 %collective-permute-start.28 = (bf16[128,256]{1,0:T(8,128)(2,1)S(1)}, bf16[128,256]{1,0:T(8,128)(2,1)S(1)}, u32[]{:S(2)}, u32[]{:S(2)}) collective-permute-start(bf16[128,256]{1,0:T(8,128)(2,1)S(1)} %add_convert_fusion.7), channel_id=1, source_target_pairs={{0,16},{4,20},{8,24},{12,28},{16,0},{20,4},{24,8},{28,12},{1,17},{... | collective-permute-start | bytes 196616 | tf_op jit(solution)/shard_map/ppermute | solution.py:29
  91.5 1.3 %collective-permute-start.29 = (bf16[128,256]{1,0:T(8,128)(2,1)S(1)}, bf16[128,256]{1,0:T(8,128)(2,1)S(1)}, u32[]{:S(2)}, u32[]{:S(2)}) collective-permute-start(bf16[128,256]{1,0:T(8,128)(2,1)S(1)} %add_convert_fusion.6.own_ref), channel_id=1, source_target_pairs={{0,4},{4,0},{8,12},{12,8},{16,20},{20,16},{24,28},{28,24},{1,5},{5... | collective-permute-start | bytes 196616 | tf_op jit(solution)/shard_map/ppermute | solution.py:29
